TPU v7x, 512 devices: a whole 4x4x16 slice. The times are simulated.
512 devices in a mesh: slab: 128 (over y, z, core), grp: 4 (over x).
Axes of the slice: x: 4, y: 4, z: 16, core: 2. Of those that a mesh axis runs over, the one named last changes fastest.
Arguments:
- pencils: float32 [256, 256, 512], P('slab', 'grp'), may hold values from -6 to 6
- send_map: int32 [128, 4, 128, 16], P('slab', 'grp'), may hold values from -1 to 511, as said below
- interp_index: int32 [2, 128, 8, 256], P(None, 'slab', None, 'grp'), may hold values from 0 to 2047, as said below
- interp_frac: float32 [128, 8, 256], P('slab', None, 'grp'), may hold values from 0 to 1
- ori_count: int32 [128], P('slab'), may hold values from 1 to 8, as said below
- spectra: bfloat16 [1024, 256, 512], P('slab', 'grp'), may hold values from -6 to 6
- class_ids: int32 [1024], P('slab'), may hold values from 0 to 15
- ctf_table: bfloat16 [16, 256, 256], P(None, 'grp'), may hold values from -1 to 1
Outputs:
- scores: float32 [1024, 512], P('slab', 'grp')
Inputs may be any that keep to these rules, and one draw needn't show every extreme that they name: `send_map`: slots with index 16 or more are never used; for every row group and owner, the used slots of one source come first, at least one, and one source fills all 16. `interp_index`: every entry names a slot that send_map fills for that owner and row group. `ori_count`: some owner lists 8 orientations.
All inputs are finite; a program needn't handle non-finite values.
Results may differ from a plain program's by a relative error of at most 0.005.
Values may be sent and summed in bfloat16 or wider, within the bound.
No kernel may reach another device: no remote copies, remote signals or barrier semaphores. Data moves between devices by JAX's collectives and lax.ppermute only.
A program may use at most 64 MiB of HBM per device.

v0:
```python
import math

import jax
import jax.numpy as jnp
from jax import lax
from jax.sharding import PartitionSpec as P

NF = 256
CAP = 16
ORI_MAX = 8
TSIDE = 8
CLASSES = 16
PART_DEV = 8
TRANS = 64


def phase_factors(first_row, row_total):
    side_ids = jnp.arange(TSIDE, dtype=jnp.int32) - TSIDE // 2
    rows_u = first_row + jnp.arange(row_total, dtype=jnp.int32)
    cols_v = jnp.arange(NF, dtype=jnp.int32)
    turns_u = side_ids[:, None] * rows_u[None, :] % NF
    turns_v = side_ids[:, None] * cols_v[None, :] % NF
    angle_u = -2.0 * math.pi / NF * turns_u.astype(jnp.float32)
    angle_v = -2.0 * math.pi / NF * turns_v.astype(jnp.float32)
    return (jnp.cos(angle_u), jnp.sin(angle_u), jnp.cos(angle_v), jnp.sin(angle_v))


def shift_score(slice_rows, weighted, factors):
    cos_u, sin_u, cos_v, sin_v = factors
    row_total = slice_rows.shape[0]
    cu = cos_u[:, None, :, None]
    su = sin_u[:, None, :, None]
    cv = cos_v[None, :, None, :]
    sv = sin_v[None, :, None, :]
    cosines = (cu * cv - su * sv).reshape(TRANS, row_total, NF)
    sines = (su * cv + cu * sv).reshape(TRANS, row_total, NF)
    real_part = slice_rows[None, :, :NF]
    imag_part = slice_rows[None, :, NF:]
    shifted = jnp.concatenate(
        [real_part * cosines - imag_part * sines, real_part * sines + imag_part * cosines], axis=-1
    ).astype(jnp.bfloat16)
    flat_refs = shifted.reshape(TRANS, -1)
    return (
        lax.dot_general(
            weighted, flat_refs, (((1,), (1,)), ((), ())), preferred_element_type=jnp.float32
        )
        / NF
    )


def shards(pencils, send_map, interp_index, interp_frac, ori_count, spectra, class_ids, ctf_table):
    slab_depth = NF // lax.axis_size("slab")
    freq_index = jnp.arange(NF, dtype=jnp.int32)
    phase_turns = freq_index[:, None] * freq_index[None, :] % NF
    angles = 2.0 * math.pi / NF * phase_turns.astype(jnp.float32)
    cosine = jnp.cos(angles)
    sine_table = jnp.sin(angles)
    norm_scale = 1.0 / math.sqrt(NF)
    real_in = pencils[..., :NF]
    imag_in = pencils[..., NF:]
    highest = lax.Precision.HIGHEST
    real_out = (
        jnp.einsum("yxz,zk->kyx", real_in, cosine, precision=highest)
        + jnp.einsum("yxz,zk->kyx", imag_in, sine_table, precision=highest)
    ) * norm_scale
    imag_out = (
        jnp.einsum("yxz,zk->kyx", imag_in, cosine, precision=highest)
        - jnp.einsum("yxz,zk->kyx", real_in, sine_table, precision=highest)
    ) * norm_scale
    planes = jnp.stack([real_out, imag_out], axis=2).astype(jnp.bfloat16)
    slab_planes = lax.all_to_all(planes, "slab", split_axis=0, concat_axis=1, tiled=True)
    gathered = lax.all_gather(slab_planes, "grp", axis=3, tiled=True)
    row_table = gathered.reshape(slab_depth * NF, 2 * NF)
    slot_map = send_map[0, 0]
    picked = jnp.take(row_table, jnp.maximum(slot_map, 0).reshape(-1), axis=0)
    picked = picked * (slot_map >= 0).reshape(-1, 1).astype(jnp.bfloat16)
    outgoing = picked.reshape(slot_map.shape[0], CAP, 2 * NF)
    arrived = lax.all_to_all(outgoing, "slab", split_axis=0, concat_axis=0, tiled=True)
    buffer = arrived.reshape(-1, 2 * NF)
    rows_local = interp_frac.shape[2]
    tap_index = interp_index[:, 0]
    weights_tap = interp_frac[0][..., None]
    lower_rows = jnp.take(buffer, tap_index[0].reshape(-1), axis=0).reshape(
        ORI_MAX, rows_local, 2 * NF
    )
    upper_rows = jnp.take(buffer, tap_index[1].reshape(-1), axis=0).reshape(
        ORI_MAX, rows_local, 2 * NF
    )
    slices = (1.0 - weights_tap) * lower_rows.astype(jnp.float32) + weights_tap * upper_rows.astype(
        jnp.float32
    )
    onehot = (class_ids[:, None] == jnp.arange(CLASSES, dtype=jnp.int32)[None, :]).astype(
        jnp.bfloat16
    )
    ctf_rows = jnp.dot(
        onehot, ctf_table.reshape(CLASSES, -1), preferred_element_type=jnp.float32
    ).reshape(PART_DEV, rows_local, NF)
    weighted = (
        (jnp.concatenate([ctf_rows, ctf_rows], axis=-1) * spectra.astype(jnp.float32))
        .astype(jnp.bfloat16)
        .reshape(PART_DEV, -1)
    )
    first_row = lax.axis_index("grp") * rows_local
    factors = phase_factors(first_row, rows_local)
    live_count = ori_count[0]

    def orient_score(orient):
        result = shift_score(slices[orient], weighted, factors)
        return jnp.where(orient < live_count, result, jnp.zeros_like(result))

    blocks_out = lax.map(orient_score, jnp.arange(ORI_MAX, dtype=jnp.int32))
    partial_scores = jnp.transpose(blocks_out, (1, 0, 2)).reshape(PART_DEV, ORI_MAX * TRANS)
    return lax.psum_scatter(partial_scores, "grp", scatter_dimension=1, tiled=True)


def solution(mesh):
    return jax.shard_map(
        shards,
        mesh=mesh,
        in_specs=(
            P("slab", "grp", None),
            P("slab", "grp", None, None),
            P(None, "slab", None, "grp"),
            P("slab", None, "grp"),
            P("slab"),
            P("slab", "grp", None),
            P("slab"),
            P(None, "grp", None),
        ),
        out_specs=P("slab", "grp"),
        check_vma=False,
    )
```

profile of v0, /device:TPU:1, one launch (start us, length us, event | category | flops | bytes accessed | tf_op | source)
XLA Modules:
  0.0 334.6 jit_solution(14726402945951975218)
XLA Ops:
  6.5 2.2 fusion.40
  8.7 2.2 fusion.42
  10.9 2.2 fusion.28
  13.1 2.2 fusion.29
  15.5 0.9 reshape.160
  16.4 20.5 %all-to-all-start = ((bf16[128,2,256]{2,1,0:T(2,128)(2,1)}), bf16[128,2,256]{2,1,0:T(2,128)(2,1)S(1)}, u32[]{:S(2)}, u32[]{:S(2)}) async-start(bf16[128,2,256]{2,1,0:T(2,128)(2,1)} %reshape.160), calls=%async_computation | async-start | bytes 262144 | tf_op jit(solution)/shard_map/all_to_all | solution.py:71
  37.4 16.9 %all-to-all-done = bf16[128,2,256]{2,1,0:T(2,128)(2,1)S(1)} async-done(((bf16[128,2,256]{2,1,0:T(2,128)(2,1)}), bf16[128,2,256]{2,1,0:T(2,128)(2,1)S(1)}, u32[]{:S(2)}, u32[]{:S(2)}) %all-to-all-start) | async-done | bytes 131104 | tf_op jit(solution)/shard_map/all_to_all | solution.py:71
  54.6 0.3 copy.25
  55.0 10.8 %all_gather.3 = bf16[2,256,2,256]{1,2,0,3:T(2,128)(2,1)S(1)} all-gather(bf16[2,256,2,64]{1,2,0,3:T(2,128)(2,1)S(1)} %copy.26), channel_id=1, replica_groups=mesh['slab'=128,'grp'=4] {'grp'}, dimensions={3}, use_global_device_ids=true | all-gather | bytes 655360 | tf_op jit(solution)/shard_map/all_gather | solution.py:72
  65.8 1.0 copy.27
  66.9 7.5 %gather_fusion = bf16[2048,512]{1,0:T(8,128)(2,1)S(1)} fusion(bf16[512,512]{1,0:T(8,128)(2,1)S(1)} %bitcast.97, s32[2048]{0:T(1024)S(1)} %broadcast_clamp_fusion), kind=kCustom, calls=%fused_computation.2 | custom fusion | bytes 4202496 | tf_op jit(solution)/shard_map/jit(_take)/gather | solution.py:75
  74.5 1.7 select_multiply_fusion
  76.2 10.0 %all-to-all-start.1 = ((bf16[128,16,512]{2,1,0:T(8,128)(2,1)}), bf16[128,16,512]{2,1,0:T(8,128)(2,1)S(1)}, u32[]{:S(2)}, u32[]{:S(2)}) async-start(bf16[128,16,512]{2,1,0:T(8,128)(2,1)} %select_multiply_fusion), calls=%async_computation.1 | async-start | bytes 4194304 | tf_op jit(solution)/shard_map/all_to_all | solution.py:78
  86.2 0.2 reduce-scatter.2.cloned.1.call-start
  86.7 0.4 fusion.32
  87.1 0.3 fusion.30
  87.5 98.0 %all-to-all-done.1 = bf16[128,16,512]{2,1,0:T(8,128)(2,1)S(1)} async-done(((bf16[128,16,512]{2,1,0:T(8,128)(2,1)}), bf16[128,16,512]{2,1,0:T(8,128)(2,1)S(1)}, u32[]{:S(2)}, u32[]{:S(2)}) %all-to-all-start.1) | async-done | bytes 2097184 | tf_op jit(solution)/shard_map/all_to_all | solution.py:78
  185.4 2.6 gather_fusion.1
  188.0 2.0 gather_fusion.2
  190.0 1.2 broadcast_select_fusion.1
  191.3 0.3 fusion.31
  191.7 117.1 %while.13 = (s32[]{:T(128)}, f32[8,8,64]{2,1,0:T(8,128)S(1)}, s32[8]{0:T(128)S(1)}, s32[]{:T(128)}, f32[8,64,512]{2,1,0:T(8,128)S(1)}, /*index=5*/bf16[8,32768]{...) while((s32[]{:T(128)}, f32[8,8,64]{2,1,0:T(8,128)S(1)}, ...), condition=%wide.region_1.3_spmd.clone.clone.clone, body=%wide.region_0.2_spmd.clone.clone.clone.sunk | while | flops 56659972 | bytes 26718700 | solution.py:111
  191.7 0.6 dynamic_slice.17
  194.5 2.2 subtract_convert_fusion.2
  196.7 0.4 pad_maximum_fusion.3
  197.1 4.5 %copy.46 = bf16[8,8,64,512]{3,1,2,0:T(8,128)(2,1)} copy(bf16[8,8,64,512]{3,2,1,0:T(8,128)(2,1)S(1)} %bitcast.99) | data formatting | bytes 8388608 | tf_op jit(solution)/shard_map/while
  202.9 3.4 %fusion.92 = f32[8,8,64]{2,1,0:T(8,128)S(1)} fusion(f32[8,8,64]{2,1,0:T(8,128)S(1)} %get-tuple-element.267, s32[]{:T(128)} %get-tuple-element.266, bf16[64,32768]{1,0:T(8,128)(2,1)} %bitcast.98, bf16[8,32768]{1,0:T(8,128)(2,1)S(1)} %get-tuple-element.282, pred[]{:T(512)S(6)} %lt.147), kind=kOutput, calls=%fused_computation.15.clone.1 | convolution fusion | flops 33555456 | bytes 4722693 | tf_op jit(solution)/shard_map/while/body/eval_jaxpr/dot_general | solution.py:44
  206.3 0.6 dynamic_slice.17
  209.1 2.2 subtract_convert_fusion.2
  211.4 0.4 pad_maximum_fusion.3
  211.8 4.5 %copy.46 = bf16[8,8,64,512]{3,1,2,0:T(8,128)(2,1)} copy(bf16[8,8,64,512]{3,2,1,0:T(8,128)(2,1)S(1)} %bitcast.99) | data formatting | bytes 8388608 | tf_op jit(solution)/shard_map/while
  217.6 3.4 %fusion.92 = f32[8,8,64]{2,1,0:T(8,128)S(1)} fusion(f32[8,8,64]{2,1,0:T(8,128)S(1)} %get-tuple-element.267, s32[]{:T(128)} %get-tuple-element.266, bf16[64,32768]{1,0:T(8,128)(2,1)} %bitcast.98, bf16[8,32768]{1,0:T(8,128)(2,1)S(1)} %get-tuple-element.282, pred[]{:T(512)S(6)} %lt.147), kind=kOutput, calls=%fused_computation.15.clone.1 | convolution fusion | flops 33555456 | bytes 4722693 | tf_op jit(solution)/shard_map/while/body/eval_jaxpr/dot_general | solution.py:44
  220.9 0.6 dynamic_slice.17
  223.8 2.2 subtract_convert_fusion.2
  226.0 0.4 pad_maximum_fusion.3
  226.4 4.5 %copy.46 = bf16[8,8,64,512]{3,1,2,0:T(8,128)(2,1)} copy(bf16[8,8,64,512]{3,2,1,0:T(8,128)(2,1)S(1)} %bitcast.99) | data formatting | bytes 8388608 | tf_op jit(solution)/shard_map/while
  232.2 3.4 %fusion.92 = f32[8,8,64]{2,1,0:T(8,128)S(1)} fusion(f32[8,8,64]{2,1,0:T(8,128)S(1)} %get-tuple-element.267, s32[]{:T(128)} %get-tuple-element.266, bf16[64,32768]{1,0:T(8,128)(2,1)} %bitcast.98, bf16[8,32768]{1,0:T(8,128)(2,1)S(1)} %get-tuple-element.282, pred[]{:T(512)S(6)} %lt.147), kind=kOutput, calls=%fused_computation.15.clone.1 | convolution fusion | flops 33555456 | bytes 4722693 | tf_op jit(solution)/shard_map/while/body/eval_jaxpr/dot_general | solution.py:44
  235.6 0.6 dynamic_slice.17
  238.4 2.2 subtract_convert_fusion.2
  240.6 0.4 pad_maximum_fusion.3
  241.0 4.5 %copy.46 = bf16[8,8,64,512]{3,1,2,0:T(8,128)(2,1)} copy(bf16[8,8,64,512]{3,2,1,0:T(8,128)(2,1)S(1)} %bitcast.99) | data formatting | bytes 8388608 | tf_op jit(solution)/shard_map/while
  246.8 3.4 %fusion.92 = f32[8,8,64]{2,1,0:T(8,128)S(1)} fusion(f32[8,8,64]{2,1,0:T(8,128)S(1)} %get-tuple-element.267, s32[]{:T(128)} %get-tuple-element.266, bf16[64,32768]{1,0:T(8,128)(2,1)} %bitcast.98, bf16[8,32768]{1,0:T(8,128)(2,1)S(1)} %get-tuple-element.282, pred[]{:T(512)S(6)} %lt.147), kind=kOutput, calls=%fused_computation.15.clone.1 | convolution fusion | flops 33555456 | bytes 4722693 | tf_op jit(solution)/shard_map/while/body/eval_jaxpr/dot_general | solution.py:44
  250.2 0.6 dynamic_slice.17
  253.1 2.2 subtract_convert_fusion.2
  255.3 0.4 pad_maximum_fusion.3
  255.7 4.5 %copy.46 = bf16[8,8,64,512]{3,1,2,0:T(8,128)(2,1)} copy(bf16[8,8,64,512]{3,2,1,0:T(8,128)(2,1)S(1)} %bitcast.99) | data formatting | bytes 8388608 | tf_op jit(solution)/shard_map/while
  261.5 3.4 %fusion.92 = f32[8,8,64]{2,1,0:T(8,128)S(1)} fusion(f32[8,8,64]{2,1,0:T(8,128)S(1)} %get-tuple-element.267, s32[]{:T(128)} %get-tuple-element.266, bf16[64,32768]{1,0:T(8,128)(2,1)} %bitcast.98, bf16[8,32768]{1,0:T(8,128)(2,1)S(1)} %get-tuple-element.282, pred[]{:T(512)S(6)} %lt.147), kind=kOutput, calls=%fused_computation.15.clone.1 | convolution fusion | flops 33555456 | bytes 4722693 | tf_op jit(solution)/shard_map/while/body/eval_jaxpr/dot_general | solution.py:44
  264.8 0.6 dynamic_slice.17
  267.7 2.2 subtract_convert_fusion.2
  269.9 0.4 pad_maximum_fusion.3
  270.3 4.5 %copy.46 = bf16[8,8,64,512]{3,1,2,0:T(8,128)(2,1)} copy(bf16[8,8,64,512]{3,2,1,0:T(8,128)(2,1)S(1)} %bitcast.99) | data formatting | bytes 8388608 | tf_op jit(solution)/shard_map/while
  276.1 3.4 %fusion.92 = f32[8,8,64]{2,1,0:T(8,128)S(1)} fusion(f32[8,8,64]{2,1,0:T(8,128)S(1)} %get-tuple-element.267, s32[]{:T(128)} %get-tuple-element.266, bf16[64,32768]{1,0:T(8,128)(2,1)} %bitcast.98, bf16[8,32768]{1,0:T(8,128)(2,1)S(1)} %get-tuple-element.282, pred[]{:T(512)S(6)} %lt.147), kind=kOutput, calls=%fused_computation.15.clone.1 | convolution fusion | flops 33555456 | bytes 4722693 | tf_op jit(solution)/shard_map/while/body/eval_jaxpr/dot_general | solution.py:44
  279.5 0.6 dynamic_slice.17
  282.3 2.2 subtract_convert_fusion.2
  284.5 0.4 pad_maximum_fusion.3
  284.9 4.5 %copy.46 = bf16[8,8,64,512]{3,1,2,0:T(8,128)(2,1)} copy(bf16[8,8,64,512]{3,2,1,0:T(8,128)(2,1)S(1)} %bitcast.99) | data formatting | bytes 8388608 | tf_op jit(solution)/shard_map/while
  290.7 3.4 %fusion.92 = f32[8,8,64]{2,1,0:T(8,128)S(1)} fusion(f32[8,8,64]{2,1,0:T(8,128)S(1)} %get-tuple-element.267, s32[]{:T(128)} %get-tuple-element.266, bf16[64,32768]{1,0:T(8,128)(2,1)} %bitcast.98, bf16[8,32768]{1,0:T(8,128)(2,1)S(1)} %get-tuple-element.282, pred[]{:T(512)S(6)} %lt.147), kind=kOutput, calls=%fused_computation.15.clone.1 | convolution fusion | flops 33555456 | bytes 4722693 | tf_op jit(solution)/shard_map/while/body/eval_jaxpr/dot_general | solution.py:44
  294.1 0.6 dynamic_slice.17
  297.0 2.2 subtract_convert_fusion.2
  299.2 0.4 pad_maximum_fusion.3
  299.6 4.5 %copy.46 = bf16[8,8,64,512]{3,1,2,0:T(8,128)(2,1)} copy(bf16[8,8,64,512]{3,2,1,0:T(8,128)(2,1)S(1)} %bitcast.99) | data formatting | bytes 8388608 | tf_op jit(solution)/shard_map/while
  305.4 3.4 %fusion.92 = f32[8,8,64]{2,1,0:T(8,128)S(1)} fusion(f32[8,8,64]{2,1,0:T(8,128)S(1)} %get-tuple-element.267, s32[]{:T(128)} %get-tuple-element.266, bf16[64,32768]{1,0:T(8,128)(2,1)} %bitcast.98, bf16[8,32768]{1,0:T(8,128)(2,1)S(1)} %get-tuple-element.282, pred[]{:T(512)S(6)} %lt.147), kind=kOutput, calls=%fused_computation.15.clone.1 | convolution fusion | flops 33555456 | bytes 4722693 | tf_op jit(solution)/shard_map/while/body/eval_jaxpr/dot_general | solution.py:44
  308.8 0.7 reshape.122
  309.5 18.3 %reduce-scatter.2.cloned.1.call-done = f32[8,128]{1,0:T(8,128)} async-done(((f32[8,512]{1,0:T(8,128)}), f32[8,128]{1,0:T(8,128)}) %reduce-scatter.2.cloned.1.call-update) | async-done | bytes 4112 | tf_op jit(solution)/shard_map/reduce_scatter | solution.py:113
  (90 shorter events, 3.9 us)
Async XLA Ops:
  6.5 30.4 %copy-start.2 = (s32[1,1,128,16]{2,3,1,0:T(8,128)S(1)}, s32[1,1,128,16]{2,3,1,0:T(8,128)}, u32[]{:S(2)}) copy-start(s32[1,1,128,16]{2,3,1,0:T(8,128)} %param.13) | copy-start | bytes 24580
  16.4 38.0 %all-to-all-start = ((bf16[128,2,256]{2,1,0:T(2,128)(2,1)}), bf16[128,2,256]{2,1,0:T(2,128)(2,1)S(1)}, u32[]{:S(2)}, u32[]{:S(2)}) async-start(bf16[128,2,256]{2,1,0:T(2,128)(2,1)} %reshape.160), calls=%async_computation | async-start | bytes 262144 | tf_op jit(solution)/shard_map/all_to_all | solution.py:71
  74.5 12.0 %copy-start.4 = (s32[2,1,8,64]{3,2,1,0:T(8,128)S(1)}, s32[2,1,8,64]{3,2,1,0:T(8,128)}, u32[]{:S(2)}) copy-start(s32[2,1,8,64]{3,2,1,0:T(8,128)} %param.14) | copy-start | bytes 12292
  74.5 12.2 %copy-start.3 = (f32[1,8,64]{2,1,0:T(8,128)S(1)}, f32[1,8,64]{2,1,0:T(8,128)}, u32[]{:S(2)}) copy-start(f32[1,8,64]{2,1,0:T(8,128)} %param.15) | copy-start | bytes 6148
  74.5 12.2 %copy-start.5 = (s32[8]{0:T(128)S(1)}, s32[8]{0:T(128)}, u32[]{:S(2)}) copy-start(s32[8]{0:T(128)} %param.18) | copy-start | bytes 100
  74.5 12.6 %copy-start = (bf16[8,64,512]{2,1,0:T(8,128)(2,1)S(1)}, bf16[8,64,512]{2,1,0:T(8,128)(2,1)}, u32[]{:S(2)}) copy-start(bf16[8,64,512]{2,1,0:T(8,128)(2,1)} %param.17) | copy-start | bytes 1572868
  76.2 10.5 %copy-start.1 = (bf16[16,64,256]{2,1,0:T(8,128)(2,1)S(1)}, bf16[16,64,256]{2,1,0:T(8,128)(2,1)}, u32[]{:S(2)}) copy-start(bf16[16,64,256]{2,1,0:T(8,128)(2,1)} %param.19) | copy-start | bytes 1572868
  76.2 109.2 %all-to-all-start.1 = ((bf16[128,16,512]{2,1,0:T(8,128)(2,1)}), bf16[128,16,512]{2,1,0:T(8,128)(2,1)S(1)}, u32[]{:S(2)}, u32[]{:S(2)}) async-start(bf16[128,16,512]{2,1,0:T(8,128)(2,1)} %select_multiply_fusion), calls=%async_computation.1 | async-start | bytes 4194304 | tf_op jit(solution)/shard_map/all_to_all | solution.py:78
  86.2 241.5 %reduce-scatter.2.cloned.1.call-start = ((), (), s32[]{:S(2)}) async-start(), calls=%async_computation.3 | async-start | bytes 20480 | tf_op jit(solution)/shard_map/reduce_scatter | solution.py:113
Sparse Core Ops, SparseCore 0:
  309.6 18.0 reduce-scatter.1
where the time goes:
time: 337 us; the launch traced here: 335 us
  waiting for transfers between devices  133 us (39%)
  local copies, waits for them, and re-layouts  57.5 us (17%)
  matrix products  36.1 us (11%)
  starting transfers between devices  30.7 us (9%)
  other arithmetic  26.5 us (8%)
  loops' own time  26 us (8%)
  between operations  13.7 us (4%)
  blocking collectives  10.8 us (3%)
    all_to_all x1, waiting for transfers between devices, shards(): lax.all_to_all(outgoing, 'slab', split_axis=0, concat_axis=0, tiled=True)  98 us
    while x8, local copies, waits for them, and re-layouts  36 us
    dot_general x8, matrix products, shift_score(): lax.dot_general(weighted, flat_refs, (((1,), (1,)), ((), ())), preferred_...  27 us
    another operation x1, loops' own time, shards(): blocks_out = lax.map(orient_score, jnp.arange(ORI_MAX, dtype=jnp.int32))  26 us
    all_to_all x1, starting transfers between devices, shards(): lax.all_to_all(planes, 'slab', split_axis=0, concat_axis=1, tiled=True)  20.5 us
    reduce_scatter x1, waiting for transfers between devices, shards(): lax.psum_scatter(partial_scores, 'grp', scatter_dimension=1, tiled=True)  18.3 us
    another operation x8, other arithmetic  17.8 us
    all_to_all x1, waiting for transfers between devices, shards(): lax.all_to_all(planes, 'slab', split_axis=0, concat_axis=1, tiled=True)  16.9 us
  transfers between devices with their start and end apart: 3, of which 3 were waited for; matrix products, arithmetic and copies ran while one was open for 0% of the time, Pallas kernels for 0%

commit v1 on v0

v1 whole, which is shorter than its diff:
```python
import math

import jax
import jax.numpy as jnp
import ml_dtypes
import numpy as np
from jax import lax
from jax.experimental import pallas as pl
from jax.experimental.pallas import tpu as pltpu
from jax.sharding import PartitionSpec as P

NF = 256
CAP = 16
ORI_MAX = 8
TSIDE = 8
CLASSES = 16
PART_DEV = 8
TRANS = 64
N_GRP = 4
COLS = NF // N_GRP
LANES = 2 * COLS
SLAB_ROWS = 512
VMEM_BYTES = 48 * 1024 * 1024


def split_bf16(values):
    high = values.astype(ml_dtypes.bfloat16)
    low = (values - high.astype(np.float64)).astype(ml_dtypes.bfloat16)
    return high, low


def fourier_tables():
    index = np.arange(NF)
    angle = 2.0 * math.pi / NF * ((index[:, None] * index[None, :]) % NF)
    table = np.concatenate([np.cos(angle), np.sin(angle)], axis=1) / math.sqrt(NF)
    return np.stack(split_bf16(table))


def column_table():
    b = np.arange(TRANS) % TSIDE - TSIDE // 2
    v = np.arange(NF)
    angle = -2.0 * math.pi / NF * ((b[None, :] * v[:, None]) % NF)
    fr = np.cos(angle).reshape(N_GRP, COLS, TRANS) / NF
    fi = np.sin(angle).reshape(N_GRP, COLS, TRANS) / NF

    def lanes(first, second):
        return np.stack([first, second], axis=1).reshape(2 * NF, TRANS)

    with_er = np.concatenate([lanes(fr, fr), lanes(-fi, fi)], axis=0)
    with_ei = np.concatenate([lanes(-fi, -fi), lanes(-fr, fr)], axis=0)
    high, low = split_bf16(np.concatenate([with_er, with_ei], axis=1))
    return np.concatenate([high, low], axis=1)


def row_table():
    a = np.arange(TRANS) // TSIDE - TSIDE // 2
    u = np.arange(NF)
    angle = -2.0 * math.pi / NF * ((a[None, :] * u[:, None]) % NF)
    table = np.concatenate([np.cos(angle), np.sin(angle)], axis=1).astype(np.float32)
    return table.reshape(N_GRP, COLS, 2 * TRANS)


def fourier_kernel(x_ref, table_ref, out_ref, wide):
    contract = (((1,), (1,)), ((), ()))
    for ky in range(2):
        lines = x_ref[ky]
        turned = jnp.concatenate([lines[:, NF:], -lines[:, :NF]], axis=1)
        both = jnp.concatenate([lines, turned], axis=0)
        high = both.astype(jnp.bfloat16)
        low = (both - high.astype(jnp.float32)).astype(jnp.bfloat16)

        def product(table, part):
            return lax.dot_general(table, part, contract, preferred_element_type=jnp.float32)

        result = (product(table_ref[0], low) + product(table_ref[1], high)) + product(
            table_ref[0], high
        )
        wide[pl.ds(ky, NF, stride=2), :] = result
    out_ref[...] = wide[...].astype(jnp.bfloat16)


def fourier(pencils, table):
    return pl.pallas_call(
        fourier_kernel,
        out_shape=jax.ShapeDtypeStruct((2 * NF, LANES), jnp.bfloat16),
        scratch_shapes=[pltpu.VMEM((2 * NF, LANES), jnp.float32)],
        compiler_params=pltpu.CompilerParams(vmem_limit_bytes=VMEM_BYTES),
        cost_estimate=pl.CostEstimate(
            flops=6 * NF * NF * 2 * NF, bytes_accessed=1 << 20, transcendentals=0
        ),
    )(pencils, table)


PICK_STEP = 512


def pick_kernel(place_ref, table_ref, out_ref):
    place = place_ref[...]
    lane = lax.broadcasted_iota(jnp.int32, (PICK_STEP, LANES), 1)
    hits = jnp.concatenate(
        [
            jnp.where(place == lane + first, 1.0, 0.0).astype(jnp.bfloat16)
            for first in range(0, SLAB_ROWS, LANES)
        ],
        axis=1,
    )
    rows = jnp.concatenate([table_ref[g] for g in range(N_GRP)], axis=1)
    out_ref[...] = jnp.dot(hits, rows, preferred_element_type=jnp.float32).astype(jnp.bfloat16)


def pick(place, table):
    total = place.shape[0]
    return pl.pallas_call(
        pick_kernel,
        grid=(total // PICK_STEP,),
        in_specs=[
            pl.BlockSpec((PICK_STEP, LANES), lambda i: (i, 0)),
            pl.BlockSpec((N_GRP, SLAB_ROWS, LANES), lambda i: (0, 0, 0)),
        ],
        out_specs=pl.BlockSpec((PICK_STEP, 2 * NF), lambda i: (i, 0)),
        out_shape=jax.ShapeDtypeStruct((total, 2 * NF), jnp.bfloat16),
        compiler_params=pltpu.CompilerParams(vmem_limit_bytes=VMEM_BYTES),
        cost_estimate=pl.CostEstimate(
            flops=2 * total * SLAB_ROWS * 2 * NF, bytes_accessed=4 << 20, transcendentals=0
        ),
    )(place, table)


def score_kernel(
    count_ref, buffer_ref, tap_ref, frac_ref, weighted_ref, col_ref, row_ref, out_ref, mix, slices
):
    total = tap_ref.shape[1]
    slots = buffer_ref.shape[0]
    lane = lax.broadcasted_iota(jnp.int32, (total, LANES), 1)
    frac = frac_ref[...]
    rest = 1.0 - frac
    for first in range(0, slots, LANES):
        entry = jnp.where(tap_ref[0] == lane + first, rest, 0.0) + jnp.where(
            tap_ref[1] == lane + first, frac, 0.0
        )
        high = entry.astype(jnp.bfloat16)
        low = (entry - high.astype(jnp.float32)).astype(jnp.bfloat16)
        mix[:total, first : first + LANES] = high
        mix[total:, first : first + LANES] = low
    both = jnp.dot(mix[...], buffer_ref[...], preferred_element_type=jnp.float32)
    slices[...] = both[:total] + both[total:]
    live_count = count_ref[0]
    phase_rows = row_ref[...]
    left = lax.broadcasted_iota(jnp.int32, (PART_DEV, LANES), 1) < TRANS
    for pair in range(ORI_MAX // 2):
        done = []
        for orient in (2 * pair, 2 * pair + 1):
            plain = slices[orient * COLS : (orient + 1) * COLS, :]
            swapped = jnp.concatenate(
                [
                    pltpu.roll(plain[:, first : first + LANES], COLS, 1)
                    for first in range(0, 2 * NF, LANES)
                ],
                axis=1,
            )
            shifted = jnp.concatenate([plain, swapped], axis=1)
            products = []
            for particle in range(PART_DEV):
                weight = weighted_ref[particle].astype(jnp.float32)
                products.append(
                    (jnp.concatenate([weight, weight], axis=1) * shifted).astype(jnp.bfloat16)
                )
            columns = jnp.dot(
                jnp.concatenate(products, axis=0),
                col_ref[...],
                preferred_element_type=jnp.float32,
            )
            columns = columns[:, :LANES] + columns[:, LANES:]
            summed = jnp.sum(columns.reshape(PART_DEV, COLS, LANES) * phase_rows[None], axis=1)
            folded = summed + pltpu.roll(summed, TRANS, 1)
            done.append(jnp.where(orient < live_count, folded, 0.0))
        out_ref[pair] = jnp.where(left, done[0], done[1])


def score(count, buffer, taps, frac, weighted, col_phase, row_phase):
    total = taps.shape[1]
    vmem = pl.BlockSpec(memory_space=pltpu.VMEM)
    return pl.pallas_call(
        score_kernel,
        in_specs=[pl.BlockSpec(memory_space=pltpu.SMEM)] + [vmem] * 6,
        out_specs=vmem,
        out_shape=jax.ShapeDtypeStruct((ORI_MAX // 2, PART_DEV, 2 * TRANS), jnp.float32),
        scratch_shapes=[
            pltpu.VMEM((2 * total, buffer.shape[0]), jnp.bfloat16),
            pltpu.VMEM((total, 2 * NF), jnp.float32),
        ],
        compiler_params=pltpu.CompilerParams(vmem_limit_bytes=VMEM_BYTES),
        cost_estimate=pl.CostEstimate(
            flops=4 << 30, bytes_accessed=4 << 20, transcendentals=0
        ),
    )(count, buffer, taps, frac, weighted, col_phase, row_phase)


def shards(pencils, send_map, interp_index, interp_frac, ori_count, spectra, class_ids, ctf_table):
    planes = fourier(pencils, jnp.asarray(fourier_tables()))
    slab_planes = lax.all_to_all(planes, "slab", split_axis=0, concat_axis=0, tiled=True)
    table = lax.all_gather(slab_planes, "grp", axis=0)
    wanted = jnp.maximum(send_map[0, 0], 0)
    place = ((wanted & (NF - 2)) << 1) | ((wanted >> 8) << 1) | (wanted & 1)
    outgoing = pick(jnp.broadcast_to(place.reshape(-1, 1), (place.size, LANES)), table)
    buffer = lax.all_to_all(outgoing, "slab", split_axis=0, concat_axis=0, tiled=True)

    rows_local = interp_frac.shape[2]
    total = ORI_MAX * rows_local
    taps = jnp.broadcast_to(interp_index.reshape(2, total, 1), (2, total, LANES))
    frac = jnp.broadcast_to(interp_frac.reshape(total, 1), (total, LANES))
    onehot = (class_ids[:, None] == jnp.arange(CLASSES, dtype=jnp.int32)[None, :]).astype(
        jnp.bfloat16
    )
    ctf_rows = jnp.dot(
        onehot, ctf_table.reshape(CLASSES, -1), preferred_element_type=jnp.float32
    ).reshape(PART_DEV, rows_local, N_GRP, 1, COLS)
    by_group = spectra.reshape(PART_DEV, rows_local, 2, N_GRP, COLS).transpose(0, 1, 3, 2, 4)
    weighted = (
        (ctf_rows * by_group.astype(jnp.float32))
        .astype(jnp.bfloat16)
        .reshape(PART_DEV, rows_local, 2 * NF)
    )
    row_phase = lax.dynamic_index_in_dim(
        jnp.asarray(row_table()), lax.axis_index("grp"), 0, keepdims=False
    )
    partial = score(
        ori_count, buffer, taps, frac, weighted, jnp.asarray(column_table()), row_phase
    )
    parts = lax.all_to_all(partial, "grp", split_axis=0, concat_axis=0, tiled=True)
    return jnp.sum(parts, axis=0)


def solution(mesh):
    return jax.shard_map(
        shards,
        mesh=mesh,
        in_specs=(
            P("slab", "grp", None),
            P("slab", "grp", None, None),
            P(None, "slab", None, "grp"),
            P("slab", None, "grp"),
            P("slab"),
            P("slab", "grp", None),
            P("slab"),
            P(None, "grp", None),
        ),
        out_specs=P("slab", "grp"),
        check_vma=False,
    )
```

time: 337 us -> 179 us (0.53)
  local copies, waits for them, and re-layouts: 57.5 us -> 17.4 us
  matrix products: 36.1 us -> 0.68 us
  waiting for transfers between devices: 133 us -> 99 us
  loops' own time: 26 us -> 0 us
  other arithmetic: 26.5 us -> 3.37 us
  between operations: 13.7 us -> 0.8 us
  Pallas kernels: 0 us -> 8.11 us
  blocking collectives: 10.8 us -> 17.8 us
    while x8 -> x0, local copies, waits for them, and re-layouts: 36 us -> none
    dot_general x12 -> x0, matrix products: 35.7 us -> none  [the longest x8 27 us: shift_score(): lax.dot_general(weighted, flat_refs, (((1,), (1,)), ((), ())), preferred_...]
    another operation x1 -> x0, loops' own time: 26 us -> none  [shards(): blocks_out = lax.map(orient_score, jnp.arange(ORI_MAX, dtype=jnp.int32))]
    reduce_scatter x1 -> x0, waiting for transfers between devices: 18.3 us -> none  [shards(): lax.psum_scatter(partial_scores, 'grp', scatter_dimension=1, tiled=True)]
    another operation x9 -> x0, other arithmetic: 17.8 us -> none
    all_to_all x1, waiting for transfers between devices: 98 us -> 82.5 us  [shards(): lax.all_to_all(outgoing, 'slab', split_axis=0, concat_axis=0, tiled=True)]
    gather x3 -> x0, local copies, waits for them, and re-layouts: 12.1 us -> none  [the longest x1 7.54 us: shards(): picked = jnp.take(row_table, jnp.maximum(slot_map, 0).reshape(-1), axis=0)]
    pallas_call x0 -> x3, Pallas kernels: none -> 8.11 us  [the longest x1 5.05 us: score(): pl.pallas_call(score_kernel, in_specs=[pl.BlockSpec(memory_space=pltpu.SM...]
  transfers between devices with their start and end apart: 3 -> 2, of which waited for: 3 -> 2; matrix products, arithmetic and copies ran while one was open for 0% -> 9% of each run, Pallas kernels for 0% -> 0%
where the time goes in v1:
time: 179 us; the launch traced here: 178 us
  waiting for transfers between devices  99 us (55%)
  starting transfers between devices  30.5 us (17%)
  blocking collectives  17.8 us (10%)
  local copies, waits for them, and re-layouts  17.4 us (10%)
  Pallas kernels  8.11 us (5%)
  other arithmetic  3.37 us (2%)
    all_to_all x1, waiting for transfers between devices, shards(): lax.all_to_all(outgoing, 'slab', split_axis=0, concat_axis=0, tiled=True)  82.5 us
    all_to_all x1, starting transfers between devices, shards(): lax.all_to_all(planes, 'slab', split_axis=0, concat_axis=0, tiled=True)  20.6 us
    all_to_all x1, waiting for transfers between devices, shards(): lax.all_to_all(planes, 'slab', split_axis=0, concat_axis=0, tiled=True)  16.5 us
    all_gather x1, blocking collectives, shards(): table = lax.all_gather(slab_planes, 'grp', axis=0)  10.8 us
    all_to_all x1, starting transfers between devices, shards(): lax.all_to_all(outgoing, 'slab', split_axis=0, concat_axis=0, tiled=True)  9.97 us
    all_to_all x1, blocking collectives, shards(): lax.all_to_all(partial, 'grp', split_axis=0, concat_axis=0, tiled=True)  7.03 us
    pallas_call x1, Pallas kernels, score(): pl.pallas_call(score_kernel, in_specs=[pl.BlockSpec(memory_space=pltpu.SM...  5.05 us
    unnamed x17, local copies, waits for them, and re-layouts  4.45 us
  transfers between devices with their start and end apart: 2, of which 2 were waited for; matrix products, arithmetic and copies ran while one was open for 9% of the time, Pallas kernels for 0%

profile of v1, /device:TPU:1, one launch (start us, length us, event | category | flops | bytes accessed | tf_op | source)
XLA Modules:
  0.0 177.8 jit_solution(11797904891765245020)
XLA Ops:
  0.0 0.0 copy-start.1
  0.0 1.0 copy-done.1
  1.0 0.0 copy-start.2
  1.0 0.9 copy-done.2
  2.0 1.2 shard_map.109
  3.2 20.6 %all-to-all-start = ((bf16[128,4,128]{2,1,0:T(4,128)(2,1)}), bf16[128,4,128]{2,1,0:T(4,128)(2,1)S(1)}, u32[]{:S(2)}, u32[]{:S(2)}) async-start(bf16[128,4,128]{2,1,0:T(4,128)(2,1)} %bitcast), calls=%async_computation | async-start | bytes 262144 | tf_op jit(solution)/shard_map/all_to_all | solution.py:201
  23.8 0.7 and_or_fusion
  24.5 0.1 copy.26
  24.6 0.1 reshape.56
  24.7 16.5 %all-to-all-done = bf16[128,4,128]{2,1,0:T(4,128)(2,1)S(1)} async-done(((bf16[128,4,128]{2,1,0:T(4,128)(2,1)}), bf16[128,4,128]{2,1,0:T(4,128)(2,1)S(1)}, u32[]{:S(2)}, u32[]{:S(2)}) %all-to-all-start) | async-done | bytes 131104 | tf_op jit(solution)/shard_map/all_to_all | solution.py:201
  41.2 10.8 %all_gather.7.table_ref = bf16[4,512,128]{2,1,0:T(8,128)(2,1)S(1)} all-gather(bf16[1,512,128]{2,1,0:T(8,128)(2,1)S(1)} %bitcast.26), channel_id=1, replica_groups=mesh['slab'=128,'grp'=4] {'grp'}, dimensions={0}, use_global_device_ids=true | all-gather | bytes 655360 | tf_op jit(solution)/shard_map/all_gather | solution.py:202
  52.0 0.3 broadcast_in_dim.10.place_ref
  52.4 1.8 %shard_map.110 = bf16[2048,512]{1,0:T(8,128)(2,1)S(1)} custom-call(s32[2048,128]{1,0:T(8,128)S(1)} %broadcast_in_dim.10.place_ref, bf16[4,512,128]{2,1,0:T(8,128)(2,1)S(1)} %all_gather.7.table_ref), custom_call_target="tpu_custom_call" | custom-call | flops 1073741824 | bytes 4194304 | tf_op jit(solution)/shard_map/pallas_call | solution.py:113
  54.2 0.0 copy-start
  54.2 1.3 copy-done
  55.5 0.0 copy-start.4
  55.5 10.0 %all-to-all-start.1 = ((bf16[128,16,512]{2,1,0:T(8,128)(2,1)}), bf16[128,16,512]{2,1,0:T(8,128)(2,1)S(1)}, u32[]{:S(2)}, u32[]{:S(2)}) async-start(bf16[128,16,512]{2,1,0:T(8,128)(2,1)} %bitcast.24), calls=%async_computation.1 | async-start | bytes 4194304 | tf_op jit(solution)/shard_map/all_to_all | solution.py:206
  65.5 0.0 copy-start.7
  65.5 0.0 copy-done.4
  65.5 1.1 copy.32
  66.6 2.0 %reshape.54 = bf16[64,4,64,16]{2,1,0,3:T(4,128)(2,1)S(1)} reshape(bf16[16384,16]{0,1:T(8,128)(2,1)} %bitcast.25) | data formatting | bytes 1048576 | tf_op jit(solution)/shard_map/reshape.17
  68.7 0.0 copy-done.7
  68.7 0.7 fusion.2
  69.3 0.6 copy.28
  70.0 3.1 %reshape.57 = f32[8,64,2,4,64]{4,3,2,1,0:T(4,128)} reshape(bf16[8,64,512]{2,1,0:T(8,128)(2,1)} %param.16) | data formatting | bytes 1572864 | tf_op jit(solution)/shard_map/convert_element_type | solution.py:220
  73.1 2.1 %fusion.1 = bf16[8,64,4,2,64]{4,1,2,3,0:T(8,128)(2,1)S(1)} fusion(f32[8,64,2,4,64]{4,3,2,1,0:T(4,128)} %reshape.57, f32[8,64,4,64]{3,1,2,0:T(8,128)S(1)} %copy.28), kind=kLoop, calls=%fused_computation.2 | loop fusion | flops 524288 | bytes 2097152 | tf_op jit(solution)/shard_map/convert_element_type | solution.py:221
  75.1 0.0 copy-start.5
  75.1 0.0 copy-start.6
  75.2 0.0 copy-start.3
  75.2 2.1 %copy.30 = bf16[8,64,4,2,64]{4,3,2,1,0:T(2,128)(2,1)} copy(bf16[8,64,4,2,64]{4,1,2,3,0:T(8,128)(2,1)S(1)} %fusion.1) | data formatting | bytes 1048576 | tf_op jit(solution)/shard_map/convert_element_type | solution.py:221
  77.2 3.4 %reshape.55.weighted_ref = bf16[8,64,512]{2,1,0:T(8,128)(2,1)S(1)} reshape(bf16[8,64,4,2,64]{4,3,2,1,0:T(2,128)(2,1)} %copy.30) | data formatting | bytes 1048576 | tf_op jit(solution)/shard_map/reshape | solution.py:222
  80.6 0.0 copy-done.5
  80.6 0.1 broadcast_in_dim.22
  80.7 0.0 copy-done.6
  80.7 0.1 broadcast_in_dim.24
  81.5 0.8 dynamic-slice_bitcast_fusion.row_ref
  82.2 82.5 %all-to-all-done.1 = bf16[128,16,512]{2,1,0:T(8,128)(2,1)S(1)} async-done(((bf16[128,16,512]{2,1,0:T(8,128)(2,1)}), bf16[128,16,512]{2,1,0:T(8,128)(2,1)S(1)}, u32[]{:S(2)}, u32[]{:S(2)}) %all-to-all-start.1) | async-done | bytes 2097184 | tf_op jit(solution)/shard_map/all_to_all | solution.py:206
  164.7 0.2 broadcast_in_dim.23.tap_ref
  164.9 0.1 broadcast_in_dim.25.frac_ref
  165.1 0.0 copy-done.3
  165.1 5.1 %shard_map.111 = f32[4,8,128]{2,1,0:T(8,128)S(1)} custom-call(s32[1]{0:T(128)S(6)} %copy.40.count_ref, bf16[2048,512]{1,0:T(8,128)(2,1)S(1)} %bitcast.23, s32[2,512,128]{2,1,0:T(8,128)S(1)} %broadcast_in_dim.23.tap_ref, f32[512,128]{1,0:T(8,128)S(1)} %broadcast_in_dim.25.frac_ref, bf16[8,64,512]{2,1,0:T(8,128)(2,1)S(1)} %reshape.55.weighted_ref, ...), custom_call_target="tpu_custom_call" | custom-call | flops 4294967296 | bytes 4194304 | tf_op jit(solution)/shard_map/pallas_call | solution.py:183
  170.1 7.0 %all_to_all.25 = f32[4,8,128]{2,1,0:T(8,128)S(1)} all-to-all(f32[4,8,128]{2,1,0:T(8,128)S(1)} %shard_map.111), channel_id=1, replica_groups=mesh['slab'=128,'grp'=4] {'grp'}, dimensions={0} | all-to-all | bytes 32768 | tf_op jit(solution)/shard_map/all_to_all | solution.py:230
  177.2 0.6 reduce_sum.9
Async XLA Ops:
  0.0 1.0 copy-start.1
  1.0 0.9 copy-start.2
  3.2 38.0 %all-to-all-start = ((bf16[128,4,128]{2,1,0:T(4,128)(2,1)}), bf16[128,4,128]{2,1,0:T(4,128)(2,1)S(1)}, u32[]{:S(2)}, u32[]{:S(2)}) async-start(bf16[128,4,128]{2,1,0:T(4,128)(2,1)} %bitcast), calls=%async_computation | async-start | bytes 262144 | tf_op jit(solution)/shard_map/all_to_all | solution.py:201
  54.2 1.3 copy-start
  55.5 10.0 %copy-start.4 = (bf16[16,64,256]{2,1,0:T(8,128)(2,1)S(1)}, bf16[16,64,256]{2,1,0:T(8,128)(2,1)}, u32[]{:S(2)}) copy-start(bf16[16,64,256]{2,1,0:T(8,128)(2,1)} %param.18) | copy-start | bytes 1572868
  55.5 109.2 %all-to-all-start.1 = ((bf16[128,16,512]{2,1,0:T(8,128)(2,1)}), bf16[128,16,512]{2,1,0:T(8,128)(2,1)S(1)}, u32[]{:S(2)}, u32[]{:S(2)}) async-start(bf16[128,16,512]{2,1,0:T(8,128)(2,1)} %bitcast.24), calls=%async_computation.1 | async-start | bytes 4194304 | tf_op jit(solution)/shard_map/all_to_all | solution.py:206
  65.5 3.2 %copy-start.7 = (s32[8]{0:T(128)S(1)}, s32[8]{0:T(128)}, u32[]{:S(2)}) copy-start(s32[8]{0:T(128)} %param.17) | copy-start | bytes 100
  75.1 5.5 %copy-start.5 = (s32[2,1,8,64]{3,2,1,0:T(8,128)S(1)}, s32[2,1,8,64]{3,2,1,0:T(8,128)}, u32[]{:S(2)}) copy-start(s32[2,1,8,64]{3,2,1,0:T(8,128)} %param.13) | copy-start | bytes 12292
  75.1 5.6 %copy-start.6 = (f32[1,8,64]{2,1,0:T(8,128)S(1)}, f32[1,8,64]{2,1,0:T(8,128)}, u32[]{:S(2)}) copy-start(f32[1,8,64]{2,1,0:T(8,128)} %param.14) | copy-start | bytes 6148
  75.2 89.9 %copy-start.3 = (bf16[1024,256]{1,0:T(8,128)(2,1)S(1)}, bf16[1024,256]{1,0:T(8,128)(2,1)}, u32[]{:S(2)}) copy-start(bf16[1024,256]{1,0:T(8,128)(2,1)} %constant.27.clone.col_ref) | copy-start | bytes 1572868

commit v2 on v1

v2 whole, which is shorter than its diff:
```python
import math

import jax
import jax.numpy as jnp
import ml_dtypes
import numpy as np
from jax import lax
from jax.experimental import pallas as pl
from jax.experimental.pallas import tpu as pltpu
from jax.sharding import Mesh
from jax.sharding import PartitionSpec as P

NF = 256
CAP = 16
ORI_MAX = 8
TSIDE = 8
PART_DEV = 8
TRANS = 64
N_GRP = 4
COLS = NF // N_GRP
LANES = 2 * COLS
SLAB_ROWS = 512
SLOTS = 2048
TAKES = ORI_MAX * COLS
PARTICLE_ROWS = PART_DEV * COLS
EXTRA_ROWS = 32
VMEM_BYTES = 48 * 1024 * 1024
SLAB_AXES = ("y", "h", "l", "c")
ROW_AXES = ("x", "y", "l", "c")


def split_bf16(values):
    high = values.astype(ml_dtypes.bfloat16)
    low = (values - high.astype(np.float64)).astype(ml_dtypes.bfloat16)
    return high, low


def fourier_tables():
    index = np.arange(NF)
    angle = 2.0 * math.pi / NF * ((index[:, None] * index[None, :]) % NF)
    table = np.concatenate([np.cos(angle), np.sin(angle)], axis=1) / math.sqrt(NF)
    return np.stack(split_bf16(table))


def column_table():
    b = np.arange(TRANS) % TSIDE - TSIDE // 2
    v = np.arange(NF)
    angle = -2.0 * math.pi / NF * ((b[None, :] * v[:, None]) % NF)
    fr = np.cos(angle).reshape(N_GRP, COLS, TRANS) / NF
    fi = np.sin(angle).reshape(N_GRP, COLS, TRANS) / NF
    with_er = np.concatenate([fr, fr, -fi, fi], axis=1)
    with_ei = np.concatenate([-fi, -fi, -fr, fr], axis=1)
    high, low = split_bf16(np.concatenate([with_er, with_ei], axis=2))
    return np.concatenate([high, low], axis=2)


def row_table():
    a = np.arange(TRANS) // TSIDE - TSIDE // 2
    u = np.arange(NF)
    angle = -2.0 * math.pi / NF * ((a[None, :] * u[:, None]) % NF)
    table = np.concatenate([np.cos(angle), np.sin(angle)], axis=1).astype(np.float32)
    return table.reshape(N_GRP, COLS, 2 * TRANS)


def down_rows(row):
    return jnp.broadcast_to(row, (LANES, LANES)).T


def fourier_kernel(x_ref, table_ref, out_ref, wide):
    contract = (((1,), (1,)), ((), ()))
    for ky in range(2):
        lines = x_ref[ky]
        turned = jnp.concatenate([lines[:, NF:], -lines[:, :NF]], axis=1)
        both = jnp.concatenate([lines, turned], axis=0)
        high = both.astype(jnp.bfloat16)
        low = (both - high.astype(jnp.float32)).astype(jnp.bfloat16)

        def product(table, part):
            return lax.dot_general(table, part, contract, preferred_element_type=jnp.float32)

        result = (product(table_ref[0], low) + product(table_ref[1], high)) + product(
            table_ref[0], high
        )
        wide[pl.ds(ky, NF, stride=2), :] = result
    rest = 32
    for y in range(4):
        for h in range(4):
            out_ref[(h * 4 + y) * rest : (h * 4 + y + 1) * rest, :] = wide[
                (y * 4 + h) * rest : (y * 4 + h + 1) * rest, :
            ].astype(jnp.bfloat16)


def fourier(pencils, table):
    return pl.pallas_call(
        fourier_kernel,
        out_shape=jax.ShapeDtypeStruct((2 * NF, LANES), jnp.bfloat16),
        scratch_shapes=[pltpu.VMEM((2 * NF, LANES), jnp.float32)],
        compiler_params=pltpu.CompilerParams(vmem_limit_bytes=VMEM_BYTES),
        cost_estimate=pl.CostEstimate(
            flops=6 * NF * NF * 2 * NF, bytes_accessed=1 << 20, transcendentals=0
        ),
    )(pencils, table)


def weigh_kernel(class_ref, spectra_ref, ctf_ref, taps_ref, out_ref):
    for particle in range(PART_DEV):
        factor = ctf_ref[class_ref[particle]].astype(jnp.float32)
        lines = spectra_ref[particle].astype(jnp.float32)
        real = lines[:, :NF] * factor
        imag = lines[:, NF:] * factor
        for part in range(N_GRP):
            span = slice(part * COLS, (part + 1) * COLS)
            out_ref[part, particle * COLS : (particle + 1) * COLS, :] = jnp.concatenate(
                [real[:, span], imag[:, span]], axis=1
            ).astype(jnp.bfloat16)
    taps = taps_ref[...]
    place = taps[:8]
    place_high = jnp.floor(place * (1.0 / 16.0))
    place_low = place - 16.0 * place_high
    frac = taps[8:12]
    first = frac.astype(jnp.bfloat16).astype(jnp.float32)
    second = (frac - first).astype(jnp.bfloat16).astype(jnp.float32)
    third = frac - first - second
    extra = jnp.concatenate(
        [place_high, place_low, first, second, third, jnp.zeros_like(frac)], axis=0
    ).astype(jnp.bfloat16)
    for part in range(N_GRP):
        out_ref[part, PARTICLE_ROWS:, :] = extra


def weigh(class_ids, spectra, ctf_table, taps):
    vmem = pl.BlockSpec(memory_space=pltpu.VMEM)
    return pl.pallas_call(
        weigh_kernel,
        in_specs=[pl.BlockSpec(memory_space=pltpu.SMEM)] + [vmem] * 3,
        out_specs=vmem,
        out_shape=jax.ShapeDtypeStruct((N_GRP, PARTICLE_ROWS + EXTRA_ROWS, LANES), jnp.bfloat16),
        compiler_params=pltpu.CompilerParams(vmem_limit_bytes=VMEM_BYTES),
        cost_estimate=pl.CostEstimate(flops=1 << 20, bytes_accessed=2 << 20, transcendentals=0),
    )(class_ids, spectra, ctf_table, taps)


PICK_STEP = 1024


def pick_kernel(order_ref, place_ref, table_ref, out_ref):
    del order_ref
    lane = lax.broadcasted_iota(jnp.int32, (LANES, LANES), 1).astype(jnp.float32)
    blocks = []
    for row in range(PICK_STEP // LANES):
        place = down_rows(place_ref[row : row + 1, :])
        blocks.append(
            jnp.concatenate(
                [
                    jnp.where(place == lane + float(first), 1.0, 0.0).astype(jnp.bfloat16)
                    for first in range(0, SLAB_ROWS, LANES)
                ],
                axis=1,
            )
        )
    hits = jnp.concatenate(blocks, axis=0)
    out_ref[...] = jnp.dot(hits, table_ref[...], preferred_element_type=jnp.float32).astype(
        jnp.bfloat16
    )


def pick(order, place, table):
    total = place.size
    halves = total // N_GRP // PICK_STEP
    return pl.pallas_call(
        pick_kernel,
        grid_spec=pltpu.PrefetchScalarGridSpec(
            num_scalar_prefetch=1,
            grid=(N_GRP, halves),
            in_specs=[
                pl.BlockSpec(
                    (PICK_STEP // LANES, LANES), lambda g, i, order: (order[g] * halves + i, 0)
                ),
                pl.BlockSpec((SLAB_ROWS, LANES), lambda g, i, order: (0, 0)),
            ],
            out_specs=pl.BlockSpec((PICK_STEP, LANES), lambda g, i, order: (g * halves + i, 0)),
        ),
        out_shape=jax.ShapeDtypeStruct((total, LANES), jnp.bfloat16),
        compiler_params=pltpu.CompilerParams(vmem_limit_bytes=VMEM_BYTES),
        cost_estimate=pl.CostEstimate(
            flops=2 * total * SLAB_ROWS * LANES, bytes_accessed=4 << 20, transcendentals=0
        ),
    )(order, place, table)


def score_kernel(order_ref, buffer_ref, weighted_ref, col_ref, row_ref, out_ref, mix, slices):
    del order_ref
    lane = lax.broadcasted_iota(jnp.int32, (LANES, LANES), 1).astype(jnp.float32)
    extra = weighted_ref[PARTICLE_ROWS:, :].astype(jnp.float32)
    place = 16.0 * extra[:8] + extra[8:16]
    frac = extra[16:20] + extra[20:24] + extra[24:28]
    for row in range(8):
        column = down_rows(place[row : row + 1])
        for first in range(0, SLOTS, LANES):
            mix[row * LANES : (row + 1) * LANES, first : first + LANES] = jnp.where(
                column == lane + float(first), 1.0, 0.0
            ).astype(jnp.bfloat16)
    taken = jnp.dot(
        mix[...], buffer_ref[...].reshape(SLOTS, LANES), preferred_element_type=jnp.float32
    )
    for row in range(4):
        share = down_rows(frac[row : row + 1])
        span = slice(row * LANES, (row + 1) * LANES)
        slices[span, :] = (1.0 - share) * taken[span] + share * taken[TAKES:][span]
    phase_rows = row_ref[...]
    left = lax.broadcasted_iota(jnp.int32, (PART_DEV, LANES), 1) < TRANS
    weight = weighted_ref[:PARTICLE_ROWS, :].astype(jnp.float32).reshape(PART_DEV, COLS, LANES)
    for pair in range(ORI_MAX // 2):
        done = []
        for orient in (2 * pair, 2 * pair + 1):
            plain = slices[orient * COLS : (orient + 1) * COLS, :]
            swapped = pltpu.roll(plain, COLS, 1)
            products = jnp.concatenate(
                [
                    (weight * plain[None]).astype(jnp.bfloat16),
                    (weight * swapped[None]).astype(jnp.bfloat16),
                ],
                axis=-1,
            ).reshape(PARTICLE_ROWS, 2 * LANES)
            columns = jnp.dot(products, col_ref[...], preferred_element_type=jnp.float32)
            columns = columns[:, :LANES] + columns[:, LANES:]
            summed = jnp.sum(columns.reshape(PART_DEV, COLS, LANES) * phase_rows[None], axis=1)
            done.append(summed + pltpu.roll(summed, TRANS, 1))
        out_ref[pair] = jnp.where(left, done[0], done[1])


def score(order, buffer, weighted, col_phase, row_phase):
    return pl.pallas_call(
        score_kernel,
        grid_spec=pltpu.PrefetchScalarGridSpec(
            num_scalar_prefetch=1,
            grid=(N_GRP,),
            in_specs=[
                pl.BlockSpec(
                    (SLOTS // CAP, None, CAP, LANES), lambda i, order: (0, order[i], 0, 0)
                ),
                pl.BlockSpec(
                    (None, PARTICLE_ROWS + EXTRA_ROWS, LANES), lambda i, order: (i, 0, 0)
                ),
                pl.BlockSpec((2 * LANES, 2 * LANES), lambda i, order: (0, 0)),
                pl.BlockSpec((COLS, LANES), lambda i, order: (0, 0)),
            ],
            out_specs=pl.BlockSpec(
                (None, ORI_MAX // 2, PART_DEV, LANES), lambda i, order: (order[i], 0, 0, 0)
            ),
            scratch_shapes=[
                pltpu.VMEM((2 * TAKES, SLOTS), jnp.bfloat16),
                pltpu.VMEM((TAKES, LANES), jnp.float32),
            ],
        ),
        out_shape=jax.ShapeDtypeStruct((N_GRP, ORI_MAX // 2, PART_DEV, LANES), jnp.float32),
        compiler_params=pltpu.CompilerParams(vmem_limit_bytes=VMEM_BYTES),
        cost_estimate=pl.CostEstimate(flops=8 << 30, bytes_accessed=4 << 20, transcendentals=0),
    )(order, buffer, weighted, col_phase, row_phase)


def exchange(values, axes):
    return lax.all_to_all(values, axes, split_axis=0, concat_axis=0, tiled=True)


def own_part(table, axis):
    return lax.dynamic_index_in_dim(jnp.asarray(table), lax.axis_index(axis), 0, keepdims=False)


def shards(pencils, send_map, interp_index, interp_frac, ori_count, spectra, class_ids, ctf_table):
    here = lax.axis_index("h")
    turn = jnp.arange(4, dtype=jnp.int32)
    planes = exchange(fourier(pencils, jnp.asarray(fourier_tables())), "x")
    planes = planes.reshape(4, 4, 32, LANES).transpose(1, 0, 2, 3).reshape(2 * NF, LANES)

    wanted, planes = lax.optimization_barrier((send_map[0, 0], planes))
    table = exchange(planes, SLAB_AXES)
    wanted = jnp.maximum(wanted, 0)
    place = ((wanted & (NF - 2)) << 1) | ((wanted >> 8) << 1) | (wanted & 1)
    place = place.reshape(4, 4, 8, CAP).transpose(0, 2, 1, 3).reshape(CAP, LANES)
    place = place.astype(jnp.float32)
    maps = [
        lax.ppermute(
            place,
            ("h", "x"),
            [(slab * 4 + g, (g + j) % 4 * 4 + slab) for g in range(4) for slab in range(4)],
        )
        for j in range(4)
    ]
    outgoing = pick((here - turn) % 4, jnp.concatenate(maps, axis=0), table)

    slot = interp_index.reshape(2, TAKES)
    source = slot >> 4
    source = (((source >> 3) & 3) << 5) | ((source >> 5) << 3) | (source & 7)
    slot = ((source << 4) | (slot & 15)).astype(jnp.float32)
    taps = jnp.concatenate([slot.reshape(8, LANES), interp_frac.reshape(4, LANES)], axis=0)
    weighted, outgoing = lax.optimization_barrier(
        (weigh(class_ids, spectra, ctf_table, taps), outgoing)
    )
    buffer = exchange(outgoing, ROW_AXES).reshape(SLOTS // CAP, 4, CAP, LANES)
    owners = [lax.dynamic_index_in_dim(weighted, here, 0, keepdims=False)]
    for k in range(1, 4):
        block = lax.dynamic_index_in_dim(weighted, (here - k) % 4, 0, keepdims=False)
        owners.append(lax.ppermute(block, "h", [((i + k) % 4, i) for i in range(4)]))
    partial = score(
        (here + turn) % 4,
        buffer,
        jnp.stack(owners),
        own_part(column_table(), "h"),
        own_part(row_table(), "x"),
    )
    parts = exchange(partial.reshape(16, PART_DEV, LANES), ("h", "x"))
    total = jnp.sum(parts, axis=0)
    orient = 2 * lax.axis_index("x") + jnp.arange(LANES, dtype=jnp.int32) // TRANS
    return jnp.where(orient[None, :] < ori_count[0], total, 0.0)


def solution(mesh):
    fine = Mesh(mesh.devices.reshape(4, 4, 4, 2, 4), SLAB_AXES + ("x",))
    return jax.shard_map(
        shards,
        mesh=fine,
        in_specs=(
            P(SLAB_AXES, "x", None),
            P(SLAB_AXES, "x", None, None),
            P(None, SLAB_AXES, None, "x"),
            P(SLAB_AXES, None, "x"),
            P(SLAB_AXES),
            P(SLAB_AXES, "x", None),
            P(SLAB_AXES),
            P(None, "x", None),
        ),
        out_specs=P(SLAB_AXES, "x"),
        check_vma=False,
    )
```

time: 179 us -> 195 us (1.089)
  starting transfers between devices: 30.5 us -> 92.6 us
  waiting for transfers between devices: 99 us -> 68.6 us
  blocking collectives: 17.8 us -> 0 us
  Pallas kernels: 8.11 us -> 21.2 us
  local copies, waits for them, and re-layouts: 17.4 us -> 7.47 us
    all_to_all x2 -> x4, waiting for transfers between devices: 99 us -> 30.1 us  [exchange(): return lax.all_to_all(values, axes, split_axis=0, concat_axis=0, tiled=True)]
    ppermute x0 -> x7, starting transfers between devices: none -> 48.5 us  [the longest x4 30.6 us: shards(): lax.ppermute(place, ('h', 'x'), [(slab * 4 + g, (g + j) % 4 * 4 + slab) f...]
    ppermute x0 -> x7, waiting for transfers between devices: none -> 38.4 us  [the longest x3 38.4 us: shards(): lax.ppermute(block, 'h', [((i + k) % 4, i) for i in range(4)])]
    all_to_all x2 -> x4, starting transfers between devices: 30.5 us -> 44.1 us  [exchange(): return lax.all_to_all(values, axes, split_axis=0, concat_axis=0, tiled=True)]
    pallas_call x2 -> x3, Pallas kernels: 6.86 us -> 20 us  [the longest x1 14.7 us: score(): pl.pallas_call(score_kernel, grid_spec=pltpu.PrefetchScalarGridSpec(num_s...]
    all_gather x1 -> x0, blocking collectives: 10.8 us -> none  [shards(): table = lax.all_gather(slab_planes, 'grp', axis=0)]
    all_to_all x1 -> x0, blocking collectives: 7.03 us -> none  [shards(): lax.all_to_all(partial, 'grp', split_axis=0, concat_axis=0, tiled=True)]
    convert_element_type x2 -> x3, local copies, waits for them, and re-layouts: 5.16 us -> 0.19 us  [the longest x2 0.12 us: shards(): place = place.astype(jnp.float32)]
  transfers between devices with their start and end apart: 2 -> 11, of which waited for: 2 -> 5; matrix products, arithmetic and copies ran while one was open for 9% -> 2% of each run, Pallas kernels for 0% -> 0%
where the time goes in v2:
time: 195 us; the launch traced here: 192 us
  starting transfers between devices  92.6 us (47%)
  waiting for transfers between devices  68.6 us (35%)
  Pallas kernels  21.2 us (11%)
  local copies, waits for them, and re-layouts  7.47 us (4%)
    all_to_all x4, starting transfers between devices, exchange(): return lax.all_to_all(values, axes, split_axis=0, concat_axis=0, tiled=True)  44.1 us
    ppermute x3, waiting for transfers between devices, shards(): lax.ppermute(block, 'h', [((i + k) % 4, i) for i in range(4)])  38.4 us
    ppermute x4, starting transfers between devices, shards(): lax.ppermute(place, ('h', 'x'), [(slab * 4 + g, (g + j) % 4 * 4 + slab) f...  30.6 us
    all_to_all x4, waiting for transfers between devices, exchange(): return lax.all_to_all(values, axes, split_axis=0, concat_axis=0, tiled=True)  30.1 us
    ppermute x3, starting transfers between devices, shards(): lax.ppermute(block, 'h', [((i + k) % 4, i) for i in range(4)])  17.9 us
    pallas_call x1, Pallas kernels, score(): pl.pallas_call(score_kernel, grid_spec=pltpu.PrefetchScalarGridSpec(num_s...  14.7 us
    pallas_call x1, Pallas kernels, pick(): pl.pallas_call(pick_kernel, grid_spec=pltpu.PrefetchScalarGridSpec(num_sc...  4.5 us
    unnamed x13, local copies, waits for them, and re-layouts  4.13 us
  transfers between devices with their start and end apart: 11, of which 5 were waited for; matrix products, arithmetic and copies ran while one was open for 2% of the time, Pallas kernels for 0%

profile of v2, /device:TPU:1, one launch (start us, length us, event | category | flops | bytes accessed | tf_op | source)
XLA Modules:
  0.0 192.3 jit_solution(8198077921304116995)
XLA Ops:
  0.0 0.0 copy-start.1
  0.0 1.0 copy-done.1
  1.0 0.0 copy-start.4
  1.0 0.9 copy-done.4
  2.0 0.0 copy-start.2
  2.0 0.0 copy-start.3
  2.0 0.0 copy-start.5
  2.0 1.3 shard_map.110
  3.3 4.8 %all-to-all-start = ((bf16[4,128,128]{2,1,0:T(8,128)(2,1)}), bf16[4,128,128]{2,1,0:T(8,128)(2,1)S(1)}, u32[]{:S(2)}, u32[]{:S(2)}) async-start(bf16[4,128,128]{2,1,0:T(8,128)(2,1)} %bitcast.2), calls=%async_computation | async-start | bytes 262144 | tf_op jit(solution)/shard_map/all_to_all | solution.py:263
  8.1 0.7 or_convert_fusion.1
  8.8 0.8 copy.14
  9.6 0.1 reshape.72
  9.7 0.8 reshape.62
  10.4 2.5 %all-to-all-done = bf16[4,128,128]{2,1,0:T(8,128)(2,1)S(1)} async-done(((bf16[4,128,128]{2,1,0:T(8,128)(2,1)}), bf16[4,128,128]{2,1,0:T(8,128)(2,1)S(1)}, u32[]{:S(2)}, u32[]{:S(2)}) %all-to-all-start) | async-done | bytes 131104 | tf_op jit(solution)/shard_map/all_to_all | solution.py:263
  12.9 0.7 copy.15
  13.6 21.2 %all-to-all-start.1 = ((bf16[128,4,128]{2,1,0:T(4,128)(2,1)}), bf16[128,4,128]{2,1,0:T(4,128)(2,1)S(1)}, u32[]{:S(2)}, u32[]{:S(2)}) async-start(bf16[128,4,128]{2,1,0:T(4,128)(2,1)} %bitcast.8), calls=%async_computation.1 | async-start | bytes 262144 | tf_op jit(solution)/shard_map/all_to_all | solution.py:263
  34.8 0.1 convert_element_type.20
  34.9 0.7 collective-permute-start
  35.6 8.5 %collective-permute-start.1 = (f32[16,128]{1,0:T(8,128)S(1)}, f32[16,128]{1,0:T(8,128)S(1)}, u32[]{:S(2)}, u32[]{:S(2)}) collective-permute-start(f32[16,128]{1,0:T(8,128)S(1)} %convert_element_type.20), channel_id=1, source_target_pairs={{0,32},{32,33},{64,34},{96,35},{1,64},{33,65},{65,66},{97,67},{2,9... | collective-permute-start | bytes 24584 | tf_op jit(solution)/shard_map/ppermute | solution.py:283
  44.1 13.5 %collective-permute-start.2 = (f32[16,128]{1,0:T(8,128)S(1)}, f32[16,128]{1,0:T(8,128)S(1)}, u32[]{:S(2)}, u32[]{:S(2)}) collective-permute-start(f32[16,128]{1,0:T(8,128)S(1)} %convert_element_type.20), channel_id=1, source_target_pairs={{0,64},{32,65},{64,66},{96,67},{1,96},{33,97},{65,98},{97,99},{2,0... | collective-permute-start | bytes 24584 | tf_op jit(solution)/shard_map/ppermute | solution.py:283
  57.7 7.9 %collective-permute-start.3 = (f32[16,128]{1,0:T(8,128)S(1)}, f32[16,128]{1,0:T(8,128)S(1)}, u32[]{:S(2)}, u32[]{:S(2)}) collective-permute-start(f32[16,128]{1,0:T(8,128)S(1)} %convert_element_type.20), channel_id=1, source_target_pairs={{0,96},{32,97},{64,98},{96,99},{1,0},{33,1},{65,2},{97,3},{2,32},{... | collective-permute-start | bytes 24584 | tf_op jit(solution)/shard_map/ppermute | solution.py:283
  65.6 0.0 copy-done.2
  65.6 0.0 copy-done.3
  65.6 0.0 copy-done.5
  65.6 0.8 shard_map.109
  66.4 0.0 collective-permute-done
  66.4 0.0 collective-permute-done.1
  66.4 0.0 collective-permute-done.2
  66.4 0.0 collective-permute-done.3
  66.5 0.0 all-to-all-done.1
  66.5 4.5 %shard_map.111 = bf16[8192,128]{1,0:T(8,128)(2,1)S(1)} custom-call(s32[4]{0:T(128)S(1)} %and_select_fusion.order_ref, f32[64,128]{1,0:T(8,128)S(1)} %pad_maximum_fusion.1.place_ref, bf16[512,128]{1,0:T(8,128)(2,1)S(1)} %bitcast.33), custom_call_target="tpu_custom_call" | custom-call | flops 1073741824 | bytes 4194304 | tf_op jit(solution)/shard_map/pallas_call | solution.py:170
  71.0 0.0 copy-start
  71.0 1.3 copy-done
  72.3 9.7 %all-to-all-start.2 = ((bf16[128,64,128]{2,1,0:T(8,128)(2,1)}), bf16[128,64,128]{2,1,0:T(8,128)(2,1)S(1)}, u32[]{:S(2)}, u32[]{:S(2)}) async-start(bf16[128,64,128]{2,1,0:T(8,128)(2,1)} %bitcast.32), calls=%async_computation.2 | async-start | bytes 4194304 | tf_op jit(solution)/shard_map/all_to_all | solution.py:263
  82.1 0.8 dynamic-slice_bitcast_fusion.4.row_ref
  82.9 6.3 %collective-permute-start.4 = (bf16[544,128]{1,0:T(8,128)(2,1)S(1)}, bf16[544,128]{1,0:T(8,128)(2,1)S(1)}, u32[]{:S(2)}, u32[]{:S(2)}) collective-permute-start(bf16[544,128]{1,0:T(8,128)(2,1)S(1)} %get-tuple-element.16), channel_id=1, source_target_pairs={{32,0},{64,32},{96,64},{0,96},{33,1},{65,33},{97,65},{1,97},{34,2}... | collective-permute-start | bytes 417800 | tf_op jit(solution)/shard_map/ppermute | solution.py:304
  89.2 5.6 %collective-permute-start.5 = (bf16[544,128]{1,0:T(8,128)(2,1)S(1)}, bf16[544,128]{1,0:T(8,128)(2,1)S(1)}, u32[]{:S(2)}, u32[]{:S(2)}) collective-permute-start(bf16[544,128]{1,0:T(8,128)(2,1)S(1)} %get-tuple-element.15), channel_id=1, source_target_pairs={{64,0},{96,32},{0,64},{32,96},{65,1},{97,33},{1,65},{33,97},{66,2}... | collective-permute-start | bytes 417800 | tf_op jit(solution)/shard_map/ppermute | solution.py:304
  94.8 6.0 %collective-permute-start.6 = (bf16[544,128]{1,0:T(8,128)(2,1)S(1)}, bf16[544,128]{1,0:T(8,128)(2,1)S(1)}, u32[]{:S(2)}, u32[]{:S(2)}) collective-permute-start(bf16[544,128]{1,0:T(8,128)(2,1)S(1)} %get-tuple-element.14), channel_id=1, source_target_pairs={{96,0},{0,32},{32,64},{64,96},{97,1},{1,33},{33,65},{65,97},{98,2}... | collective-permute-start | bytes 417800 | tf_op jit(solution)/shard_map/ppermute | solution.py:304
  100.9 0.9 dynamic-slice_bitcast_fusion.3.col_ref
  101.8 0.0 collective-permute-done.4
  101.8 37.5 %collective-permute-done.5 = bf16[544,128]{1,0:T(8,128)(2,1)S(1)} collective-permute-done((bf16[544,128]{1,0:T(8,128)(2,1)S(1)}, bf16[544,128]{1,0:T(8,128)(2,1)S(1)}, u32[]{:S(2)}, u32[]{:S(2)}) %collective-permute-start.5) | collective-permute-done | bytes 139296 | tf_op jit(solution)/shard_map/ppermute | solution.py:304
  139.3 1.0 collective-permute-done.6
  140.2 0.1 pad_maximum_fusion.weighted_ref
  140.3 14.6 %all-to-all-done.2 = bf16[128,64,128]{2,1,0:T(8,128)(2,1)S(1)} async-done(((bf16[128,64,128]{2,1,0:T(8,128)(2,1)}), bf16[128,64,128]{2,1,0:T(8,128)(2,1)S(1)}, u32[]{:S(2)}, u32[]{:S(2)}) %all-to-all-start.2) | async-done | bytes 2097184 | tf_op jit(solution)/shard_map/all_to_all | solution.py:263
  154.9 14.7 %shard_map.112 = f32[4,4,8,128]{3,2,1,0:T(8,128)} custom-call(s32[4]{0:T(128)S(1)} %and_select_fusion.1.order_ref, bf16[128,4,16,128]{3,2,1,0:T(8,128)(2,1)S(1)} %bitcast.31, bf16[4,544,128]{2,1,0:T(8,128)(2,1)S(1)} %pad_maximum_fusion.weighted_ref, bf16[256,256]{1,0:T(8,128)(2,1)S(1)} %dynamic-slice_bitcast_fusion.3.col_ref, ...), custom_call_target="tpu_custom_call" | custom-call | flops 8589934592 | bytes 4194304 | tf_op jit(solution)/shard_map/pallas_call | solution.py:233
  169.6 8.4 %all-to-all-start.3 = ((f32[16,8,128]{2,1,0:T(8,128)}), f32[16,8,128]{2,1,0:T(8,128)S(1)}, u32[]{:S(2)}, u32[]{:S(2)}) async-start(f32[16,8,128]{2,1,0:T(8,128)} %bitcast.20), calls=%async_computation.3 | async-start | bytes 131072 | tf_op jit(solution)/shard_map/all_to_all | solution.py:263
  178.6 13.1 %all-to-all-done.3 = f32[16,8,128]{2,1,0:T(8,128)S(1)} async-done(((f32[16,8,128]{2,1,0:T(8,128)}), f32[16,8,128]{2,1,0:T(8,128)S(1)}, u32[]{:S(2)}, u32[]{:S(2)}) %all-to-all-start.3) | async-done | bytes 65568 | tf_op jit(solution)/shard_map/all_to_all | solution.py:263
  191.7 0.6 broadcast_select_fusion
  (9 shorter events, 0.1 us)
Async XLA Ops:
  0.0 1.0 copy-start.1
  1.0 0.9 copy-start.4
  2.0 63.6 %copy-start.2 = (bf16[8,64,512]{2,1,0:T(8,128)(2,1)S(1)}, bf16[8,64,512]{2,1,0:T(8,128)(2,1)}, u32[]{:S(2)}) copy-start(bf16[8,64,512]{2,1,0:T(8,128)(2,1)} %spectra_ref.1) | copy-start | bytes 1572868
  2.0 63.6 %copy-start.3 = (bf16[16,64,256]{2,1,0:T(8,128)(2,1)S(1)}, bf16[16,64,256]{2,1,0:T(8,128)(2,1)}, u32[]{:S(2)}) copy-start(bf16[16,64,256]{2,1,0:T(8,128)(2,1)} %ctf_ref.1) | copy-start | bytes 1572868
  2.0 63.6 %copy-start.5 = (s32[8]{0:T(128)S(1)}, s32[8]{0:T(128)}, u32[]{:S(2)}) copy-start(s32[8]{0:T(128)} %class_ref.1) | copy-start | bytes 100
  3.3 9.7 %all-to-all-start = ((bf16[4,128,128]{2,1,0:T(8,128)(2,1)}), bf16[4,128,128]{2,1,0:T(8,128)(2,1)S(1)}, u32[]{:S(2)}, u32[]{:S(2)}) async-start(bf16[4,128,128]{2,1,0:T(8,128)(2,1)} %bitcast.2), calls=%async_computation | async-start | bytes 262144 | tf_op jit(solution)/shard_map/all_to_all | solution.py:263
  13.6 52.9 %all-to-all-start.1 = ((bf16[128,4,128]{2,1,0:T(4,128)(2,1)}), bf16[128,4,128]{2,1,0:T(4,128)(2,1)S(1)}, u32[]{:S(2)}, u32[]{:S(2)}) async-start(bf16[128,4,128]{2,1,0:T(4,128)(2,1)} %bitcast.8), calls=%async_computation.1 | async-start | bytes 262144 | tf_op jit(solution)/shard_map/all_to_all | solution.py:263
  34.9 31.5 %collective-permute-start = (f32[16,128]{1,0:T(8,128)S(1)}, f32[16,128]{1,0:T(8,128)S(1)}, u32[]{:S(2)}, u32[]{:S(2)}) collective-permute-start(f32[16,128]{1,0:T(8,128)S(1)} %convert_element_type.20), channel_id=1, source_target_pairs={{0,0},{32,1},{64,2},{96,3},{1,32},{33,33},{65,34},{97,35},{2,64},{... | collective-permute-start | bytes 24584 | tf_op jit(solution)/shard_map/ppermute | solution.py:283
  35.6 30.8 %collective-permute-start.1 = (f32[16,128]{1,0:T(8,128)S(1)}, f32[16,128]{1,0:T(8,128)S(1)}, u32[]{:S(2)}, u32[]{:S(2)}) collective-permute-start(f32[16,128]{1,0:T(8,128)S(1)} %convert_element_type.20), channel_id=1, source_target_pairs={{0,32},{32,33},{64,34},{96,35},{1,64},{33,65},{65,66},{97,67},{2,9... | collective-permute-start | bytes 24584 | tf_op jit(solution)/shard_map/ppermute | solution.py:283
  44.1 22.3 %collective-permute-start.2 = (f32[16,128]{1,0:T(8,128)S(1)}, f32[16,128]{1,0:T(8,128)S(1)}, u32[]{:S(2)}, u32[]{:S(2)}) collective-permute-start(f32[16,128]{1,0:T(8,128)S(1)} %convert_element_type.20), channel_id=1, source_target_pairs={{0,64},{32,65},{64,66},{96,67},{1,96},{33,97},{65,98},{97,99},{2,0... | collective-permute-start | bytes 24584 | tf_op jit(solution)/shard_map/ppermute | solution.py:283
  57.7 8.8 %collective-permute-start.3 = (f32[16,128]{1,0:T(8,128)S(1)}, f32[16,128]{1,0:T(8,128)S(1)}, u32[]{:S(2)}, u32[]{:S(2)}) collective-permute-start(f32[16,128]{1,0:T(8,128)S(1)} %convert_element_type.20), channel_id=1, source_target_pairs={{0,96},{32,97},{64,98},{96,99},{1,0},{33,1},{65,2},{97,3},{2,32},{... | collective-permute-start | bytes 24584 | tf_op jit(solution)/shard_map/ppermute | solution.py:283
  71.0 1.3 copy-start
  72.3 82.6 %all-to-all-start.2 = ((bf16[128,64,128]{2,1,0:T(8,128)(2,1)}), bf16[128,64,128]{2,1,0:T(8,128)(2,1)S(1)}, u32[]{:S(2)}, u32[]{:S(2)}) async-start(bf16[128,64,128]{2,1,0:T(8,128)(2,1)} %bitcast.32), calls=%async_computation.2 | async-start | bytes 4194304 | tf_op jit(solution)/shard_map/all_to_all | solution.py:263
  82.9 18.9 %collective-permute-start.4 = (bf16[544,128]{1,0:T(8,128)(2,1)S(1)}, bf16[544,128]{1,0:T(8,128)(2,1)S(1)}, u32[]{:S(2)}, u32[]{:S(2)}) collective-permute-start(bf16[544,128]{1,0:T(8,128)(2,1)S(1)} %get-tuple-element.16), channel_id=1, source_target_pairs={{32,0},{64,32},{96,64},{0,96},{33,1},{65,33},{97,65},{1,97},{34,2}... | collective-permute-start | bytes 417800 | tf_op jit(solution)/shard_map/ppermute | solution.py:304
  89.2 50.0 %collective-permute-start.5 = (bf16[544,128]{1,0:T(8,128)(2,1)S(1)}, bf16[544,128]{1,0:T(8,128)(2,1)S(1)}, u32[]{:S(2)}, u32[]{:S(2)}) collective-permute-start(bf16[544,128]{1,0:T(8,128)(2,1)S(1)} %get-tuple-element.15), channel_id=1, source_target_pairs={{64,0},{96,32},{0,64},{32,96},{65,1},{97,33},{1,65},{33,97},{66,2}... | collective-permute-start | bytes 417800 | tf_op jit(solution)/shard_map/ppermute | solution.py:304
  94.8 45.4 %collective-permute-start.6 = (bf16[544,128]{1,0:T(8,128)(2,1)S(1)}, bf16[544,128]{1,0:T(8,128)(2,1)S(1)}, u32[]{:S(2)}, u32[]{:S(2)}) collective-permute-start(bf16[544,128]{1,0:T(8,128)(2,1)S(1)} %get-tuple-element.14), channel_id=1, source_target_pairs={{96,0},{0,32},{32,64},{64,96},{97,1},{1,33},{33,65},{65,97},{98,2}... | collective-permute-start | bytes 417800 | tf_op jit(solution)/shard_map/ppermute | solution.py:304
  169.6 22.1 %all-to-all-start.3 = ((f32[16,8,128]{2,1,0:T(8,128)}), f32[16,8,128]{2,1,0:T(8,128)S(1)}, u32[]{:S(2)}, u32[]{:S(2)}) async-start(f32[16,8,128]{2,1,0:T(8,128)} %bitcast.20), calls=%async_computation.3 | async-start | bytes 131072 | tf_op jit(solution)/shard_map/all_to_all | solution.py:263

commit v3 on v2

--- a/solution.py
+++ b/solution.py
@@ -26,7 +26,7 @@
 EXTRA_ROWS = 32
 VMEM_BYTES = 48 * 1024 * 1024
 SLAB_AXES = ("y", "h", "l", "c")
-ROW_AXES = ("x", "y", "l", "c")
+ROW_AXES = ("y", "l", "c")
 
 
 def split_bf16(values):
@@ -37,7 +37,8 @@
 
 def fourier_tables():
     index = np.arange(NF)
-    angle = 2.0 * math.pi / NF * ((index[:, None] * index[None, :]) % NF)
+    kz = index.reshape(4, 4, 8, 2).transpose(0, 2, 3, 1).reshape(NF)
+    angle = 2.0 * math.pi / NF * ((kz[:, None] * index[None, :]) % NF)
     table = np.concatenate([np.cos(angle), np.sin(angle)], axis=1) / math.sqrt(NF)
     return np.stack(split_bf16(table))
 
@@ -66,6 +67,19 @@
     return jnp.broadcast_to(row, (LANES, LANES)).T
 
 
+def hit_tiles(row, total):
+    high = jnp.floor(row * (1.0 / LANES))
+    low = down_rows(row - float(LANES) * high).astype(jnp.bfloat16)
+    high = down_rows(high).astype(jnp.bfloat16)
+    lane = lax.broadcasted_iota(jnp.int32, (LANES, LANES), 1).astype(jnp.float32)
+    inner = jnp.where(low == lane.astype(jnp.bfloat16), 1.0, 0.0).astype(jnp.bfloat16)
+    zero = jnp.zeros_like(inner)
+    return [
+        jnp.where(high == jnp.full_like(high, float(tile)), inner, zero)
+        for tile in range(total // LANES)
+    ]
+
+
 def fourier_kernel(x_ref, table_ref, out_ref, wide):
     contract = (((1,), (1,)), ((), ()))
     for ky in range(2):
@@ -82,18 +96,17 @@
             table_ref[0], high
         )
         wide[pl.ds(ky, NF, stride=2), :] = result
-    rest = 32
+    rest = 2 * NF // 4
     for y in range(4):
+        block = wide[y * rest : (y + 1) * rest, :].astype(jnp.bfloat16)
         for h in range(4):
-            out_ref[(h * 4 + y) * rest : (h * 4 + y + 1) * rest, :] = wide[
-                (y * 4 + h) * rest : (y * 4 + h + 1) * rest, :
-            ].astype(jnp.bfloat16)
+            out_ref[(y * 4 + h) * rest : (y * 4 + h + 1) * rest, :] = block
 
 
 def fourier(pencils, table):
     return pl.pallas_call(
         fourier_kernel,
-        out_shape=jax.ShapeDtypeStruct((2 * NF, LANES), jnp.bfloat16),
+        out_shape=jax.ShapeDtypeStruct((8 * NF, LANES), jnp.bfloat16),
         scratch_shapes=[pltpu.VMEM((2 * NF, LANES), jnp.float32)],
         compiler_params=pltpu.CompilerParams(vmem_limit_bytes=VMEM_BYTES),
         cost_estimate=pl.CostEstimate(
@@ -140,66 +153,55 @@
     )(class_ids, spectra, ctf_table, taps)
 
 
-PICK_STEP = 1024
-
-
-def pick_kernel(order_ref, place_ref, table_ref, out_ref):
-    del order_ref
-    lane = lax.broadcasted_iota(jnp.int32, (LANES, LANES), 1).astype(jnp.float32)
-    blocks = []
-    for row in range(PICK_STEP // LANES):
-        place = down_rows(place_ref[row : row + 1, :])
-        blocks.append(
-            jnp.concatenate(
-                [
-                    jnp.where(place == lane + float(first), 1.0, 0.0).astype(jnp.bfloat16)
-                    for first in range(0, SLAB_ROWS, LANES)
-                ],
-                axis=1,
-            )
-        )
-    hits = jnp.concatenate(blocks, axis=0)
-    out_ref[...] = jnp.dot(hits, table_ref[...], preferred_element_type=jnp.float32).astype(
-        jnp.bfloat16
-    )
-
-
-def pick(order, place, table):
-    total = place.size
-    halves = total // N_GRP // PICK_STEP
+def pick_kernel(place_ref, table_ref, out_ref, wide, slabs, hits):
+    @pl.when(pl.program_id(0) == 0)
+    def _():
+        wide[...] = table_ref[...].astype(jnp.float32)
+        for slab in range(4):
+            for ky in range(2):
+                slabs[slab, ky * NF : (ky + 1) * NF, :] = wide[
+                    pl.ds(2 * slab + ky, NF, stride=8), :
+                ].astype(jnp.bfloat16)
+
+    for slab in range(4):
+        for row in range(4):
+            tiles = hit_tiles(place_ref[slab * 4 + row : slab * 4 + row + 1, :], SLAB_ROWS)
+            for at, tile in enumerate(tiles):
+                hits[row * LANES : (row + 1) * LANES, at * LANES : (at + 1) * LANES] = tile
+        taken = jnp.dot(hits[...], slabs[slab], preferred_element_type=jnp.float32)
+        out_ref[:, slab, :, :] = taken.astype(jnp.bfloat16).reshape(32, CAP, LANES)
+
+
+def pick(place, table):
     return pl.pallas_call(
         pick_kernel,
-        grid_spec=pltpu.PrefetchScalarGridSpec(
-            num_scalar_prefetch=1,
-            grid=(N_GRP, halves),
-            in_specs=[
-                pl.BlockSpec(
-                    (PICK_STEP // LANES, LANES), lambda g, i, order: (order[g] * halves + i, 0)
-                ),
-                pl.BlockSpec((SLAB_ROWS, LANES), lambda g, i, order: (0, 0)),
-            ],
-            out_specs=pl.BlockSpec((PICK_STEP, LANES), lambda g, i, order: (g * halves + i, 0)),
-        ),
-        out_shape=jax.ShapeDtypeStruct((total, LANES), jnp.bfloat16),
+        grid=(N_GRP,),
+        in_specs=[
+            pl.BlockSpec((CAP, LANES), lambda g: (g, 0)),
+            pl.BlockSpec((4 * SLAB_ROWS, LANES), lambda g: (0, 0)),
+        ],
+        out_specs=pl.BlockSpec((32, None, 4, CAP, LANES), lambda g: (0, g, 0, 0, 0)),
+        out_shape=jax.ShapeDtypeStruct((32, N_GRP, 4, CAP, LANES), jnp.bfloat16),
+        scratch_shapes=[
+            pltpu.VMEM((4 * SLAB_ROWS, LANES), jnp.float32),
+            pltpu.VMEM((4, SLAB_ROWS, LANES), jnp.bfloat16),
+            pltpu.VMEM((SLAB_ROWS, SLAB_ROWS), jnp.bfloat16),
+        ],
         compiler_params=pltpu.CompilerParams(vmem_limit_bytes=VMEM_BYTES),
         cost_estimate=pl.CostEstimate(
-            flops=2 * total * SLAB_ROWS * LANES, bytes_accessed=4 << 20, transcendentals=0
+            flops=16 * SLOTS * SLAB_ROWS * LANES, bytes_accessed=4 << 20, transcendentals=0
         ),
-    )(order, place, table)
+    )(place, table)
 
 
 def score_kernel(order_ref, buffer_ref, weighted_ref, col_ref, row_ref, out_ref, mix, slices):
     del order_ref
-    lane = lax.broadcasted_iota(jnp.int32, (LANES, LANES), 1).astype(jnp.float32)
     extra = weighted_ref[PARTICLE_ROWS:, :].astype(jnp.float32)
     place = 16.0 * extra[:8] + extra[8:16]
     frac = extra[16:20] + extra[20:24] + extra[24:28]
     for row in range(8):
-        column = down_rows(place[row : row + 1])
-        for first in range(0, SLOTS, LANES):
-            mix[row * LANES : (row + 1) * LANES, first : first + LANES] = jnp.where(
-                column == lane + float(first), 1.0, 0.0
-            ).astype(jnp.bfloat16)
+        for at, tile in enumerate(hit_tiles(place[row : row + 1], SLOTS)):
+            mix[row * LANES : (row + 1) * LANES, at * LANES : (at + 1) * LANES] = tile
     taken = jnp.dot(
         mix[...], buffer_ref[...].reshape(SLOTS, LANES), preferred_element_type=jnp.float32
     )
@@ -226,7 +228,15 @@
             columns = columns[:, :LANES] + columns[:, LANES:]
             summed = jnp.sum(columns.reshape(PART_DEV, COLS, LANES) * phase_rows[None], axis=1)
             done.append(summed + pltpu.roll(summed, TRANS, 1))
-        out_ref[pair] = jnp.where(left, done[0], done[1])
+        total = jnp.where(left, done[0], done[1])
+
+        @pl.when(pl.program_id(0) == 0)
+        def _():
+            out_ref[pair] = total
+
+        @pl.when(pl.program_id(0) > 0)
+        def _():
+            out_ref[pair] += total
 
 
 def score(order, buffer, weighted, col_phase, row_phase):
@@ -237,23 +247,23 @@
             grid=(N_GRP,),
             in_specs=[
                 pl.BlockSpec(
-                    (SLOTS // CAP, None, CAP, LANES), lambda i, order: (0, order[i], 0, 0)
+                    (32, None, 4 * CAP, LANES), lambda i, order: (0, order[i], 0, 0)
                 ),
                 pl.BlockSpec(
                     (None, PARTICLE_ROWS + EXTRA_ROWS, LANES), lambda i, order: (i, 0, 0)
                 ),
                 pl.BlockSpec((2 * LANES, 2 * LANES), lambda i, order: (0, 0)),
-                pl.BlockSpec((COLS, LANES), lambda i, order: (0, 0)),
+                pl.BlockSpec((None, COLS, LANES), lambda i, order: (order[i], 0, 0)),
             ],
             out_specs=pl.BlockSpec(
-                (None, ORI_MAX // 2, PART_DEV, LANES), lambda i, order: (order[i], 0, 0, 0)
+                (ORI_MAX // 2, PART_DEV, LANES), lambda i, order: (0, 0, 0)
             ),
             scratch_shapes=[
                 pltpu.VMEM((2 * TAKES, SLOTS), jnp.bfloat16),
                 pltpu.VMEM((TAKES, LANES), jnp.float32),
             ],
         ),
-        out_shape=jax.ShapeDtypeStruct((N_GRP, ORI_MAX // 2, PART_DEV, LANES), jnp.float32),
+        out_shape=jax.ShapeDtypeStruct((ORI_MAX // 2, PART_DEV, LANES), jnp.float32),
         compiler_params=pltpu.CompilerParams(vmem_limit_bytes=VMEM_BYTES),
         cost_estimate=pl.CostEstimate(flops=8 << 30, bytes_accessed=4 << 20, transcendentals=0),
     )(order, buffer, weighted, col_phase, row_phase)
@@ -268,50 +278,39 @@
 
 
 def shards(pencils, send_map, interp_index, interp_frac, ori_count, spectra, class_ids, ctf_table):
-    here = lax.axis_index("h")
+    here = lax.axis_index("x")
     turn = jnp.arange(4, dtype=jnp.int32)
-    planes = exchange(fourier(pencils, jnp.asarray(fourier_tables())), "x")
-    planes = planes.reshape(4, 4, 32, LANES).transpose(1, 0, 2, 3).reshape(2 * NF, LANES)
-
-    wanted, planes = lax.optimization_barrier((send_map[0, 0], planes))
-    table = exchange(planes, SLAB_AXES)
-    wanted = jnp.maximum(wanted, 0)
-    place = ((wanted & (NF - 2)) << 1) | ((wanted >> 8) << 1) | (wanted & 1)
-    place = place.reshape(4, 4, 8, CAP).transpose(0, 2, 1, 3).reshape(CAP, LANES)
-    place = place.astype(jnp.float32)
-    maps = [
-        lax.ppermute(
-            place,
-            ("h", "x"),
-            [(slab * 4 + g, (g + j) % 4 * 4 + slab) for g in range(4) for slab in range(4)],
-        )
-        for j in range(4)
-    ]
-    outgoing = pick((here - turn) % 4, jnp.concatenate(maps, axis=0), table)
+    table = exchange(fourier(pencils, jnp.asarray(fourier_tables())), SLAB_AXES)
+
+    wanted = jnp.maximum(send_map[0, 0], 0)
+    place = ((wanted & 1) << 8) | (wanted & (NF - 2)) | (wanted >> 8)
+    place = place.astype(jnp.float32).reshape(4, 4, 8, CAP).transpose(1, 0, 2, 3)
+    maps = lax.all_gather(place.reshape(4, 4, LANES), "h", axis=0)
+    maps = lax.dynamic_index_in_dim(maps, lax.axis_index("h"), 1, keepdims=False)
+    maps = lax.all_gather(maps.reshape(CAP, LANES), "x", axis=0, tiled=True)
+    outgoing = pick(maps, table)
 
     slot = interp_index.reshape(2, TAKES)
-    source = slot >> 4
-    source = (((source >> 3) & 3) << 5) | ((source >> 5) << 3) | (source & 7)
-    slot = ((source << 4) | (slot & 15)).astype(jnp.float32)
+    slab = slot >> 4
+    source = ((slab >> 5) << 3) | (slab & 7)
+    slot = ((source << 6) | (((slab >> 3) & 3) << 4) | (slot & 15)).astype(jnp.float32)
     taps = jnp.concatenate([slot.reshape(8, LANES), interp_frac.reshape(4, LANES)], axis=0)
-    weighted, outgoing = lax.optimization_barrier(
-        (weigh(class_ids, spectra, ctf_table, taps), outgoing)
-    )
-    buffer = exchange(outgoing, ROW_AXES).reshape(SLOTS // CAP, 4, CAP, LANES)
-    owners = [lax.dynamic_index_in_dim(weighted, here, 0, keepdims=False)]
+    weighted = weigh(class_ids, spectra, ctf_table, taps)
+    outgoing = outgoing.reshape(32 * N_GRP * 4 * CAP, LANES)
+    buffer = exchange(outgoing, ROW_AXES).reshape(32, N_GRP, 4 * CAP, LANES)
+    groups = [lax.dynamic_index_in_dim(weighted, here, 0, keepdims=False)]
     for k in range(1, 4):
         block = lax.dynamic_index_in_dim(weighted, (here - k) % 4, 0, keepdims=False)
-        owners.append(lax.ppermute(block, "h", [((i + k) % 4, i) for i in range(4)]))
+        groups.append(lax.ppermute(block, "x", [((i + k) % 4, i) for i in range(4)]))
     partial = score(
         (here + turn) % 4,
         buffer,
-        jnp.stack(owners),
-        own_part(column_table(), "h"),
-        own_part(row_table(), "x"),
+        jnp.stack(groups),
+        own_part(column_table(), "x"),
+        jnp.asarray(row_table()),
     )
-    parts = exchange(partial.reshape(16, PART_DEV, LANES), ("h", "x"))
-    total = jnp.sum(parts, axis=0)
-    orient = 2 * lax.axis_index("x") + jnp.arange(LANES, dtype=jnp.int32) // TRANS
+    total = jnp.sum(exchange(partial, "x"), axis=0)
+    orient = 2 * here + jnp.arange(LANES, dtype=jnp.int32) // TRANS
     return jnp.where(orient[None, :] < ori_count[0], total, 0.0)
 
 

time: 195 us -> 165 us (0.85); the launches traced: 192 us -> 165 us
  starting transfers between devices: 92.6 us -> 45.4 us
  blocking collectives: 0 us -> 45.5 us
  waiting for transfers between devices: 68.6 us -> 41.1 us
  Pallas kernels: 21.2 us -> 25.6 us
  local copies, waits for them, and re-layouts: 7.47 us -> 4.67 us
    all_gather x0 -> x2, blocking collectives: none -> 45.5 us  [the longest x1 36.1 us: shards(): maps = lax.all_gather(place.reshape(4, 4, LANES), 'h', axis=0)]
    ppermute x7 -> x3, starting transfers between devices: 48.5 us -> 9.05 us  [shards(): lax.ppermute(block, 'x', [((i + k) % 4, i) for i in range(4)])]
    ppermute x7 -> x3, waiting for transfers between devices: 38.4 us -> 2.87 us  [shards(): lax.ppermute(block, 'x', [((i + k) % 4, i) for i in range(4)])]
    all_to_all x4 -> x3, waiting for transfers between devices: 30.1 us -> 38.3 us  [exchange(): return lax.all_to_all(values, axes, split_axis=0, concat_axis=0, tiled=True)]
    all_to_all x4 -> x3, starting transfers between devices: 44.1 us -> 36.3 us  [exchange(): return lax.all_to_all(values, axes, split_axis=0, concat_axis=0, tiled=True)]
    pallas_call x1, Pallas kernels: 14.7 us -> 17.8 us  [score(): pl.pallas_call(score_kernel, grid_spec=pltpu.PrefetchScalarGridSpec(num_s...]
    unnamed x13 -> x20, local copies, waits for them, and re-layouts: 4.13 us -> 3.36 us
  transfers between devices with their start and end apart: 11 -> 6, of which waited for: 5 -> 4; matrix products, arithmetic and copies ran while one was open for 2% -> 1% of each run, Pallas kernels for 0% -> 0%
where the time goes in v3:
time: 165 us
  blocking collectives  45.5 us (28%)
  starting transfers between devices  45.4 us (28%)
  waiting for transfers between devices  41.1 us (25%)
  Pallas kernels  25.6 us (16%)
  local copies, waits for them, and re-layouts  4.67 us (3%)
  other arithmetic  1.7 us (1%)
    all_to_all x3, waiting for transfers between devices, exchange(): return lax.all_to_all(values, axes, split_axis=0, concat_axis=0, tiled=True)  38.3 us
    all_to_all x3, starting transfers between devices, exchange(): return lax.all_to_all(values, axes, split_axis=0, concat_axis=0, tiled=True)  36.3 us
    all_gather x1, blocking collectives, shards(): maps = lax.all_gather(place.reshape(4, 4, LANES), 'h', axis=0)  36.1 us
    pallas_call x1, Pallas kernels, score(): pl.pallas_call(score_kernel, grid_spec=pltpu.PrefetchScalarGridSpec(num_s...  17.8 us
    all_gather x1, blocking collectives, shards(): maps = lax.all_gather(maps.reshape(CAP, LANES), 'x', axis=0, tiled=True)  9.36 us
    ppermute x3, starting transfers between devices, shards(): lax.ppermute(block, 'x', [((i + k) % 4, i) for i in range(4)])  9.05 us
    pallas_call x1, Pallas kernels, pick(): pl.pallas_call(pick_kernel, grid=(N_GRP,), in_specs=[pl.BlockSpec((CAP, L...  5.61 us
    unnamed x20, local copies, waits for them, and re-layouts  3.36 us
  transfers between devices with their start and end apart: 6, of which 4 were waited for; matrix products, arithmetic and copies ran while one was open for 1% of the time, Pallas kernels for 0%

profile of v3, /device:TPU:1, one launch (start us, length us, event | category | flops | bytes accessed | tf_op | source)
XLA Modules:
  0.0 164.8 jit_solution(13013245151857118999)
XLA Ops:
  0.0 0.0 copy-start.3
  0.0 1.0 copy-done.3
  1.0 0.0 copy-start.4
  1.0 0.9 copy-done.4
  2.0 0.0 copy-start.7
  2.0 1.4 shard_map.109
  3.4 20.6 %all-to-all-start = ((bf16[128,16,128]{2,1,0:T(8,128)(2,1)}), bf16[128,16,128]{2,1,0:T(8,128)(2,1)S(1)}, u32[]{:S(2)}, u32[]{:S(2)}) async-start(bf16[128,16,128]{2,1,0:T(8,128)(2,1)} %bitcast.4), calls=%async_computation | async-start | bytes 1048576 | tf_op jit(solution)/shard_map/all_to_all | solution.py:273
  24.0 0.0 copy-done.7
  24.0 0.1 copy.15
  24.1 0.1 all_gather_reshape.3
  24.2 36.1 %all_gather.6 = f32[4,4,4,128]{3,2,0,1:T(4,128)S(1)} all-gather(f32[1,4,4,128]{3,2,0,1:T(4,128)S(1)} %copy.16), channel_id=1, replica_groups=mesh['y'=4,'h'=4,'l'=4,'c'=2,'x'=4] {'h'}, dimensions={0}, use_global_device_ids=true | all-gather | bytes 40960 | tf_op jit(solution)/shard_map/all_gather | solution.py:288
  60.3 9.4 %all_gather.7.place_ref = f32[64,128]{1,0:T(8,128)S(1)} all-gather(f32[16,128]{1,0:T(8,128)S(1)} %bitcast.32), channel_id=1, replica_groups=mesh['y'=4,'h'=4,'l'=4,'c'=2,'x'=4] {'x'}, dimensions={0}, use_global_device_ids=true | all-gather | bytes 40960 | tf_op jit(solution)/shard_map/all_gather | solution.py:290
  69.7 0.0 all-to-all-done
  69.7 5.6 %shard_map.110 = bf16[32,4,4,16,128]{4,3,2,1,0:T(8,128)(2,1)S(1)} custom-call(f32[64,128]{1,0:T(8,128)S(1)} %all_gather.7.place_ref, bf16[2048,128]{1,0:T(8,128)(2,1)S(1)} %bitcast.29), custom_call_target="tpu_custom_call" | custom-call | flops 2147483648 | bytes 4194304 | tf_op jit(solution)/shard_map/pallas_call | solution.py:176
  75.3 0.0 copy-start
  75.3 1.3 copy-done
  76.6 0.0 copy-start.9
  76.6 0.0 copy-start.8
  76.6 0.0 copy-start.1
  76.6 0.0 copy-start.2
  76.6 0.0 copy-start.5
  76.7 12.4 %all-to-all-start.1 = ((bf16[32,256,128]{2,1,0:T(8,128)(2,1)}), bf16[32,256,128]{2,1,0:T(8,128)(2,1)S(1)}, u32[]{:S(2)}, u32[]{:S(2)}) async-start(bf16[32,256,128]{2,1,0:T(8,128)(2,1)} %bitcast.28), calls=%async_computation.1 | async-start | bytes 4194304 | tf_op jit(solution)/shard_map/all_to_all | solution.py:273
  89.1 0.0 copy-start.6
  89.1 0.0 copy-done.9
  89.1 0.1 reshape.68
  89.2 0.0 copy-done.8
  89.2 0.1 reshape.75
  89.3 0.0 copy-done.1
  89.3 0.0 copy-done.2
  89.3 0.0 copy-done.5
  89.3 0.8 shard_map.111
  90.1 0.1 constant_dynamic-slice_fusion
  90.2 2.8 %collective-permute-start.2 = (bf16[544,128]{1,0:T(8,128)(2,1)S(1)}, bf16[544,128]{1,0:T(8,128)(2,1)S(1)}, u32[]{:S(2)}, u32[]{:S(2)}) collective-permute-start(bf16[544,128]{1,0:T(8,128)(2,1)S(1)} %get-tuple-element.6), channel_id=1, source_target_pairs={{3,0},{0,1},{1,2},{2,3},{7,4},{4,5},{5,6},{6,7},{11,8},{8,9},{9,10... | collective-permute-start | bytes 417800 | tf_op jit(solution)/shard_map/ppermute | solution.py:304
  93.0 4.3 %collective-permute-start.1 = (bf16[544,128]{1,0:T(8,128)(2,1)S(1)}, bf16[544,128]{1,0:T(8,128)(2,1)}, u32[]{:S(2)}, u32[]{:S(2)}) collective-permute-start(bf16[544,128]{1,0:T(8,128)(2,1)S(1)} %get-tuple-element.7), channel_id=1, source_target_pairs={{2,0},{3,1},{0,2},{1,3},{6,4},{7,5},{4,6},{5,7},{10,8},{11,9},{8,1... | collective-permute-start | bytes 417800 | tf_op jit(solution)/shard_map/ppermute | solution.py:304
  97.3 1.9 %collective-permute-start = (bf16[544,128]{1,0:T(8,128)(2,1)S(1)}, bf16[544,128]{1,0:T(8,128)(2,1)}, u32[]{:S(2)}, u32[]{:S(2)}) collective-permute-start(bf16[544,128]{1,0:T(8,128)(2,1)S(1)} %get-tuple-element.8), channel_id=1, source_target_pairs={{1,0},{2,1},{3,2},{0,3},{5,4},{6,5},{7,6},{4,7},{9,8},{10,9},{11,1... | collective-permute-start | bytes 417800 | tf_op jit(solution)/shard_map/ppermute | solution.py:304
  99.9 0.9 dynamic-slice_bitcast_fusion.3.col_ref
  100.8 0.0 collective-permute-done.2
  100.8 1.4 collective-permute-done.1
  102.2 1.5 collective-permute-done
  103.7 1.0 pad_maximum_fusion.weighted_ref
  104.7 34.1 %all-to-all-done.1 = bf16[32,256,128]{2,1,0:T(8,128)(2,1)S(1)} async-done(((bf16[32,256,128]{2,1,0:T(8,128)(2,1)}), bf16[32,256,128]{2,1,0:T(8,128)(2,1)S(1)}, u32[]{:S(2)}, u32[]{:S(2)}) %all-to-all-start.1) | async-done | bytes 2097184 | tf_op jit(solution)/shard_map/all_to_all | solution.py:273
  138.8 0.0 copy-done.6
  138.8 17.8 %shard_map.112 = f32[4,8,128]{2,1,0:T(8,128)} custom-call(s32[4]{0:T(128)S(1)} %and_select_fusion.order_ref, bf16[32,4,64,128]{3,2,1,0:T(8,128)(2,1)S(1)} %bitcast.27, bf16[4,544,128]{2,1,0:T(8,128)(2,1)S(1)} %pad_maximum_fusion.weighted_ref, bf16[256,256]{1,0:T(8,128)(2,1)S(1)} %dynamic-slice_bitcast_fusion.3.col_ref, f32[4,64,128]{2,1,0:T(8,128)S(1)} %copy-done.6), custom_call_target="tpu_custom_call" | custom-call | flops 8589934592 | bytes 4194304 | tf_op jit(solution)/shard_map/pallas_call | solution.py:243
  156.6 3.4 %all-to-all-start.2 = ((f32[4,8,128]{2,1,0:T(8,128)}), f32[4,8,128]{2,1,0:T(8,128)S(1)}, u32[]{:S(2)}, u32[]{:S(2)}) async-start(f32[4,8,128]{2,1,0:T(8,128)} %shard_map.112), calls=%async_computation.2 | async-start | bytes 32768 | tf_op jit(solution)/shard_map/all_to_all | solution.py:273
  160.0 4.2 %all-to-all-done.2 = f32[4,8,128]{2,1,0:T(8,128)S(1)} async-done(((f32[4,8,128]{2,1,0:T(8,128)}), f32[4,8,128]{2,1,0:T(8,128)S(1)}, u32[]{:S(2)}, u32[]{:S(2)}) %all-to-all-start.2) | async-done | bytes 16416 | tf_op jit(solution)/shard_map/all_to_all | solution.py:273
  164.2 0.6 broadcast_select_fusion
  (8 shorter events, 0.1 us)
Async XLA Ops:
  0.0 1.0 copy-start.3
  1.0 0.9 copy-start.4
  2.0 22.0 %copy-start.7 = (s32[1,1,128,16]{2,3,1,0:T(8,128)S(1)}, s32[1,1,128,16]{2,3,1,0:T(8,128)}, u32[]{:S(2)}) copy-start(s32[1,1,128,16]{2,3,1,0:T(8,128)} %param.12) | copy-start | bytes 24580
  3.4 66.3 %all-to-all-start = ((bf16[128,16,128]{2,1,0:T(8,128)(2,1)}), bf16[128,16,128]{2,1,0:T(8,128)(2,1)S(1)}, u32[]{:S(2)}, u32[]{:S(2)}) async-start(bf16[128,16,128]{2,1,0:T(8,128)(2,1)} %bitcast.4), calls=%async_computation | async-start | bytes 1048576 | tf_op jit(solution)/shard_map/all_to_all | solution.py:273
  75.3 1.3 copy-start
  76.6 12.5 %copy-start.9 = (f32[1,8,64]{2,1,0:T(8,128)S(1)}, f32[1,8,64]{2,1,0:T(8,128)}, u32[]{:S(2)}) copy-start(f32[1,8,64]{2,1,0:T(8,128)} %param.14) | copy-start | bytes 6148
  76.6 12.6 %copy-start.8 = (s32[2,1,8,64]{3,2,1,0:T(8,128)S(1)}, s32[2,1,8,64]{3,2,1,0:T(8,128)}, u32[]{:S(2)}) copy-start(s32[2,1,8,64]{3,2,1,0:T(8,128)} %param.13) | copy-start | bytes 12292
  76.6 12.7 %copy-start.1 = (bf16[8,64,512]{2,1,0:T(8,128)(2,1)S(1)}, bf16[8,64,512]{2,1,0:T(8,128)(2,1)}, u32[]{:S(2)}) copy-start(bf16[8,64,512]{2,1,0:T(8,128)(2,1)} %spectra_ref.1) | copy-start | bytes 1572868
  76.6 12.7 %copy-start.2 = (bf16[16,64,256]{2,1,0:T(8,128)(2,1)S(1)}, bf16[16,64,256]{2,1,0:T(8,128)(2,1)}, u32[]{:S(2)}) copy-start(bf16[16,64,256]{2,1,0:T(8,128)(2,1)} %ctf_ref.1) | copy-start | bytes 1572868
  76.6 12.7 %copy-start.5 = (s32[8]{0:T(128)S(1)}, s32[8]{0:T(128)}, u32[]{:S(2)}) copy-start(s32[8]{0:T(128)} %class_ref.1) | copy-start | bytes 100
  76.7 62.2 %all-to-all-start.1 = ((bf16[32,256,128]{2,1,0:T(8,128)(2,1)}), bf16[32,256,128]{2,1,0:T(8,128)(2,1)S(1)}, u32[]{:S(2)}, u32[]{:S(2)}) async-start(bf16[32,256,128]{2,1,0:T(8,128)(2,1)} %bitcast.28), calls=%async_computation.1 | async-start | bytes 4194304 | tf_op jit(solution)/shard_map/all_to_all | solution.py:273
  89.1 49.7 %copy-start.6 = (f32[4,64,128]{2,1,0:T(8,128)S(1)}, f32[4,64,128]{2,1,0:T(8,128)}, u32[]{:S(2)}) copy-start(f32[4,64,128]{2,1,0:T(8,128)} %constant.106.clone.row_ref) | copy-start | bytes 393220
  90.2 10.7 %collective-permute-start.2 = (bf16[544,128]{1,0:T(8,128)(2,1)S(1)}, bf16[544,128]{1,0:T(8,128)(2,1)S(1)}, u32[]{:S(2)}, u32[]{:S(2)}) collective-permute-start(bf16[544,128]{1,0:T(8,128)(2,1)S(1)} %get-tuple-element.6), channel_id=1, source_target_pairs={{3,0},{0,1},{1,2},{2,3},{7,4},{4,5},{5,6},{6,7},{11,8},{8,9},{9,10... | collective-permute-start | bytes 417800 | tf_op jit(solution)/shard_map/ppermute | solution.py:304
  93.0 9.2 %collective-permute-start.1 = (bf16[544,128]{1,0:T(8,128)(2,1)S(1)}, bf16[544,128]{1,0:T(8,128)(2,1)}, u32[]{:S(2)}, u32[]{:S(2)}) collective-permute-start(bf16[544,128]{1,0:T(8,128)(2,1)S(1)} %get-tuple-element.7), channel_id=1, source_target_pairs={{2,0},{3,1},{0,2},{1,3},{6,4},{7,5},{4,6},{5,7},{10,8},{11,9},{8,1... | collective-permute-start | bytes 417800 | tf_op jit(solution)/shard_map/ppermute | solution.py:304
  97.3 6.4 %collective-permute-start = (bf16[544,128]{1,0:T(8,128)(2,1)S(1)}, bf16[544,128]{1,0:T(8,128)(2,1)}, u32[]{:S(2)}, u32[]{:S(2)}) collective-permute-start(bf16[544,128]{1,0:T(8,128)(2,1)S(1)} %get-tuple-element.8), channel_id=1, source_target_pairs={{1,0},{2,1},{3,2},{0,3},{5,4},{6,5},{7,6},{4,7},{9,8},{10,9},{11,1... | collective-permute-start | bytes 417800 | tf_op jit(solution)/shard_map/ppermute | solution.py:304
  156.6 7.6 %all-to-all-start.2 = ((f32[4,8,128]{2,1,0:T(8,128)}), f32[4,8,128]{2,1,0:T(8,128)S(1)}, u32[]{:S(2)}, u32[]{:S(2)}) async-start(f32[4,8,128]{2,1,0:T(8,128)} %shard_map.112), calls=%async_computation.2 | async-start | bytes 32768 | tf_op jit(solution)/shard_map/all_to_all | solution.py:273

commit v4 on v3

--- a/solution.py
+++ b/solution.py
@@ -23,6 +23,7 @@
 SLOTS = 2048
 TAKES = ORI_MAX * COLS
 PARTICLE_ROWS = PART_DEV * COLS
+MIX_STEP = 256
 EXTRA_ROWS = 32
 VMEM_BYTES = 48 * 1024 * 1024
 SLAB_AXES = ("y", "h", "l", "c")
@@ -67,17 +68,14 @@
     return jnp.broadcast_to(row, (LANES, LANES)).T
 
 
-def hit_tiles(row, total):
-    high = jnp.floor(row * (1.0 / LANES))
-    low = down_rows(row - float(LANES) * high).astype(jnp.bfloat16)
-    high = down_rows(high).astype(jnp.bfloat16)
+def hit_tiles(rows, total, weights=(1.0,)):
     lane = lax.broadcasted_iota(jnp.int32, (LANES, LANES), 1).astype(jnp.float32)
-    inner = jnp.where(low == lane.astype(jnp.bfloat16), 1.0, 0.0).astype(jnp.bfloat16)
-    zero = jnp.zeros_like(inner)
-    return [
-        jnp.where(high == jnp.full_like(high, float(tile)), inner, zero)
-        for tile in range(total // LANES)
-    ]
+    ahead = [down_rows(row) - lane for row in rows]
+    tiles = []
+    for first in range(0, total, LANES):
+        parts = [jnp.where(far == float(first), w, 0.0) for far, w in zip(ahead, weights)]
+        tiles.append(sum(parts[1:], parts[0]).astype(jnp.bfloat16))
+    return tiles
 
 
 def fourier_kernel(x_ref, table_ref, out_ref, wide):
@@ -153,7 +151,9 @@
     )(class_ids, spectra, ctf_table, taps)
 
 
-def pick_kernel(place_ref, table_ref, out_ref, wide, slabs, hits):
+def pick_kernel(order_ref, place_ref, table_ref, out_ref, wide, slabs, hits):
+    del order_ref
+
     @pl.when(pl.program_id(0) == 0)
     def _():
         wide[...] = table_ref[...].astype(jnp.float32)
@@ -165,69 +165,103 @@
 
     for slab in range(4):
         for row in range(4):
-            tiles = hit_tiles(place_ref[slab * 4 + row : slab * 4 + row + 1, :], SLAB_ROWS)
+            tiles = hit_tiles([place_ref[slab, row : row + 1, :]], SLAB_ROWS)
             for at, tile in enumerate(tiles):
                 hits[row * LANES : (row + 1) * LANES, at * LANES : (at + 1) * LANES] = tile
         taken = jnp.dot(hits[...], slabs[slab], preferred_element_type=jnp.float32)
         out_ref[:, slab, :, :] = taken.astype(jnp.bfloat16).reshape(32, CAP, LANES)
 
 
-def pick(place, table):
+def pick(order, place, table):
     return pl.pallas_call(
         pick_kernel,
-        grid=(N_GRP,),
-        in_specs=[
-            pl.BlockSpec((CAP, LANES), lambda g: (g, 0)),
-            pl.BlockSpec((4 * SLAB_ROWS, LANES), lambda g: (0, 0)),
-        ],
-        out_specs=pl.BlockSpec((32, None, 4, CAP, LANES), lambda g: (0, g, 0, 0, 0)),
-        out_shape=jax.ShapeDtypeStruct((32, N_GRP, 4, CAP, LANES), jnp.bfloat16),
-        scratch_shapes=[
-            pltpu.VMEM((4 * SLAB_ROWS, LANES), jnp.float32),
-            pltpu.VMEM((4, SLAB_ROWS, LANES), jnp.bfloat16),
-            pltpu.VMEM((SLAB_ROWS, SLAB_ROWS), jnp.bfloat16),
-        ],
+        grid_spec=pltpu.PrefetchScalarGridSpec(
+            num_scalar_prefetch=1,
+            grid=(N_GRP,),
+            in_specs=[
+                pl.BlockSpec((4, None, 4, LANES), lambda i, order: (0, i, 0, 0)),
+                pl.BlockSpec((4 * SLAB_ROWS, LANES), lambda i, order: (0, 0)),
+            ],
+            out_specs=pl.BlockSpec(
+                (32, None, 4, CAP, LANES), lambda i, order: (0, order[i], 0, 0, 0)
+            ),
+            scratch_shapes=[
+                pltpu.VMEM((4 * SLAB_ROWS, LANES), jnp.float32),
+                pltpu.VMEM((4, SLAB_ROWS, LANES), jnp.bfloat16),
+                pltpu.VMEM((SLAB_ROWS, SLAB_ROWS), jnp.bfloat16),
+            ],
+        ),
+        out_shape=pltpu.HBM((32, N_GRP, 4, CAP, LANES), jnp.bfloat16),
         compiler_params=pltpu.CompilerParams(vmem_limit_bytes=VMEM_BYTES),
         cost_estimate=pl.CostEstimate(
             flops=16 * SLOTS * SLAB_ROWS * LANES, bytes_accessed=4 << 20, transcendentals=0
         ),
-    )(place, table)
-
-
-def score_kernel(order_ref, buffer_ref, weighted_ref, col_ref, row_ref, out_ref, mix, slices):
+    )(order, place, table)
+
+
+def score_kernel(order_ref, buffer_ref, weighted_ref, col_ref, row_ref, out_ref, slices):
     del order_ref
     extra = weighted_ref[PARTICLE_ROWS:, :].astype(jnp.float32)
     place = 16.0 * extra[:8] + extra[8:16]
     frac = extra[16:20] + extra[20:24] + extra[24:28]
-    for row in range(8):
-        for at, tile in enumerate(hit_tiles(place[row : row + 1], SLOTS)):
-            mix[row * LANES : (row + 1) * LANES, at * LANES : (at + 1) * LANES] = tile
-    taken = jnp.dot(
-        mix[...], buffer_ref[...].reshape(SLOTS, LANES), preferred_element_type=jnp.float32
-    )
+    lane = lax.broadcasted_iota(jnp.int32, (LANES, LANES), 1).astype(jnp.float32)
+    takes = []
     for row in range(4):
         share = down_rows(frac[row : row + 1])
-        span = slice(row * LANES, (row + 1) * LANES)
-        slices[span, :] = (1.0 - share) * taken[span] + share * taken[TAKES:][span]
+        takes.append(
+            (
+                down_rows(place[row : row + 1]) - lane,
+                1.0 - share,
+                down_rows(place[row + 4 : row + 5]) - lane,
+                share,
+            )
+        )
+    rows = buffer_ref[...].reshape(SLOTS, LANES)
+    mixed = None
+    for start in range(0, SLOTS, MIX_STEP):
+        blocks = [
+            jnp.concatenate(
+                [
+                    (
+                        jnp.where(far == float(first), rest, 0.0)
+                        + jnp.where(far_next == float(first), share, 0.0)
+                    ).astype(jnp.bfloat16)
+                    for first in range(start, start + MIX_STEP, LANES)
+                ],
+                axis=1,
+            )
+            for far, rest, far_next, share in takes
+        ]
+        part = jnp.dot(
+            jnp.concatenate(blocks, axis=0),
+            rows[start : start + MIX_STEP],
+            preferred_element_type=jnp.float32,
+        )
+        mixed = part if mixed is None else mixed + part
+    slices[...] = mixed
     phase_rows = row_ref[...]
     left = lax.broadcasted_iota(jnp.int32, (PART_DEV, LANES), 1) < TRANS
     weight = weighted_ref[:PARTICLE_ROWS, :].astype(jnp.float32).reshape(PART_DEV, COLS, LANES)
     for pair in range(ORI_MAX // 2):
-        done = []
+        products = []
         for orient in (2 * pair, 2 * pair + 1):
             plain = slices[orient * COLS : (orient + 1) * COLS, :]
             swapped = pltpu.roll(plain, COLS, 1)
-            products = jnp.concatenate(
-                [
-                    (weight * plain[None]).astype(jnp.bfloat16),
-                    (weight * swapped[None]).astype(jnp.bfloat16),
-                ],
-                axis=-1,
-            ).reshape(PARTICLE_ROWS, 2 * LANES)
-            columns = jnp.dot(products, col_ref[...], preferred_element_type=jnp.float32)
-            columns = columns[:, :LANES] + columns[:, LANES:]
-            summed = jnp.sum(columns.reshape(PART_DEV, COLS, LANES) * phase_rows[None], axis=1)
-            done.append(summed + pltpu.roll(summed, TRANS, 1))
+            products.append(
+                jnp.concatenate(
+                    [
+                        (weight * plain[None]).astype(jnp.bfloat16),
+                        (weight * swapped[None]).astype(jnp.bfloat16),
+                    ],
+                    axis=-1,
+                ).reshape(PARTICLE_ROWS, 2 * LANES)
+            )
+        columns = jnp.dot(
+            jnp.concatenate(products, axis=0), col_ref[...], preferred_element_type=jnp.float32
+        )
+        columns = (columns[:, :LANES] + columns[:, LANES:]).reshape(2, PART_DEV, COLS, LANES)
+        summed = jnp.sum(columns * phase_rows[None, None], axis=2)
+        done = [summed[at] + pltpu.roll(summed[at], TRANS, 1) for at in range(2)]
         total = jnp.where(left, done[0], done[1])
 
         @pl.when(pl.program_id(0) == 0)
@@ -259,7 +293,6 @@
                 (ORI_MAX // 2, PART_DEV, LANES), lambda i, order: (0, 0, 0)
             ),
             scratch_shapes=[
-                pltpu.VMEM((2 * TAKES, SLOTS), jnp.bfloat16),
                 pltpu.VMEM((TAKES, LANES), jnp.float32),
             ],
         ),
@@ -285,10 +318,13 @@
     wanted = jnp.maximum(send_map[0, 0], 0)
     place = ((wanted & 1) << 8) | (wanted & (NF - 2)) | (wanted >> 8)
     place = place.astype(jnp.float32).reshape(4, 4, 8, CAP).transpose(1, 0, 2, 3)
-    maps = lax.all_gather(place.reshape(4, 4, LANES), "h", axis=0)
-    maps = lax.dynamic_index_in_dim(maps, lax.axis_index("h"), 1, keepdims=False)
-    maps = lax.all_gather(maps.reshape(CAP, LANES), "x", axis=0, tiled=True)
-    outgoing = pick(maps, table)
+    place = place.reshape(4, 4, LANES)
+    maps = [place] + [
+        lax.ppermute(place, "x", [((i + k) % 4, i) for i in range(4)]) for k in range(1, 4)
+    ]
+    maps = lax.all_gather(jnp.stack(maps), "h", axis=0)
+    maps = lax.dynamic_index_in_dim(maps, lax.axis_index("h"), 2, keepdims=False)
+    outgoing = pick((here + turn) % 4, maps, table)
 
     slot = interp_index.reshape(2, TAKES)
     slab = slot >> 4

time: 165 us -> 151 us (0.915)
  blocking collectives: 45.5 us -> 24.5 us
  starting transfers between devices: 45.4 us -> 55.4 us
  Pallas kernels: 25.6 us -> 22.9 us
    all_gather x2 -> x1, blocking collectives: 45.5 us -> 24.5 us  [shards(): maps = lax.all_gather(jnp.stack(maps), 'h', axis=0)]
    ppermute x0 -> x3, starting transfers between devices: none -> 10.5 us  [shards(): lax.ppermute(place, 'x', [((i + k) % 4, i) for i in range(4)])]
    pallas_call x1, Pallas kernels: 17.8 us -> 14.8 us  [score(): pl.pallas_call(score_kernel, grid_spec=pltpu.PrefetchScalarGridSpec(num_s...]
    all_to_all x3, starting transfers between devices: 36.3 us -> 34.3 us  [exchange(): return lax.all_to_all(values, axes, split_axis=0, concat_axis=0, tiled=True)]
    unnamed x20 -> x18, local copies, waits for them, and re-layouts: 3.36 us -> 2.02 us
  transfers between devices with their start and end apart: 6 -> 9, of which waited for: 4 -> 5; matrix products, arithmetic and copies ran while one was open for 1% -> 2% of each run, Pallas kernels for 0% -> 1%
where the time goes in v4:
time: 151 us; the launch traced here: 150 us
  starting transfers between devices  55.4 us (37%)
  waiting for transfers between devices  41.2 us (27%)
  blocking collectives  24.5 us (16%)
  Pallas kernels  22.9 us (15%)
  local copies, waits for them, and re-layouts  3.43 us (2%)
  other arithmetic  1.7 us (1%)
    all_to_all x3, waiting for transfers between devices, exchange(): return lax.all_to_all(values, axes, split_axis=0, concat_axis=0, tiled=True)  37.7 us
    all_to_all x3, starting transfers between devices, exchange(): return lax.all_to_all(values, axes, split_axis=0, concat_axis=0, tiled=True)  34.3 us
    all_gather x1, blocking collectives, shards(): maps = lax.all_gather(jnp.stack(maps), 'h', axis=0)  24.5 us
    pallas_call x1, Pallas kernels, score(): pl.pallas_call(score_kernel, grid_spec=pltpu.PrefetchScalarGridSpec(num_s...  14.8 us
    ppermute x3, starting transfers between devices, shards(): lax.ppermute(place, 'x', [((i + k) % 4, i) for i in range(4)])  10.5 us
    ppermute x3, starting transfers between devices, shards(): lax.ppermute(block, 'x', [((i + k) % 4, i) for i in range(4)])  10.5 us
    pallas_call x1, Pallas kernels, pick(): pl.pallas_call(pick_kernel, grid_spec=pltpu.PrefetchScalarGridSpec(num_sc...  5.91 us
  transfers between devices with their start and end apart: 9, of which 5 were waited for; matrix products, arithmetic and copies ran while one was open for 2% of the time, Pallas kernels for 1%

profile of v4, /device:TPU:1, one launch (start us, length us, event | category | flops | bytes accessed | tf_op | source)
XLA Modules:
  0.0 150.0 jit_solution(2789541286403158222)
XLA Ops:
  0.0 0.0 copy-start.2
  0.0 1.0 copy-done.2
  1.0 0.0 copy-start.3
  1.0 0.9 copy-done.3
  2.0 0.0 copy-start.6
  2.0 1.4 shard_map.109
  3.4 20.6 %all-to-all-start = ((bf16[128,16,128]{2,1,0:T(8,128)(2,1)}), bf16[128,16,128]{2,1,0:T(8,128)(2,1)S(1)}, u32[]{:S(2)}, u32[]{:S(2)}) async-start(bf16[128,16,128]{2,1,0:T(8,128)(2,1)} %bitcast.8), calls=%async_computation | async-start | bytes 1048576 | tf_op jit(solution)/shard_map/all_to_all | solution.py:306
  24.0 0.0 copy-done.6
  24.0 0.1 copy.22
  24.1 0.1 reshape.65
  24.2 3.1 %collective-permute-start.2 = (f32[4,4,128]{2,1,0:T(4,128)S(1)}, f32[4,4,128]{2,1,0:T(4,128)S(1)}, u32[]{:S(2)}, u32[]{:S(2)}) collective-permute-start(f32[4,4,128]{2,1,0:T(4,128)S(1)} %reshape.65), channel_id=1, source_target_pairs={{3,0},{0,1},{1,2},{2,3},{7,4},{4,5},{5,6},{6,7},{11,8},{8,9},{9,10... | collective-permute-start | bytes 24584 | tf_op jit(solution)/shard_map/ppermute | solution.py:323
  27.3 4.4 %collective-permute-start.1 = (f32[4,4,128]{2,1,0:T(4,128)S(1)}, f32[4,4,128]{2,1,0:T(4,128)S(1)}, u32[]{:S(2)}, u32[]{:S(2)}) collective-permute-start(f32[4,4,128]{2,1,0:T(4,128)S(1)} %reshape.65), channel_id=1, source_target_pairs={{2,0},{3,1},{0,2},{1,3},{6,4},{7,5},{4,6},{5,7},{10,8},{11,9},{8,1... | collective-permute-start | bytes 24584 | tf_op jit(solution)/shard_map/ppermute | solution.py:323
  31.7 3.1 %collective-permute-start = (f32[4,4,128]{2,1,0:T(4,128)S(1)}, f32[4,4,128]{2,1,0:T(4,128)S(1)}, u32[]{:S(2)}, u32[]{:S(2)}) collective-permute-start(f32[4,4,128]{2,1,0:T(4,128)S(1)} %reshape.65), channel_id=1, source_target_pairs={{1,0},{2,1},{3,2},{0,3},{5,4},{6,5},{7,6},{4,7},{9,8},{10,9},{11,1... | collective-permute-start | bytes 24584 | tf_op jit(solution)/shard_map/ppermute | solution.py:323
  34.8 0.1 stack_reshape.3
  34.9 0.0 collective-permute-done.2
  34.9 0.0 collective-permute-done.1
  34.9 1.5 collective-permute-done
  36.4 24.5 %all-gather = f32[16,4,4,128]{3,2,1,0:T(4,128)S(1)} all-gather(f32[4,4,4,128]{3,2,1,0:T(4,128)S(1)} %pad_maximum_fusion.1), channel_id=2, replica_groups=mesh['y'=4,'h'=4,'l'=4,'c'=2,'x'=4] {'h'}, dimensions={0}, use_global_device_ids=true | all-gather | bytes 163840 | tf_op jit(solution)/shard_map/all_gather | solution.py:325
  60.9 0.0 all-to-all-done
  60.9 5.9 %shard_map.110 = bf16[32,4,4,16,128]{4,3,2,1,0:T(8,128)(2,1)} custom-call(s32[4]{0:T(128)S(1)} %and_select_fusion.order_ref, f32[4,4,4,128]{3,2,1,0:T(4,128)S(1)} %dynamic-slice_bitcast_fusion.4.place_ref, bf16[2048,128]{1,0:T(8,128)(2,1)S(1)} %bitcast.35), custom_call_target="tpu_custom_call" | custom-call | flops 2147483648 | bytes 4194304 | tf_op jit(solution)/shard_map/pallas_call | solution.py:176
  66.8 0.0 copy-start.8
  66.8 0.0 copy-start.7
  66.8 0.0 copy-start
  66.8 0.0 copy-start.1
  66.8 0.0 copy-start.4
  66.8 9.8 %all-to-all-start.1 = ((bf16[32,256,128]{2,1,0:T(8,128)(2,1)}), bf16[32,256,128]{2,1,0:T(8,128)(2,1)S(1)}, u32[]{:S(2)}, u32[]{:S(2)}) async-start(bf16[32,256,128]{2,1,0:T(8,128)(2,1)} %bitcast.36), calls=%async_computation.1 | async-start | bytes 4194304 | tf_op jit(solution)/shard_map/all_to_all | solution.py:306
  76.7 0.0 copy-start.5
  76.7 0.0 copy-done.8
  76.7 0.1 reshape.67
  76.8 0.0 copy-done.7
  76.8 0.1 reshape.74
  76.9 0.0 copy-done
  76.9 0.0 copy-done.1
  76.9 0.0 copy-done.4
  76.9 0.8 shard_map.111
  77.7 0.1 constant_dynamic-slice_fusion
  77.7 3.1 %collective-permute-start.5 = (bf16[544,128]{1,0:T(8,128)(2,1)S(1)}, bf16[544,128]{1,0:T(8,128)(2,1)S(1)}, u32[]{:S(2)}, u32[]{:S(2)}) collective-permute-start(bf16[544,128]{1,0:T(8,128)(2,1)S(1)} %get-tuple-element.6), channel_id=1, source_target_pairs={{3,0},{0,1},{1,2},{2,3},{7,4},{4,5},{5,6},{6,7},{11,8},{8,9},{9,10... | collective-permute-start | bytes 417800 | tf_op jit(solution)/shard_map/ppermute | solution.py:340
  80.9 4.6 %collective-permute-start.4 = (bf16[544,128]{1,0:T(8,128)(2,1)S(1)}, bf16[544,128]{1,0:T(8,128)(2,1)}, u32[]{:S(2)}, u32[]{:S(2)}) collective-permute-start(bf16[544,128]{1,0:T(8,128)(2,1)S(1)} %get-tuple-element.7), channel_id=1, source_target_pairs={{2,0},{3,1},{0,2},{1,3},{6,4},{7,5},{4,6},{5,7},{10,8},{11,9},{8,1... | collective-permute-start | bytes 417800 | tf_op jit(solution)/shard_map/ppermute | solution.py:340
  85.4 2.8 %collective-permute-start.3 = (bf16[544,128]{1,0:T(8,128)(2,1)S(1)}, bf16[544,128]{1,0:T(8,128)(2,1)}, u32[]{:S(2)}, u32[]{:S(2)}) collective-permute-start(bf16[544,128]{1,0:T(8,128)(2,1)S(1)} %get-tuple-element.8), channel_id=1, source_target_pairs={{1,0},{2,1},{3,2},{0,3},{5,4},{6,5},{7,6},{4,7},{9,8},{10,9},{11,1... | collective-permute-start | bytes 417800 | tf_op jit(solution)/shard_map/ppermute | solution.py:340
  88.9 0.9 dynamic-slice_bitcast_fusion.3.col_ref
  89.8 0.0 collective-permute-done.5
  89.9 0.3 collective-permute-done.4
  90.1 1.7 %collective-permute-done.3 = bf16[544,128]{1,0:T(8,128)(2,1)} collective-permute-done((bf16[544,128]{1,0:T(8,128)(2,1)S(1)}, bf16[544,128]{1,0:T(8,128)(2,1)}, u32[]{:S(2)}, u32[]{:S(2)}) %collective-permute-start.3) | collective-permute-done | bytes 139296 | tf_op jit(solution)/shard_map/ppermute | solution.py:340
  91.8 1.0 pad_maximum_fusion.weighted_ref
  92.9 33.5 %all-to-all-done.1 = bf16[32,256,128]{2,1,0:T(8,128)(2,1)S(1)} async-done(((bf16[32,256,128]{2,1,0:T(8,128)(2,1)}), bf16[32,256,128]{2,1,0:T(8,128)(2,1)S(1)}, u32[]{:S(2)}, u32[]{:S(2)}) %all-to-all-start.1) | async-done | bytes 2097184 | tf_op jit(solution)/shard_map/all_to_all | solution.py:306
  126.4 0.0 copy-done.5
  126.4 14.8 %shard_map.112 = f32[4,8,128]{2,1,0:T(8,128)} custom-call(s32[4]{0:T(128)S(1)} %and_select_fusion.order_ref, bf16[32,4,64,128]{3,2,1,0:T(8,128)(2,1)S(1)} %bitcast.34, bf16[4,544,128]{2,1,0:T(8,128)(2,1)S(1)} %pad_maximum_fusion.weighted_ref, bf16[256,256]{1,0:T(8,128)(2,1)S(1)} %dynamic-slice_bitcast_fusion.3.col_ref, f32[4,64,128]{2,1,0:T(8,128)S(1)} %copy-done.5), custom_call_target="tpu_custom_call" | custom-call | flops 8589934592 | bytes 4194304 | tf_op jit(solution)/shard_map/pallas_call | solution.py:277
  141.2 4.0 %all-to-all-start.2 = ((f32[4,8,128]{2,1,0:T(8,128)}), f32[4,8,128]{2,1,0:T(8,128)S(1)}, u32[]{:S(2)}, u32[]{:S(2)}) async-start(f32[4,8,128]{2,1,0:T(8,128)} %shard_map.112), calls=%async_computation.2 | async-start | bytes 32768 | tf_op jit(solution)/shard_map/all_to_all | solution.py:306
  145.2 4.2 %all-to-all-done.2 = f32[4,8,128]{2,1,0:T(8,128)S(1)} async-done(((f32[4,8,128]{2,1,0:T(8,128)}), f32[4,8,128]{2,1,0:T(8,128)S(1)}, u32[]{:S(2)}, u32[]{:S(2)}) %all-to-all-start.2) | async-done | bytes 16416 | tf_op jit(solution)/shard_map/all_to_all | solution.py:306
  149.4 0.6 broadcast_select_fusion
  (9 shorter events, 0.1 us)
Async XLA Ops:
  0.0 1.0 copy-start.2
  1.0 0.9 copy-start.3
  2.0 22.0 %copy-start.6 = (s32[1,1,128,16]{2,3,1,0:T(8,128)S(1)}, s32[1,1,128,16]{2,3,1,0:T(8,128)}, u32[]{:S(2)}) copy-start(s32[1,1,128,16]{2,3,1,0:T(8,128)} %param.12) | copy-start | bytes 24580
  3.4 57.5 %all-to-all-start = ((bf16[128,16,128]{2,1,0:T(8,128)(2,1)}), bf16[128,16,128]{2,1,0:T(8,128)(2,1)S(1)}, u32[]{:S(2)}, u32[]{:S(2)}) async-start(bf16[128,16,128]{2,1,0:T(8,128)(2,1)} %bitcast.8), calls=%async_computation | async-start | bytes 1048576 | tf_op jit(solution)/shard_map/all_to_all | solution.py:306
  24.2 10.7 %collective-permute-start.2 = (f32[4,4,128]{2,1,0:T(4,128)S(1)}, f32[4,4,128]{2,1,0:T(4,128)S(1)}, u32[]{:S(2)}, u32[]{:S(2)}) collective-permute-start(f32[4,4,128]{2,1,0:T(4,128)S(1)} %reshape.65), channel_id=1, source_target_pairs={{3,0},{0,1},{1,2},{2,3},{7,4},{4,5},{5,6},{6,7},{11,8},{8,9},{9,10... | collective-permute-start | bytes 24584 | tf_op jit(solution)/shard_map/ppermute | solution.py:323
  27.3 7.6 %collective-permute-start.1 = (f32[4,4,128]{2,1,0:T(4,128)S(1)}, f32[4,4,128]{2,1,0:T(4,128)S(1)}, u32[]{:S(2)}, u32[]{:S(2)}) collective-permute-start(f32[4,4,128]{2,1,0:T(4,128)S(1)} %reshape.65), channel_id=1, source_target_pairs={{2,0},{3,1},{0,2},{1,3},{6,4},{7,5},{4,6},{5,7},{10,8},{11,9},{8,1... | collective-permute-start | bytes 24584 | tf_op jit(solution)/shard_map/ppermute | solution.py:323
  31.7 4.7 %collective-permute-start = (f32[4,4,128]{2,1,0:T(4,128)S(1)}, f32[4,4,128]{2,1,0:T(4,128)S(1)}, u32[]{:S(2)}, u32[]{:S(2)}) collective-permute-start(f32[4,4,128]{2,1,0:T(4,128)S(1)} %reshape.65), channel_id=1, source_target_pairs={{1,0},{2,1},{3,2},{0,3},{5,4},{6,5},{7,6},{4,7},{9,8},{10,9},{11,1... | collective-permute-start | bytes 24584 | tf_op jit(solution)/shard_map/ppermute | solution.py:323
  66.8 9.9 %copy-start.8 = (f32[1,8,64]{2,1,0:T(8,128)S(1)}, f32[1,8,64]{2,1,0:T(8,128)}, u32[]{:S(2)}) copy-start(f32[1,8,64]{2,1,0:T(8,128)} %param.14) | copy-start | bytes 6148
  66.8 10.0 %copy-start.7 = (s32[2,1,8,64]{3,2,1,0:T(8,128)S(1)}, s32[2,1,8,64]{3,2,1,0:T(8,128)}, u32[]{:S(2)}) copy-start(s32[2,1,8,64]{3,2,1,0:T(8,128)} %param.13) | copy-start | bytes 12292
  66.8 10.1 %copy-start = (bf16[8,64,512]{2,1,0:T(8,128)(2,1)S(1)}, bf16[8,64,512]{2,1,0:T(8,128)(2,1)}, u32[]{:S(2)}) copy-start(bf16[8,64,512]{2,1,0:T(8,128)(2,1)} %spectra_ref.1) | copy-start | bytes 1572868
  66.8 10.1 %copy-start.1 = (bf16[16,64,256]{2,1,0:T(8,128)(2,1)S(1)}, bf16[16,64,256]{2,1,0:T(8,128)(2,1)}, u32[]{:S(2)}) copy-start(bf16[16,64,256]{2,1,0:T(8,128)(2,1)} %ctf_ref.1) | copy-start | bytes 1572868
  66.8 10.1 %copy-start.4 = (s32[8]{0:T(128)S(1)}, s32[8]{0:T(128)}, u32[]{:S(2)}) copy-start(s32[8]{0:T(128)} %class_ref.1) | copy-start | bytes 100
  66.8 59.5 %all-to-all-start.1 = ((bf16[32,256,128]{2,1,0:T(8,128)(2,1)}), bf16[32,256,128]{2,1,0:T(8,128)(2,1)S(1)}, u32[]{:S(2)}, u32[]{:S(2)}) async-start(bf16[32,256,128]{2,1,0:T(8,128)(2,1)} %bitcast.36), calls=%async_computation.1 | async-start | bytes 4194304 | tf_op jit(solution)/shard_map/all_to_all | solution.py:306
  76.7 49.7 %copy-start.5 = (f32[4,64,128]{2,1,0:T(8,128)S(1)}, f32[4,64,128]{2,1,0:T(8,128)}, u32[]{:S(2)}) copy-start(f32[4,64,128]{2,1,0:T(8,128)} %constant.109.clone.row_ref) | copy-start | bytes 393220
  77.7 12.1 %collective-permute-start.5 = (bf16[544,128]{1,0:T(8,128)(2,1)S(1)}, bf16[544,128]{1,0:T(8,128)(2,1)S(1)}, u32[]{:S(2)}, u32[]{:S(2)}) collective-permute-start(bf16[544,128]{1,0:T(8,128)(2,1)S(1)} %get-tuple-element.6), channel_id=1, source_target_pairs={{3,0},{0,1},{1,2},{2,3},{7,4},{4,5},{5,6},{6,7},{11,8},{8,9},{9,10... | collective-permute-start | bytes 417800 | tf_op jit(solution)/shard_map/ppermute | solution.py:340
  80.9 9.3 %collective-permute-start.4 = (bf16[544,128]{1,0:T(8,128)(2,1)S(1)}, bf16[544,128]{1,0:T(8,128)(2,1)}, u32[]{:S(2)}, u32[]{:S(2)}) collective-permute-start(bf16[544,128]{1,0:T(8,128)(2,1)S(1)} %get-tuple-element.7), channel_id=1, source_target_pairs={{2,0},{3,1},{0,2},{1,3},{6,4},{7,5},{4,6},{5,7},{10,8},{11,9},{8,1... | collective-permute-start | bytes 417800 | tf_op jit(solution)/shard_map/ppermute | solution.py:340
  85.4 6.4 %collective-permute-start.3 = (bf16[544,128]{1,0:T(8,128)(2,1)S(1)}, bf16[544,128]{1,0:T(8,128)(2,1)}, u32[]{:S(2)}, u32[]{:S(2)}) collective-permute-start(bf16[544,128]{1,0:T(8,128)(2,1)S(1)} %get-tuple-element.8), channel_id=1, source_target_pairs={{1,0},{2,1},{3,2},{0,3},{5,4},{6,5},{7,6},{4,7},{9,8},{10,9},{11,1... | collective-permute-start | bytes 417800 | tf_op jit(solution)/shard_map/ppermute | solution.py:340
  141.2 8.2 %all-to-all-start.2 = ((f32[4,8,128]{2,1,0:T(8,128)}), f32[4,8,128]{2,1,0:T(8,128)S(1)}, u32[]{:S(2)}, u32[]{:S(2)}) async-start(f32[4,8,128]{2,1,0:T(8,128)} %shard_map.112), calls=%async_computation.2 | async-start | bytes 32768 | tf_op jit(solution)/shard_map/all_to_all | solution.py:306

commit v5 on v4

--- a/solution.py
+++ b/solution.py
@@ -45,23 +45,25 @@
 
 
 def column_table():
-    b = np.arange(TRANS) % TSIDE - TSIDE // 2
-    v = np.arange(NF)
-    angle = -2.0 * math.pi / NF * ((b[None, :] * v[:, None]) % NF)
-    fr = np.cos(angle).reshape(N_GRP, COLS, TRANS) / NF
-    fi = np.sin(angle).reshape(N_GRP, COLS, TRANS) / NF
-    with_er = np.concatenate([fr, fr, -fi, fi], axis=1)
-    with_ei = np.concatenate([-fi, -fi, -fr, fr], axis=1)
-    high, low = split_bf16(np.concatenate([with_er, with_ei], axis=2))
-    return np.concatenate([high, low], axis=2)
+    t = np.arange(TRANS)
+    a = t // TSIDE - TSIDE // 2
+    b = t % TSIDE - TSIDE // 2
+    v = np.arange(NF).reshape(N_GRP, 1, COLS, 1)
+    d = np.arange(8).reshape(1, 8, 1, 1)
+    angle = -2.0 * math.pi / NF * ((b * v + 8 * a * d) % NF)
+    fr = np.cos(angle) / NF
+    fi = np.sin(angle) / NF
+    with_er = np.concatenate([fr, fr, -fi, fi], axis=2)
+    with_ei = np.concatenate([-fi, -fi, -fr, fr], axis=2)
+    high, low = split_bf16(np.concatenate([with_er, with_ei], axis=3))
+    return np.concatenate([high, low], axis=3)
 
 
 def row_table():
     a = np.arange(TRANS) // TSIDE - TSIDE // 2
-    u = np.arange(NF)
-    angle = -2.0 * math.pi / NF * ((a[None, :] * u[:, None]) % NF)
-    table = np.concatenate([np.cos(angle), np.sin(angle)], axis=1).astype(np.float32)
-    return table.reshape(N_GRP, COLS, 2 * TRANS)
+    u = np.arange(NF).reshape(N_GRP, COLS)[:, :8]
+    angle = -2.0 * math.pi / NF * ((a * u[:, :, None]) % NF)
+    return np.concatenate([np.cos(angle), np.sin(angle)], axis=2).astype(np.float32)
 
 
 def down_rows(row):
@@ -239,38 +241,35 @@
         )
         mixed = part if mixed is None else mixed + part
     slices[...] = mixed
-    phase_rows = row_ref[...]
-    left = lax.broadcasted_iota(jnp.int32, (PART_DEV, LANES), 1) < TRANS
-    weight = weighted_ref[:PARTICLE_ROWS, :].astype(jnp.float32).reshape(PART_DEV, COLS, LANES)
-    for pair in range(ORI_MAX // 2):
-        products = []
-        for orient in (2 * pair, 2 * pair + 1):
-            plain = slices[orient * COLS : (orient + 1) * COLS, :]
-            swapped = pltpu.roll(plain, COLS, 1)
-            products.append(
-                jnp.concatenate(
-                    [
-                        (weight * plain[None]).astype(jnp.bfloat16),
-                        (weight * swapped[None]).astype(jnp.bfloat16),
-                    ],
-                    axis=-1,
-                ).reshape(PARTICLE_ROWS, 2 * LANES)
-            )
-        columns = jnp.dot(
-            jnp.concatenate(products, axis=0), col_ref[...], preferred_element_type=jnp.float32
+    plain = slices[...]
+    plain_parts = plain.reshape(ORI_MAX, 1, 8, 8, LANES)
+    swapped_parts = pltpu.roll(plain, COLS, 1).reshape(ORI_MAX, 1, 8, 8, LANES)
+    weight = weighted_ref[:PARTICLE_ROWS, :].astype(jnp.float32)
+    weight = weight.reshape(1, PART_DEV, 8, 8, LANES)
+    columns = None
+    for d in range(8):
+        products = jnp.concatenate(
+            [
+                (weight[:, :, d] * parts[:, :, d]).reshape(8 * COLS, LANES).astype(jnp.bfloat16)
+                for parts in (plain_parts, swapped_parts)
+            ],
+            axis=1,
         )
-        columns = (columns[:, :LANES] + columns[:, LANES:]).reshape(2, PART_DEV, COLS, LANES)
-        summed = jnp.sum(columns * phase_rows[None, None], axis=2)
-        done = [summed[at] + pltpu.roll(summed[at], TRANS, 1) for at in range(2)]
-        total = jnp.where(left, done[0], done[1])
-
-        @pl.when(pl.program_id(0) == 0)
-        def _():
-            out_ref[pair] = total
-
-        @pl.when(pl.program_id(0) > 0)
-        def _():
-            out_ref[pair] += total
+        part = jnp.dot(products, col_ref[d], preferred_element_type=jnp.float32)
+        columns = part if columns is None else columns + part
+    columns = (columns[:, :LANES] + columns[:, LANES:]).reshape(ORI_MAX * PART_DEV, 8, LANES)
+    summed = jnp.sum(columns * row_ref[...][None], axis=1)
+    folded = (summed + pltpu.roll(summed, TRANS, 1)).reshape(ORI_MAX // 2, 2, PART_DEV, LANES)
+    left = lax.broadcasted_iota(jnp.int32, (ORI_MAX // 2, PART_DEV, LANES), 2) < TRANS
+    total = jnp.where(left, folded[:, 0], folded[:, 1])
+
+    @pl.when(pl.program_id(0) == 0)
+    def _():
+        out_ref[...] = total
+
+    @pl.when(pl.program_id(0) > 0)
+    def _():
+        out_ref[...] += total
 
 
 def score(order, buffer, weighted, col_phase, row_phase):
@@ -286,8 +285,8 @@
                 pl.BlockSpec(
                     (None, PARTICLE_ROWS + EXTRA_ROWS, LANES), lambda i, order: (i, 0, 0)
                 ),
-                pl.BlockSpec((2 * LANES, 2 * LANES), lambda i, order: (0, 0)),
-                pl.BlockSpec((None, COLS, LANES), lambda i, order: (order[i], 0, 0)),
+                pl.BlockSpec((8, 2 * LANES, 2 * LANES), lambda i, order: (0, 0, 0)),
+                pl.BlockSpec((None, 8, LANES), lambda i, order: (order[i], 0, 0)),
             ],
             out_specs=pl.BlockSpec(
                 (ORI_MAX // 2, PART_DEV, LANES), lambda i, order: (0, 0, 0)

time: 151 us -> 149 us (0.987)
  Pallas kernels: 22.9 us -> 19.7 us
  local copies, waits for them, and re-layouts: 3.43 us -> 5.58 us
  waiting for transfers between devices: 41.2 us -> 39.6 us
  other arithmetic: 1.7 us -> 3.27 us
    pallas_call x1, Pallas kernels: 14.8 us -> 11.6 us  [score(): pl.pallas_call(score_kernel, grid_spec=pltpu.PrefetchScalarGridSpec(num_s...]
  transfers between devices with their start and end apart: 9 -> 9, of which waited for: 5 -> 5; matrix products, arithmetic and copies ran while one was open for 2% -> 3% of each run, Pallas kernels for 1% -> 1%
where the time goes in v5:
time: 149 us; the launch traced here: 148 us
  starting transfers between devices  55.3 us (37%)
  waiting for transfers between devices  39.6 us (27%)
  blocking collectives  23.7 us (16%)
  Pallas kernels  19.7 us (13%)
  local copies, waits for them, and re-layouts  5.58 us (4%)
  other arithmetic  3.27 us (2%)
    all_to_all x3, waiting for transfers between devices, exchange(): return lax.all_to_all(values, axes, split_axis=0, concat_axis=0, tiled=True)  36.3 us
    all_to_all x3, starting transfers between devices, exchange(): return lax.all_to_all(values, axes, split_axis=0, concat_axis=0, tiled=True)  34.6 us
    all_gather x1, blocking collectives, shards(): maps = lax.all_gather(jnp.stack(maps), 'h', axis=0)  23.7 us
    pallas_call x1, Pallas kernels, score(): pl.pallas_call(score_kernel, grid_spec=pltpu.PrefetchScalarGridSpec(num_s...  11.6 us
    ppermute x3, starting transfers between devices, shards(): lax.ppermute(place, 'x', [((i + k) % 4, i) for i in range(4)])  10.5 us
    ppermute x3, starting transfers between devices, shards(): lax.ppermute(block, 'x', [((i + k) % 4, i) for i in range(4)])  10.1 us
    pallas_call x1, Pallas kernels, pick(): pl.pallas_call(pick_kernel, grid_spec=pltpu.PrefetchScalarGridSpec(num_sc...  5.92 us
    unnamed x18, local copies, waits for them, and re-layouts  3.08 us
  transfers between devices with their start and end apart: 9, of which 5 were waited for; matrix products, arithmetic and copies ran while one was open for 3% of the time, Pallas kernels for 1%

profile of v5, /device:TPU:1, one launch (start us, length us, event | category | flops | bytes accessed | tf_op | source)
XLA Modules:
  0.0 148.1 jit_solution(747635654143839071)
XLA Ops:
  0.0 0.0 copy-start.3
  0.0 1.0 copy-done.3
  1.0 0.0 copy-start.4
  1.0 0.9 copy-done.4
  2.0 1.4 shard_map.109
  3.4 20.6 %all-to-all-start = ((bf16[128,16,128]{2,1,0:T(8,128)(2,1)}), bf16[128,16,128]{2,1,0:T(8,128)(2,1)S(1)}, u32[]{:S(2)}, u32[]{:S(2)}) async-start(bf16[128,16,128]{2,1,0:T(8,128)(2,1)} %bitcast.8), calls=%async_computation | async-start | bytes 1048576 | tf_op jit(solution)/shard_map/all_to_all | solution.py:305
  24.0 0.7 or_convert_fusion.1
  24.7 0.1 copy.22
  24.8 0.1 reshape.65
  24.9 3.1 %collective-permute-start.2 = (f32[4,4,128]{2,1,0:T(4,128)S(1)}, f32[4,4,128]{2,1,0:T(4,128)S(1)}, u32[]{:S(2)}, u32[]{:S(2)}) collective-permute-start(f32[4,4,128]{2,1,0:T(4,128)S(1)} %reshape.65), channel_id=1, source_target_pairs={{3,0},{0,1},{1,2},{2,3},{7,4},{4,5},{5,6},{6,7},{11,8},{8,9},{9,10... | collective-permute-start | bytes 24584 | tf_op jit(solution)/shard_map/ppermute | solution.py:322
  28.0 4.4 %collective-permute-start.1 = (f32[4,4,128]{2,1,0:T(4,128)S(1)}, f32[4,4,128]{2,1,0:T(4,128)S(1)}, u32[]{:S(2)}, u32[]{:S(2)}) collective-permute-start(f32[4,4,128]{2,1,0:T(4,128)S(1)} %reshape.65), channel_id=1, source_target_pairs={{2,0},{3,1},{0,2},{1,3},{6,4},{7,5},{4,6},{5,7},{10,8},{11,9},{8,1... | collective-permute-start | bytes 24584 | tf_op jit(solution)/shard_map/ppermute | solution.py:322
  32.4 3.1 %collective-permute-start = (f32[4,4,128]{2,1,0:T(4,128)S(1)}, f32[4,4,128]{2,1,0:T(4,128)S(1)}, u32[]{:S(2)}, u32[]{:S(2)}) collective-permute-start(f32[4,4,128]{2,1,0:T(4,128)S(1)} %reshape.65), channel_id=1, source_target_pairs={{1,0},{2,1},{3,2},{0,3},{5,4},{6,5},{7,6},{4,7},{9,8},{10,9},{11,1... | collective-permute-start | bytes 24584 | tf_op jit(solution)/shard_map/ppermute | solution.py:322
  35.5 0.1 stack_reshape.3
  35.6 0.0 collective-permute-done.2
  35.6 0.0 collective-permute-done.1
  35.6 1.5 %collective-permute-done = f32[4,4,128]{2,1,0:T(4,128)S(1)} collective-permute-done((f32[4,4,128]{2,1,0:T(4,128)S(1)}, f32[4,4,128]{2,1,0:T(4,128)S(1)}, u32[]{:S(2)}, u32[]{:S(2)}) %collective-permute-start) | collective-permute-done | bytes 8224 | tf_op jit(solution)/shard_map/ppermute | solution.py:322
  37.1 23.7 %all-gather = f32[16,4,4,128]{3,2,1,0:T(4,128)S(1)} all-gather(f32[4,4,4,128]{3,2,1,0:T(4,128)S(1)} %pad_maximum_fusion.1), channel_id=2, replica_groups=mesh['y'=4,'h'=4,'l'=4,'c'=2,'x'=4] {'h'}, dimensions={0}, use_global_device_ids=true | all-gather | bytes 163840 | tf_op jit(solution)/shard_map/all_gather | solution.py:324
  60.8 0.0 all-to-all-done
  60.8 0.0 copy-start.8
  60.9 0.0 copy-start.7
  60.9 0.0 copy-start.1
  60.9 0.0 copy-start.2
  60.9 0.0 copy-start.5
  60.9 5.9 %shard_map.110 = bf16[32,4,4,16,128]{4,3,2,1,0:T(8,128)(2,1)} custom-call(s32[4]{0:T(128)S(1)} %and_select_fusion.order_ref, f32[4,4,4,128]{3,2,1,0:T(4,128)S(1)} %dynamic-slice_bitcast_fusion.4.place_ref, bf16[2048,128]{1,0:T(8,128)(2,1)S(1)} %bitcast.35), custom_call_target="tpu_custom_call" | custom-call | flops 2147483648 | bytes 4194304 | tf_op jit(solution)/shard_map/pallas_call | solution.py:178
  66.8 0.0 copy-start.6
  66.8 10.2 %all-to-all-start.1 = ((bf16[32,256,128]{2,1,0:T(8,128)(2,1)}), bf16[32,256,128]{2,1,0:T(8,128)(2,1)S(1)}, u32[]{:S(2)}, u32[]{:S(2)}) async-start(bf16[32,256,128]{2,1,0:T(8,128)(2,1)} %bitcast.36), calls=%async_computation.1 | async-start | bytes 4194304 | tf_op jit(solution)/shard_map/all_to_all | solution.py:305
  77.1 0.0 copy-done.8
  77.1 0.1 reshape.67
  77.2 0.0 copy-done.7
  77.2 0.1 reshape.74
  77.3 0.0 copy-done.1
  77.3 0.0 copy-done.2
  77.3 0.0 copy-done.5
  77.3 0.8 shard_map.111
  78.1 0.8 constant_dynamic-slice_fusion
  78.8 2.8 %collective-permute-start.5 = (bf16[544,128]{1,0:T(8,128)(2,1)}, bf16[544,128]{1,0:T(8,128)(2,1)}, u32[]{:S(2)}, u32[]{:S(2)}) collective-permute-start(bf16[544,128]{1,0:T(8,128)(2,1)} %get-tuple-element.6), channel_id=1, source_target_pairs={{3,0},{0,1},{1,2},{2,3},{7,4},{4,5},{5,6},{6,7},{11,8},{8,9},{9,10... | collective-permute-start | bytes 417800 | tf_op jit(solution)/shard_map/ppermute | solution.py:339
  81.6 4.8 %collective-permute-start.4 = (bf16[544,128]{1,0:T(8,128)(2,1)}, bf16[544,128]{1,0:T(8,128)(2,1)}, u32[]{:S(2)}, u32[]{:S(2)}) collective-permute-start(bf16[544,128]{1,0:T(8,128)(2,1)} %get-tuple-element.7), channel_id=1, source_target_pairs={{2,0},{3,1},{0,2},{1,3},{6,4},{7,5},{4,6},{5,7},{10,8},{11,9},{8,1... | collective-permute-start | bytes 417800 | tf_op jit(solution)/shard_map/ppermute | solution.py:339
  86.4 2.6 %collective-permute-start.3 = (bf16[544,128]{1,0:T(8,128)(2,1)S(1)}, bf16[544,128]{1,0:T(8,128)(2,1)}, u32[]{:S(2)}, u32[]{:S(2)}) collective-permute-start(bf16[544,128]{1,0:T(8,128)(2,1)S(1)} %get-tuple-element.8), channel_id=1, source_target_pairs={{1,0},{2,1},{3,2},{0,3},{5,4},{6,5},{7,6},{4,7},{9,8},{10,9},{11,1... | collective-permute-start | bytes 417800 | tf_op jit(solution)/shard_map/ppermute | solution.py:339
  89.7 1.3 dynamic-slice_bitcast_fusion.col_ref
  91.0 0.0 collective-permute-done.5
  91.0 0.4 collective-permute-done.4
  91.4 1.5 collective-permute-done.3
  92.8 1.9 %pad_maximum_fusion.weighted_ref = bf16[4,544,128]{2,1,0:T(8,128)(2,1)} fusion(bf16[1,544,128]{2,1,0:T(8,128)(2,1)} %bitcast.17, bf16[1,544,128]{2,1,0:T(8,128)(2,1)} %bitcast.15, bf16[1,544,128]{2,1,0:T(8,128)(2,1)} %bitcast.13, bf16[1,544,128]{2,1,0:T(8,128)(2,1)S(1)} %get-tuple-element.5), kind=kLoop, calls=%fused_computation.1 | loop fusion | flops 835584 | bytes 1114112 | tf_op jit(solution)/shard_map/stack | solution.py:343
  94.7 32.1 %all-to-all-done.1 = bf16[32,256,128]{2,1,0:T(8,128)(2,1)S(1)} async-done(((bf16[32,256,128]{2,1,0:T(8,128)(2,1)}), bf16[32,256,128]{2,1,0:T(8,128)(2,1)S(1)}, u32[]{:S(2)}, u32[]{:S(2)}) %all-to-all-start.1) | async-done | bytes 2097184 | tf_op jit(solution)/shard_map/all_to_all | solution.py:305
  126.8 0.0 copy-done.6
  126.8 0.0 copy-start
  126.8 1.1 copy-done
  127.9 11.6 %shard_map.112 = f32[4,8,128]{2,1,0:T(8,128)} custom-call(s32[4]{0:T(128)S(1)} %and_select_fusion.order_ref, bf16[32,4,64,128]{3,2,1,0:T(8,128)(2,1)S(1)} %bitcast.34, bf16[4,544,128]{2,1,0:T(8,128)(2,1)S(1)} %copy-done, bf16[8,256,256]{2,1,0:T(8,128)(2,1)S(1)} %dynamic-slice_bitcast_fusion.col_ref, f32[4,8,128]{2,1,0:T(8,128)S(1)} %copy-done.6), custom_call_target="tpu_custom_call" | custom-call | flops 8589934592 | bytes 4194304 | tf_op jit(solution)/shard_map/pallas_call | solution.py:276
  139.4 3.8 %all-to-all-start.2 = ((f32[4,8,128]{2,1,0:T(8,128)}), f32[4,8,128]{2,1,0:T(8,128)S(1)}, u32[]{:S(2)}, u32[]{:S(2)}) async-start(f32[4,8,128]{2,1,0:T(8,128)} %shard_map.112), calls=%async_computation.2 | async-start | bytes 32768 | tf_op jit(solution)/shard_map/all_to_all | solution.py:305
  143.3 4.2 %all-to-all-done.2 = f32[4,8,128]{2,1,0:T(8,128)S(1)} async-done(((f32[4,8,128]{2,1,0:T(8,128)}), f32[4,8,128]{2,1,0:T(8,128)S(1)}, u32[]{:S(2)}, u32[]{:S(2)}) %all-to-all-start.2) | async-done | bytes 16416 | tf_op jit(solution)/shard_map/all_to_all | solution.py:305
  147.5 0.6 broadcast_select_fusion
  (8 shorter events, 0.1 us)
Async XLA Ops:
  0.0 1.0 copy-start.3
  1.0 0.9 copy-start.4
  3.4 57.4 %all-to-all-start = ((bf16[128,16,128]{2,1,0:T(8,128)(2,1)}), bf16[128,16,128]{2,1,0:T(8,128)(2,1)S(1)}, u32[]{:S(2)}, u32[]{:S(2)}) async-start(bf16[128,16,128]{2,1,0:T(8,128)(2,1)} %bitcast.8), calls=%async_computation | async-start | bytes 1048576 | tf_op jit(solution)/shard_map/all_to_all | solution.py:305
  24.9 10.7 %collective-permute-start.2 = (f32[4,4,128]{2,1,0:T(4,128)S(1)}, f32[4,4,128]{2,1,0:T(4,128)S(1)}, u32[]{:S(2)}, u32[]{:S(2)}) collective-permute-start(f32[4,4,128]{2,1,0:T(4,128)S(1)} %reshape.65), channel_id=1, source_target_pairs={{3,0},{0,1},{1,2},{2,3},{7,4},{4,5},{5,6},{6,7},{11,8},{8,9},{9,10... | collective-permute-start | bytes 24584 | tf_op jit(solution)/shard_map/ppermute | solution.py:322
  28.0 7.6 %collective-permute-start.1 = (f32[4,4,128]{2,1,0:T(4,128)S(1)}, f32[4,4,128]{2,1,0:T(4,128)S(1)}, u32[]{:S(2)}, u32[]{:S(2)}) collective-permute-start(f32[4,4,128]{2,1,0:T(4,128)S(1)} %reshape.65), channel_id=1, source_target_pairs={{2,0},{3,1},{0,2},{1,3},{6,4},{7,5},{4,6},{5,7},{10,8},{11,9},{8,1... | collective-permute-start | bytes 24584 | tf_op jit(solution)/shard_map/ppermute | solution.py:322
  32.4 4.7 %collective-permute-start = (f32[4,4,128]{2,1,0:T(4,128)S(1)}, f32[4,4,128]{2,1,0:T(4,128)S(1)}, u32[]{:S(2)}, u32[]{:S(2)}) collective-permute-start(f32[4,4,128]{2,1,0:T(4,128)S(1)} %reshape.65), channel_id=1, source_target_pairs={{1,0},{2,1},{3,2},{0,3},{5,4},{6,5},{7,6},{4,7},{9,8},{10,9},{11,1... | collective-permute-start | bytes 24584 | tf_op jit(solution)/shard_map/ppermute | solution.py:322
  60.8 16.3 %copy-start.8 = (f32[1,8,64]{2,1,0:T(8,128)S(1)}, f32[1,8,64]{2,1,0:T(8,128)}, u32[]{:S(2)}) copy-start(f32[1,8,64]{2,1,0:T(8,128)} %param.14) | copy-start | bytes 6148
  60.9 16.3 %copy-start.7 = (s32[2,1,8,64]{3,2,1,0:T(8,128)S(1)}, s32[2,1,8,64]{3,2,1,0:T(8,128)}, u32[]{:S(2)}) copy-start(s32[2,1,8,64]{3,2,1,0:T(8,128)} %param.13) | copy-start | bytes 12292
  60.9 16.4 %copy-start.1 = (bf16[8,64,512]{2,1,0:T(8,128)(2,1)S(1)}, bf16[8,64,512]{2,1,0:T(8,128)(2,1)}, u32[]{:S(2)}) copy-start(bf16[8,64,512]{2,1,0:T(8,128)(2,1)} %spectra_ref.1) | copy-start | bytes 1572868
  60.9 16.4 %copy-start.2 = (bf16[16,64,256]{2,1,0:T(8,128)(2,1)S(1)}, bf16[16,64,256]{2,1,0:T(8,128)(2,1)}, u32[]{:S(2)}) copy-start(bf16[16,64,256]{2,1,0:T(8,128)(2,1)} %ctf_ref.1) | copy-start | bytes 1572868
  60.9 16.4 %copy-start.5 = (s32[8]{0:T(128)S(1)}, s32[8]{0:T(128)}, u32[]{:S(2)}) copy-start(s32[8]{0:T(128)} %class_ref.1) | copy-start | bytes 100
  66.8 60.0 %copy-start.6 = (f32[4,8,128]{2,1,0:T(8,128)S(1)}, f32[4,8,128]{2,1,0:T(8,128)}, u32[]{:S(2)}) copy-start(f32[4,8,128]{2,1,0:T(8,128)} %constant.109.clone.row_ref) | copy-start | bytes 49156
  66.8 60.0 %all-to-all-start.1 = ((bf16[32,256,128]{2,1,0:T(8,128)(2,1)}), bf16[32,256,128]{2,1,0:T(8,128)(2,1)S(1)}, u32[]{:S(2)}, u32[]{:S(2)}) async-start(bf16[32,256,128]{2,1,0:T(8,128)(2,1)} %bitcast.36), calls=%async_computation.1 | async-start | bytes 4194304 | tf_op jit(solution)/shard_map/all_to_all | solution.py:305
  78.8 12.1 %collective-permute-start.5 = (bf16[544,128]{1,0:T(8,128)(2,1)}, bf16[544,128]{1,0:T(8,128)(2,1)}, u32[]{:S(2)}, u32[]{:S(2)}) collective-permute-start(bf16[544,128]{1,0:T(8,128)(2,1)} %get-tuple-element.6), channel_id=1, source_target_pairs={{3,0},{0,1},{1,2},{2,3},{7,4},{4,5},{5,6},{6,7},{11,8},{8,9},{9,10... | collective-permute-start | bytes 417800 | tf_op jit(solution)/shard_map/ppermute | solution.py:339
  81.6 9.7 %collective-permute-start.4 = (bf16[544,128]{1,0:T(8,128)(2,1)}, bf16[544,128]{1,0:T(8,128)(2,1)}, u32[]{:S(2)}, u32[]{:S(2)}) collective-permute-start(bf16[544,128]{1,0:T(8,128)(2,1)} %get-tuple-element.7), channel_id=1, source_target_pairs={{2,0},{3,1},{0,2},{1,3},{6,4},{7,5},{4,6},{5,7},{10,8},{11,9},{8,1... | collective-permute-start | bytes 417800 | tf_op jit(solution)/shard_map/ppermute | solution.py:339
  86.4 6.4 %collective-permute-start.3 = (bf16[544,128]{1,0:T(8,128)(2,1)S(1)}, bf16[544,128]{1,0:T(8,128)(2,1)}, u32[]{:S(2)}, u32[]{:S(2)}) collective-permute-start(bf16[544,128]{1,0:T(8,128)(2,1)S(1)} %get-tuple-element.8), channel_id=1, source_target_pairs={{1,0},{2,1},{3,2},{0,3},{5,4},{6,5},{7,6},{4,7},{9,8},{10,9},{11,1... | collective-permute-start | bytes 417800 | tf_op jit(solution)/shard_map/ppermute | solution.py:339
  126.8 1.1 copy-start
  139.4 8.1 %all-to-all-start.2 = ((f32[4,8,128]{2,1,0:T(8,128)}), f32[4,8,128]{2,1,0:T(8,128)S(1)}, u32[]{:S(2)}, u32[]{:S(2)}) async-start(f32[4,8,128]{2,1,0:T(8,128)} %shard_map.112), calls=%async_computation.2 | async-start | bytes 32768 | tf_op jit(solution)/shard_map/all_to_all | solution.py:305

commit v6 on v5

--- a/solution.py
+++ b/solution.py
@@ -68,16 +68,6 @@
 
 def down_rows(row):
     return jnp.broadcast_to(row, (LANES, LANES)).T
-
-
-def hit_tiles(rows, total, weights=(1.0,)):
-    lane = lax.broadcasted_iota(jnp.int32, (LANES, LANES), 1).astype(jnp.float32)
-    ahead = [down_rows(row) - lane for row in rows]
-    tiles = []
-    for first in range(0, total, LANES):
-        parts = [jnp.where(far == float(first), w, 0.0) for far, w in zip(ahead, weights)]
-        tiles.append(sum(parts[1:], parts[0]).astype(jnp.bfloat16))
-    return tiles
 
 
 def fourier_kernel(x_ref, table_ref, out_ref, wide):
@@ -161,17 +151,28 @@
         wide[...] = table_ref[...].astype(jnp.float32)
         for slab in range(4):
             for ky in range(2):
-                slabs[slab, ky * NF : (ky + 1) * NF, :] = wide[
+                slabs[slab, :, ky * LANES : (ky + 1) * LANES] = wide[
                     pl.ds(2 * slab + ky, NF, stride=8), :
                 ].astype(jnp.bfloat16)
 
+    lane = lax.broadcasted_iota(jnp.int32, (LANES, LANES), 1).astype(jnp.float32)
     for slab in range(4):
+        later = []
         for row in range(4):
-            tiles = hit_tiles([place_ref[slab, row : row + 1, :]], SLAB_ROWS)
-            for at, tile in enumerate(tiles):
-                hits[row * LANES : (row + 1) * LANES, at * LANES : (at + 1) * LANES] = tile
+            column = down_rows(place_ref[slab, row : row + 1, :])
+            later.append(column >= float(NF))
+            ahead = jnp.where(later[-1], column - float(NF), column) - lane
+            for first in range(0, NF, LANES):
+                hits[row * LANES : (row + 1) * LANES, first : first + LANES] = jnp.where(
+                    ahead == float(first), 1.0, 0.0
+                ).astype(jnp.bfloat16)
         taken = jnp.dot(hits[...], slabs[slab], preferred_element_type=jnp.float32)
-        out_ref[:, slab, :, :] = taken.astype(jnp.bfloat16).reshape(32, CAP, LANES)
+        for row in range(4):
+            span = taken[row * LANES : (row + 1) * LANES]
+            chosen = jnp.where(later[row], span[:, LANES:], span[:, :LANES])
+            out_ref[row * 8 : (row + 1) * 8, slab, :, :] = chosen.astype(jnp.bfloat16).reshape(
+                8, CAP, LANES
+            )
 
 
 def pick(order, place, table):
@@ -189,8 +190,8 @@
             ),
             scratch_shapes=[
                 pltpu.VMEM((4 * SLAB_ROWS, LANES), jnp.float32),
-                pltpu.VMEM((4, SLAB_ROWS, LANES), jnp.bfloat16),
-                pltpu.VMEM((SLAB_ROWS, SLAB_ROWS), jnp.bfloat16),
+                pltpu.VMEM((4, NF, 2 * LANES), jnp.bfloat16),
+                pltpu.VMEM((SLAB_ROWS, NF), jnp.bfloat16),
             ],
         ),
         out_shape=pltpu.HBM((32, N_GRP, 4, CAP, LANES), jnp.bfloat16),
@@ -201,8 +202,14 @@
     )(order, place, table)
 
 
-def score_kernel(order_ref, buffer_ref, weighted_ref, col_ref, row_ref, out_ref, slices):
+def score_kernel(order_ref, buffer_ref, w0, w1, w2, w3, col_ref, row_ref, out_ref, slices, weighted_ref):
     del order_ref
+    for at, source in enumerate((w0, w1, w2, w3)):
+
+        @pl.when(pl.program_id(0) == at)
+        def _(source=source):
+            weighted_ref[...] = source[...]
+
     extra = weighted_ref[PARTICLE_ROWS:, :].astype(jnp.float32)
     place = 16.0 * extra[:8] + extra[8:16]
     frac = extra[16:20] + extra[20:24] + extra[24:28]
@@ -282,9 +289,9 @@
                 pl.BlockSpec(
                     (32, None, 4 * CAP, LANES), lambda i, order: (0, order[i], 0, 0)
                 ),
-                pl.BlockSpec(
-                    (None, PARTICLE_ROWS + EXTRA_ROWS, LANES), lambda i, order: (i, 0, 0)
-                ),
+            ]
+            + [pl.BlockSpec((PARTICLE_ROWS + EXTRA_ROWS, LANES), lambda i, order: (0, 0))] * 4
+            + [
                 pl.BlockSpec((8, 2 * LANES, 2 * LANES), lambda i, order: (0, 0, 0)),
                 pl.BlockSpec((None, 8, LANES), lambda i, order: (order[i], 0, 0)),
             ],
@@ -293,12 +300,13 @@
             ),
             scratch_shapes=[
                 pltpu.VMEM((TAKES, LANES), jnp.float32),
+                pltpu.VMEM((PARTICLE_ROWS + EXTRA_ROWS, LANES), jnp.bfloat16),
             ],
         ),
         out_shape=jax.ShapeDtypeStruct((ORI_MAX // 2, PART_DEV, LANES), jnp.float32),
         compiler_params=pltpu.CompilerParams(vmem_limit_bytes=VMEM_BYTES),
         cost_estimate=pl.CostEstimate(flops=8 << 30, bytes_accessed=4 << 20, transcendentals=0),
-    )(order, buffer, weighted, col_phase, row_phase)
+    )(order, buffer, *weighted, col_phase, row_phase)
 
 
 def exchange(values, axes):
@@ -340,7 +348,7 @@
     partial = score(
         (here + turn) % 4,
         buffer,
-        jnp.stack(groups),
+        groups,
         own_part(column_table(), "x"),
         jnp.asarray(row_table()),
     )

time: 149 us -> 148 us (level)
  waiting for transfers between devices: 39.6 us -> 42.7 us
  other arithmetic: 3.27 us -> 1.36 us
    ppermute x3, waiting for transfers between devices: 1.87 us -> 5.4 us  [shards(): lax.ppermute(block, 'x', [((i + k) % 4, i) for i in range(4)])]
    another operation x1 -> x0, other arithmetic: 1.91 us -> none  [shards(): jnp.stack(groups)]
    unnamed x18 -> x16, local copies, waits for them, and re-layouts: 3.08 us -> 2.03 us
  transfers between devices with their start and end apart: 9 -> 9, of which waited for: 5 -> 5; matrix products, arithmetic and copies ran while one was open for 3% -> 2% of each run, Pallas kernels for 1% -> 1%
where the time goes in v6:
time: 148 us; the launch traced here: 147 us
  starting transfers between devices  54.1 us (37%)
  waiting for transfers between devices  42.7 us (29%)
  blocking collectives  23.7 us (16%)
  Pallas kernels  19.5 us (13%)
  local copies, waits for them, and re-layouts  4.58 us (3%)
    all_to_all x3, waiting for transfers between devices, exchange(): return lax.all_to_all(values, axes, split_axis=0, concat_axis=0, tiled=True)  35.8 us
    all_to_all x3, starting transfers between devices, exchange(): return lax.all_to_all(values, axes, split_axis=0, concat_axis=0, tiled=True)  34.6 us
    all_gather x1, blocking collectives, shards(): maps = lax.all_gather(jnp.stack(maps), 'h', axis=0)  23.7 us
    pallas_call x1, Pallas kernels, score(): pl.pallas_call(score_kernel, grid_spec=pltpu.PrefetchScalarGridSpec(num_s...  12.6 us
    ppermute x3, starting transfers between devices, shards(): lax.ppermute(place, 'x', [((i + k) % 4, i) for i in range(4)])  10.5 us
    ppermute x3, starting transfers between devices, shards(): lax.ppermute(block, 'x', [((i + k) % 4, i) for i in range(4)])  8.94 us
    ppermute x3, waiting for transfers between devices, shards(): lax.ppermute(block, 'x', [((i + k) % 4, i) for i in range(4)])  5.4 us
    pallas_call x1, Pallas kernels, pick(): pl.pallas_call(pick_kernel, grid_spec=pltpu.PrefetchScalarGridSpec(num_sc...  4.74 us
  transfers between devices with their start and end apart: 9, of which 5 were waited for; matrix products, arithmetic and copies ran while one was open for 2% of the time, Pallas kernels for 1%

profile of v6, /device:TPU:1, one launch (start us, length us, event | category | flops | bytes accessed | tf_op | source)
XLA Modules:
  0.0 146.8 jit_solution(15902359334603214469)
XLA Ops:
  0.0 0.0 copy-start.2
  0.0 1.0 copy-done.2
  1.0 0.0 copy-start.3
  1.0 0.9 copy-done.3
  2.0 1.4 shard_map.109
  3.4 20.6 %all-to-all-start = ((bf16[128,16,128]{2,1,0:T(8,128)(2,1)}), bf16[128,16,128]{2,1,0:T(8,128)(2,1)S(1)}, u32[]{:S(2)}, u32[]{:S(2)}) async-start(bf16[128,16,128]{2,1,0:T(8,128)(2,1)} %bitcast.8), calls=%async_computation | async-start | bytes 1048576 | tf_op jit(solution)/shard_map/all_to_all | solution.py:313
  24.0 0.7 or_convert_fusion.1
  24.7 0.1 copy.22
  24.8 0.1 reshape.65
  24.9 3.1 %collective-permute-start.2 = (f32[4,4,128]{2,1,0:T(4,128)S(1)}, f32[4,4,128]{2,1,0:T(4,128)S(1)}, u32[]{:S(2)}, u32[]{:S(2)}) collective-permute-start(f32[4,4,128]{2,1,0:T(4,128)S(1)} %reshape.65), channel_id=1, source_target_pairs={{3,0},{0,1},{1,2},{2,3},{7,4},{4,5},{5,6},{6,7},{11,8},{8,9},{9,10... | collective-permute-start | bytes 24584 | tf_op jit(solution)/shard_map/ppermute | solution.py:330
  28.0 4.4 %collective-permute-start.1 = (f32[4,4,128]{2,1,0:T(4,128)S(1)}, f32[4,4,128]{2,1,0:T(4,128)S(1)}, u32[]{:S(2)}, u32[]{:S(2)}) collective-permute-start(f32[4,4,128]{2,1,0:T(4,128)S(1)} %reshape.65), channel_id=1, source_target_pairs={{2,0},{3,1},{0,2},{1,3},{6,4},{7,5},{4,6},{5,7},{10,8},{11,9},{8,1... | collective-permute-start | bytes 24584 | tf_op jit(solution)/shard_map/ppermute | solution.py:330
  32.4 3.1 %collective-permute-start = (f32[4,4,128]{2,1,0:T(4,128)S(1)}, f32[4,4,128]{2,1,0:T(4,128)S(1)}, u32[]{:S(2)}, u32[]{:S(2)}) collective-permute-start(f32[4,4,128]{2,1,0:T(4,128)S(1)} %reshape.65), channel_id=1, source_target_pairs={{1,0},{2,1},{3,2},{0,3},{5,4},{6,5},{7,6},{4,7},{9,8},{10,9},{11,1... | collective-permute-start | bytes 24584 | tf_op jit(solution)/shard_map/ppermute | solution.py:330
  35.5 0.1 stack_reshape.3
  35.6 0.0 collective-permute-done.2
  35.6 0.0 collective-permute-done.1
  35.6 1.5 %collective-permute-done = f32[4,4,128]{2,1,0:T(4,128)S(1)} collective-permute-done((f32[4,4,128]{2,1,0:T(4,128)S(1)}, f32[4,4,128]{2,1,0:T(4,128)S(1)}, u32[]{:S(2)}, u32[]{:S(2)}) %collective-permute-start) | collective-permute-done | bytes 8224 | tf_op jit(solution)/shard_map/ppermute | solution.py:330
  37.1 23.7 %all-gather = f32[16,4,4,128]{3,2,1,0:T(4,128)S(1)} all-gather(f32[4,4,4,128]{3,2,1,0:T(4,128)S(1)} %pad_maximum_fusion), channel_id=2, replica_groups=mesh['y'=4,'h'=4,'l'=4,'c'=2,'x'=4] {'h'}, dimensions={0}, use_global_device_ids=true | all-gather | bytes 163840 | tf_op jit(solution)/shard_map/all_gather | solution.py:332
  60.8 0.0 all-to-all-done
  60.8 0.0 copy-start.7
  60.9 0.0 copy-start.6
  60.9 0.0 copy-start
  60.9 0.0 copy-start.1
  60.9 0.0 copy-start.4
  60.9 4.7 %shard_map.110 = bf16[32,4,4,16,128]{4,3,2,1,0:T(8,128)(2,1)} custom-call(s32[4]{0:T(128)S(1)} %and_select_fusion.order_ref, f32[4,4,4,128]{3,2,1,0:T(4,128)S(1)} %dynamic-slice_bitcast_fusion.5.place_ref, bf16[2048,128]{1,0:T(8,128)(2,1)S(1)} %bitcast.34), custom_call_target="tpu_custom_call" | custom-call | flops 2147483648 | bytes 4194304 | tf_op jit(solution)/shard_map/pallas_call | solution.py:179
  65.6 0.0 copy-start.5
  65.6 10.2 %all-to-all-start.1 = ((bf16[32,256,128]{2,1,0:T(8,128)(2,1)}), bf16[32,256,128]{2,1,0:T(8,128)(2,1)S(1)}, u32[]{:S(2)}, u32[]{:S(2)}) async-start(bf16[32,256,128]{2,1,0:T(8,128)(2,1)} %bitcast.35), calls=%async_computation.1 | async-start | bytes 4194304 | tf_op jit(solution)/shard_map/all_to_all | solution.py:313
  75.9 0.0 copy-done.7
  75.9 0.1 reshape.67
  76.0 0.0 copy-done.6
  76.0 0.1 reshape.74
  76.1 0.0 copy-done
  76.1 0.0 copy-done.1
  76.1 0.0 copy-done.4
  76.1 0.8 shard_map.111
  76.9 0.8 dynamic-slice_bitcast_fusion.1
  77.7 4.4 %collective-permute-start.3 = (bf16[544,128]{1,0:T(8,128)(2,1)}, bf16[544,128]{1,0:T(8,128)(2,1)S(1)}, u32[]{:S(2)}, u32[]{:S(2)}) collective-permute-start(bf16[544,128]{1,0:T(8,128)(2,1)} %get-tuple-element.7), channel_id=1, source_target_pairs={{1,0},{2,1},{3,2},{0,3},{5,4},{6,5},{7,6},{4,7},{9,8},{10,9},{11,1... | collective-permute-start | bytes 417800 | tf_op jit(solution)/shard_map/ppermute | solution.py:347
  82.2 2.0 %collective-permute-start.4 = (bf16[544,128]{1,0:T(8,128)(2,1)}, bf16[544,128]{1,0:T(8,128)(2,1)}, u32[]{:S(2)}, u32[]{:S(2)}) collective-permute-start(bf16[544,128]{1,0:T(8,128)(2,1)} %get-tuple-element.6), channel_id=1, source_target_pairs={{2,0},{3,1},{0,2},{1,3},{6,4},{7,5},{4,6},{5,7},{10,8},{11,9},{8,1... | collective-permute-start | bytes 417800 | tf_op jit(solution)/shard_map/ppermute | solution.py:347
  84.2 2.5 %collective-permute-start.5 = (bf16[544,128]{1,0:T(8,128)(2,1)}, bf16[544,128]{1,0:T(8,128)(2,1)}, u32[]{:S(2)}, u32[]{:S(2)}) collective-permute-start(bf16[544,128]{1,0:T(8,128)(2,1)} %get-tuple-element.5), channel_id=1, source_target_pairs={{3,0},{0,1},{1,2},{2,3},{7,4},{4,5},{5,6},{6,7},{11,8},{8,9},{9,10... | collective-permute-start | bytes 417800 | tf_op jit(solution)/shard_map/ppermute | solution.py:347
  87.3 1.3 dynamic-slice_bitcast_fusion.col_ref
  88.6 0.0 collective-permute-done.3.w1
  88.7 2.0 %collective-permute-done.4.w2 = bf16[544,128]{1,0:T(8,128)(2,1)} collective-permute-done((bf16[544,128]{1,0:T(8,128)(2,1)}, bf16[544,128]{1,0:T(8,128)(2,1)}, u32[]{:S(2)}, u32[]{:S(2)}) %collective-permute-start.4) | collective-permute-done | bytes 139296 | tf_op jit(solution)/shard_map/ppermute | solution.py:347
  90.6 3.4 %collective-permute-done.5.w3 = bf16[544,128]{1,0:T(8,128)(2,1)} collective-permute-done((bf16[544,128]{1,0:T(8,128)(2,1)}, bf16[544,128]{1,0:T(8,128)(2,1)}, u32[]{:S(2)}, u32[]{:S(2)}) %collective-permute-start.5) | collective-permute-done | bytes 139296 | tf_op jit(solution)/shard_map/ppermute | solution.py:347
  94.0 31.6 %all-to-all-done.1 = bf16[32,256,128]{2,1,0:T(8,128)(2,1)S(1)} async-done(((bf16[32,256,128]{2,1,0:T(8,128)(2,1)}), bf16[32,256,128]{2,1,0:T(8,128)(2,1)S(1)}, u32[]{:S(2)}, u32[]{:S(2)}) %all-to-all-start.1) | async-done | bytes 2097184 | tf_op jit(solution)/shard_map/all_to_all | solution.py:313
  125.6 0.0 copy-done.5
  125.6 12.6 %shard_map.112 = f32[4,8,128]{2,1,0:T(8,128)} custom-call(s32[4]{0:T(128)S(1)} %and_select_fusion.order_ref, bf16[32,4,64,128]{3,2,1,0:T(8,128)(2,1)S(1)} %bitcast.33, bf16[544,128]{1,0:T(8,128)(2,1)S(1)} %get-tuple-element.8.w0, bf16[544,128]{1,0:T(8,128)(2,1)S(1)} %collective-permute-done.3.w1, bf16[544,128]{1,0:T(8,128)(2,1)} %collective-permute-done.4.w2, ...), custom_call_target="tpu_custom_call" | custom-call | flops 8589934592 | bytes 4194304 | tf_op jit(solution)/shard_map/pallas_call | solution.py:283
  138.2 3.8 %all-to-all-start.2 = ((f32[4,8,128]{2,1,0:T(8,128)}), f32[4,8,128]{2,1,0:T(8,128)S(1)}, u32[]{:S(2)}, u32[]{:S(2)}) async-start(f32[4,8,128]{2,1,0:T(8,128)} %shard_map.112), calls=%async_computation.2 | async-start | bytes 32768 | tf_op jit(solution)/shard_map/all_to_all | solution.py:313
  142.0 4.2 %all-to-all-done.2 = f32[4,8,128]{2,1,0:T(8,128)S(1)} async-done(((f32[4,8,128]{2,1,0:T(8,128)}), f32[4,8,128]{2,1,0:T(8,128)S(1)}, u32[]{:S(2)}, u32[]{:S(2)}) %all-to-all-start.2) | async-done | bytes 16416 | tf_op jit(solution)/shard_map/all_to_all | solution.py:313
  146.2 0.6 broadcast_select_fusion
  (8 shorter events, 0.1 us)
Async XLA Ops:
  0.0 1.0 copy-start.2
  1.0 0.9 copy-start.3
  3.4 57.4 %all-to-all-start = ((bf16[128,16,128]{2,1,0:T(8,128)(2,1)}), bf16[128,16,128]{2,1,0:T(8,128)(2,1)S(1)}, u32[]{:S(2)}, u32[]{:S(2)}) async-start(bf16[128,16,128]{2,1,0:T(8,128)(2,1)} %bitcast.8), calls=%async_computation | async-start | bytes 1048576 | tf_op jit(solution)/shard_map/all_to_all | solution.py:313
  24.9 10.7 %collective-permute-start.2 = (f32[4,4,128]{2,1,0:T(4,128)S(1)}, f32[4,4,128]{2,1,0:T(4,128)S(1)}, u32[]{:S(2)}, u32[]{:S(2)}) collective-permute-start(f32[4,4,128]{2,1,0:T(4,128)S(1)} %reshape.65), channel_id=1, source_target_pairs={{3,0},{0,1},{1,2},{2,3},{7,4},{4,5},{5,6},{6,7},{11,8},{8,9},{9,10... | collective-permute-start | bytes 24584 | tf_op jit(solution)/shard_map/ppermute | solution.py:330
  28.0 7.6 %collective-permute-start.1 = (f32[4,4,128]{2,1,0:T(4,128)S(1)}, f32[4,4,128]{2,1,0:T(4,128)S(1)}, u32[]{:S(2)}, u32[]{:S(2)}) collective-permute-start(f32[4,4,128]{2,1,0:T(4,128)S(1)} %reshape.65), channel_id=1, source_target_pairs={{2,0},{3,1},{0,2},{1,3},{6,4},{7,5},{4,6},{5,7},{10,8},{11,9},{8,1... | collective-permute-start | bytes 24584 | tf_op jit(solution)/shard_map/ppermute | solution.py:330
  32.4 4.7 %collective-permute-start = (f32[4,4,128]{2,1,0:T(4,128)S(1)}, f32[4,4,128]{2,1,0:T(4,128)S(1)}, u32[]{:S(2)}, u32[]{:S(2)}) collective-permute-start(f32[4,4,128]{2,1,0:T(4,128)S(1)} %reshape.65), channel_id=1, source_target_pairs={{1,0},{2,1},{3,2},{0,3},{5,4},{6,5},{7,6},{4,7},{9,8},{10,9},{11,1... | collective-permute-start | bytes 24584 | tf_op jit(solution)/shard_map/ppermute | solution.py:330
  60.8 15.1 %copy-start.7 = (f32[1,8,64]{2,1,0:T(8,128)S(1)}, f32[1,8,64]{2,1,0:T(8,128)}, u32[]{:S(2)}) copy-start(f32[1,8,64]{2,1,0:T(8,128)} %param.14) | copy-start | bytes 6148
  60.9 15.2 %copy-start.6 = (s32[2,1,8,64]{3,2,1,0:T(8,128)S(1)}, s32[2,1,8,64]{3,2,1,0:T(8,128)}, u32[]{:S(2)}) copy-start(s32[2,1,8,64]{3,2,1,0:T(8,128)} %param.13) | copy-start | bytes 12292
  60.9 15.2 %copy-start = (bf16[8,64,512]{2,1,0:T(8,128)(2,1)S(1)}, bf16[8,64,512]{2,1,0:T(8,128)(2,1)}, u32[]{:S(2)}) copy-start(bf16[8,64,512]{2,1,0:T(8,128)(2,1)} %spectra_ref.1) | copy-start | bytes 1572868
  60.9 15.2 %copy-start.1 = (bf16[16,64,256]{2,1,0:T(8,128)(2,1)S(1)}, bf16[16,64,256]{2,1,0:T(8,128)(2,1)}, u32[]{:S(2)}) copy-start(bf16[16,64,256]{2,1,0:T(8,128)(2,1)} %ctf_ref.1) | copy-start | bytes 1572868
  60.9 15.2 %copy-start.4 = (s32[8]{0:T(128)S(1)}, s32[8]{0:T(128)}, u32[]{:S(2)}) copy-start(s32[8]{0:T(128)} %class_ref.1) | copy-start | bytes 100
  65.6 60.0 %copy-start.5 = (f32[4,8,128]{2,1,0:T(8,128)S(1)}, f32[4,8,128]{2,1,0:T(8,128)}, u32[]{:S(2)}) copy-start(f32[4,8,128]{2,1,0:T(8,128)} %constant.109.clone.row_ref) | copy-start | bytes 49156
  65.6 60.0 %all-to-all-start.1 = ((bf16[32,256,128]{2,1,0:T(8,128)(2,1)}), bf16[32,256,128]{2,1,0:T(8,128)(2,1)S(1)}, u32[]{:S(2)}, u32[]{:S(2)}) async-start(bf16[32,256,128]{2,1,0:T(8,128)(2,1)} %bitcast.35), calls=%async_computation.1 | async-start | bytes 4194304 | tf_op jit(solution)/shard_map/all_to_all | solution.py:313
  77.7 10.9 %collective-permute-start.3 = (bf16[544,128]{1,0:T(8,128)(2,1)}, bf16[544,128]{1,0:T(8,128)(2,1)S(1)}, u32[]{:S(2)}, u32[]{:S(2)}) collective-permute-start(bf16[544,128]{1,0:T(8,128)(2,1)} %get-tuple-element.7), channel_id=1, source_target_pairs={{1,0},{2,1},{3,2},{0,3},{5,4},{6,5},{7,6},{4,7},{9,8},{10,9},{11,1... | collective-permute-start | bytes 417800 | tf_op jit(solution)/shard_map/ppermute | solution.py:347
  82.2 8.4 %collective-permute-start.4 = (bf16[544,128]{1,0:T(8,128)(2,1)}, bf16[544,128]{1,0:T(8,128)(2,1)}, u32[]{:S(2)}, u32[]{:S(2)}) collective-permute-start(bf16[544,128]{1,0:T(8,128)(2,1)} %get-tuple-element.6), channel_id=1, source_target_pairs={{2,0},{3,1},{0,2},{1,3},{6,4},{7,5},{4,6},{5,7},{10,8},{11,9},{8,1... | collective-permute-start | bytes 417800 | tf_op jit(solution)/shard_map/ppermute | solution.py:347
  84.2 9.8 %collective-permute-start.5 = (bf16[544,128]{1,0:T(8,128)(2,1)}, bf16[544,128]{1,0:T(8,128)(2,1)}, u32[]{:S(2)}, u32[]{:S(2)}) collective-permute-start(bf16[544,128]{1,0:T(8,128)(2,1)} %get-tuple-element.5), channel_id=1, source_target_pairs={{3,0},{0,1},{1,2},{2,3},{7,4},{4,5},{5,6},{6,7},{11,8},{8,9},{9,10... | collective-permute-start | bytes 417800 | tf_op jit(solution)/shard_map/ppermute | solution.py:347
  138.2 8.0 %all-to-all-start.2 = ((f32[4,8,128]{2,1,0:T(8,128)}), f32[4,8,128]{2,1,0:T(8,128)S(1)}, u32[]{:S(2)}, u32[]{:S(2)}) async-start(f32[4,8,128]{2,1,0:T(8,128)} %shard_map.112), calls=%async_computation.2 | async-start | bytes 32768 | tf_op jit(solution)/shard_map/all_to_all | solution.py:313

commit v7 on v6

--- a/solution.py
+++ b/solution.py
@@ -183,7 +183,7 @@
             grid=(N_GRP,),
             in_specs=[
                 pl.BlockSpec((4, None, 4, LANES), lambda i, order: (0, i, 0, 0)),
-                pl.BlockSpec((4 * SLAB_ROWS, LANES), lambda i, order: (0, 0)),
+                pl.BlockSpec(memory_space=pltpu.VMEM),
             ],
             out_specs=pl.BlockSpec(
                 (32, None, 4, CAP, LANES), lambda i, order: (0, order[i], 0, 0, 0)
@@ -203,7 +203,6 @@
 
 
 def score_kernel(order_ref, buffer_ref, w0, w1, w2, w3, col_ref, row_ref, out_ref, slices, weighted_ref):
-    del order_ref
     for at, source in enumerate((w0, w1, w2, w3)):
 
         @pl.when(pl.program_id(0) == at)
@@ -225,7 +224,7 @@
                 share,
             )
         )
-    rows = buffer_ref[...].reshape(SLOTS, LANES)
+    rows = buffer_ref[:, order_ref[pl.program_id(0)]].reshape(SLOTS, LANES)
     mixed = None
     for start in range(0, SLOTS, MIX_STEP):
         blocks = [
@@ -286,13 +285,11 @@
             num_scalar_prefetch=1,
             grid=(N_GRP,),
             in_specs=[
-                pl.BlockSpec(
-                    (32, None, 4 * CAP, LANES), lambda i, order: (0, order[i], 0, 0)
-                ),
+                pl.BlockSpec(memory_space=pltpu.VMEM),
             ]
-            + [pl.BlockSpec((PARTICLE_ROWS + EXTRA_ROWS, LANES), lambda i, order: (0, 0))] * 4
+            + [pl.BlockSpec(memory_space=pltpu.VMEM)] * 4
             + [
-                pl.BlockSpec((8, 2 * LANES, 2 * LANES), lambda i, order: (0, 0, 0)),
+                pl.BlockSpec(memory_space=pltpu.VMEM),
                 pl.BlockSpec((None, 8, LANES), lambda i, order: (order[i], 0, 0)),
             ],
             out_specs=pl.BlockSpec(

time: 148 us -> 147 us (level)
  no operation moved by 1% of the time
where the time goes in v7:
time: 147 us
  starting transfers between devices  54.1 us (37%)
  waiting for transfers between devices  42.7 us (29%)
  blocking collectives  23.7 us (16%)
  Pallas kernels  19.4 us (13%)
  local copies, waits for them, and re-layouts  4.58 us (3%)
    all_to_all x3, waiting for transfers between devices, exchange(): return lax.all_to_all(values, axes, split_axis=0, concat_axis=0, tiled=True)  35.8 us
    all_to_all x3, starting transfers between devices, exchange(): return lax.all_to_all(values, axes, split_axis=0, concat_axis=0, tiled=True)  34.6 us
    all_gather x1, blocking collectives, shards(): maps = lax.all_gather(jnp.stack(maps), 'h', axis=0)  23.7 us
    pallas_call x1, Pallas kernels, score(): pl.pallas_call(score_kernel, grid_spec=pltpu.PrefetchScalarGridSpec(num_s...  12.5 us
    ppermute x3, starting transfers between devices, shards(): lax.ppermute(place, 'x', [((i + k) % 4, i) for i in range(4)])  10.5 us
    ppermute x3, starting transfers between devices, shards(): lax.ppermute(block, 'x', [((i + k) % 4, i) for i in range(4)])  8.94 us
    ppermute x3, waiting for transfers between devices, shards(): lax.ppermute(block, 'x', [((i + k) % 4, i) for i in range(4)])  5.4 us
    pallas_call x1, Pallas kernels, pick(): pl.pallas_call(pick_kernel, grid_spec=pltpu.PrefetchScalarGridSpec(num_sc...  4.74 us
  transfers between devices with their start and end apart: 9, of which 5 were waited for; matrix products, arithmetic and copies ran while one was open for 2% of the time, Pallas kernels for 1%

profile of v7, /device:TPU:1, one launch (start us, length us, event | category | flops | bytes accessed | tf_op | source)
XLA Modules:
  0.0 146.8 jit_solution(13760951107108841652)
XLA Ops:
  0.0 0.0 copy-start.2
  0.0 1.0 copy-done.2
  1.0 0.0 copy-start.3
  1.0 0.9 copy-done.3
  2.0 1.4 shard_map.109
  3.4 20.6 %all-to-all-start = ((bf16[128,16,128]{2,1,0:T(8,128)(2,1)}), bf16[128,16,128]{2,1,0:T(8,128)(2,1)S(1)}, u32[]{:S(2)}, u32[]{:S(2)}) async-start(bf16[128,16,128]{2,1,0:T(8,128)(2,1)} %bitcast.8), calls=%async_computation | async-start | bytes 1048576 | tf_op jit(solution)/shard_map/all_to_all | solution.py:310
  24.0 0.7 or_convert_fusion.1
  24.7 0.1 copy.22
  24.8 0.1 reshape.65
  24.9 3.1 %collective-permute-start.2 = (f32[4,4,128]{2,1,0:T(4,128)S(1)}, f32[4,4,128]{2,1,0:T(4,128)S(1)}, u32[]{:S(2)}, u32[]{:S(2)}) collective-permute-start(f32[4,4,128]{2,1,0:T(4,128)S(1)} %reshape.65), channel_id=1, source_target_pairs={{3,0},{0,1},{1,2},{2,3},{7,4},{4,5},{5,6},{6,7},{11,8},{8,9},{9,10... | collective-permute-start | bytes 24584 | tf_op jit(solution)/shard_map/ppermute | solution.py:327
  28.0 4.4 %collective-permute-start.1 = (f32[4,4,128]{2,1,0:T(4,128)S(1)}, f32[4,4,128]{2,1,0:T(4,128)S(1)}, u32[]{:S(2)}, u32[]{:S(2)}) collective-permute-start(f32[4,4,128]{2,1,0:T(4,128)S(1)} %reshape.65), channel_id=1, source_target_pairs={{2,0},{3,1},{0,2},{1,3},{6,4},{7,5},{4,6},{5,7},{10,8},{11,9},{8,1... | collective-permute-start | bytes 24584 | tf_op jit(solution)/shard_map/ppermute | solution.py:327
  32.4 3.1 %collective-permute-start = (f32[4,4,128]{2,1,0:T(4,128)S(1)}, f32[4,4,128]{2,1,0:T(4,128)S(1)}, u32[]{:S(2)}, u32[]{:S(2)}) collective-permute-start(f32[4,4,128]{2,1,0:T(4,128)S(1)} %reshape.65), channel_id=1, source_target_pairs={{1,0},{2,1},{3,2},{0,3},{5,4},{6,5},{7,6},{4,7},{9,8},{10,9},{11,1... | collective-permute-start | bytes 24584 | tf_op jit(solution)/shard_map/ppermute | solution.py:327
  35.5 0.1 stack_reshape.3
  35.6 0.0 collective-permute-done.2
  35.6 0.0 collective-permute-done.1
  35.6 1.5 %collective-permute-done = f32[4,4,128]{2,1,0:T(4,128)S(1)} collective-permute-done((f32[4,4,128]{2,1,0:T(4,128)S(1)}, f32[4,4,128]{2,1,0:T(4,128)S(1)}, u32[]{:S(2)}, u32[]{:S(2)}) %collective-permute-start) | collective-permute-done | bytes 8224 | tf_op jit(solution)/shard_map/ppermute | solution.py:327
  37.1 23.7 %all-gather = f32[16,4,4,128]{3,2,1,0:T(4,128)S(1)} all-gather(f32[4,4,4,128]{3,2,1,0:T(4,128)S(1)} %pad_maximum_fusion), channel_id=2, replica_groups=mesh['y'=4,'h'=4,'l'=4,'c'=2,'x'=4] {'h'}, dimensions={0}, use_global_device_ids=true | all-gather | bytes 163840 | tf_op jit(solution)/shard_map/all_gather | solution.py:329
  60.8 0.0 all-to-all-done
  60.8 0.0 copy-start.7
  60.9 0.0 copy-start.6
  60.9 0.0 copy-start
  60.9 0.0 copy-start.1
  60.9 0.0 copy-start.4
  60.9 4.7 %shard_map.110 = bf16[32,4,4,16,128]{4,3,2,1,0:T(8,128)(2,1)} custom-call(s32[4]{0:T(128)S(1)} %and_select_fusion.order_ref, f32[4,4,4,128]{3,2,1,0:T(4,128)S(1)} %dynamic-slice_bitcast_fusion.5.place_ref, bf16[2048,128]{1,0:T(8,128)(2,1)S(1)} %bitcast.34), custom_call_target="tpu_custom_call" | custom-call | flops 2147483648 | bytes 4194304 | tf_op jit(solution)/shard_map/pallas_call | solution.py:179
  65.6 0.0 copy-start.5
  65.6 10.2 %all-to-all-start.1 = ((bf16[32,256,128]{2,1,0:T(8,128)(2,1)}), bf16[32,256,128]{2,1,0:T(8,128)(2,1)S(1)}, u32[]{:S(2)}, u32[]{:S(2)}) async-start(bf16[32,256,128]{2,1,0:T(8,128)(2,1)} %bitcast.35), calls=%async_computation.1 | async-start | bytes 4194304 | tf_op jit(solution)/shard_map/all_to_all | solution.py:310
  75.9 0.0 copy-done.7
  75.9 0.1 reshape.67
  76.0 0.0 copy-done.6
  76.0 0.1 reshape.74
  76.1 0.0 copy-done
  76.1 0.0 copy-done.1
  76.1 0.0 copy-done.4
  76.1 0.8 shard_map.111
  76.9 0.8 dynamic-slice_bitcast_fusion.1
  77.7 4.4 %collective-permute-start.3 = (bf16[544,128]{1,0:T(8,128)(2,1)}, bf16[544,128]{1,0:T(8,128)(2,1)S(1)}, u32[]{:S(2)}, u32[]{:S(2)}) collective-permute-start(bf16[544,128]{1,0:T(8,128)(2,1)} %get-tuple-element.7), channel_id=1, source_target_pairs={{1,0},{2,1},{3,2},{0,3},{5,4},{6,5},{7,6},{4,7},{9,8},{10,9},{11,1... | collective-permute-start | bytes 417800 | tf_op jit(solution)/shard_map/ppermute | solution.py:344
  82.2 2.0 %collective-permute-start.4 = (bf16[544,128]{1,0:T(8,128)(2,1)}, bf16[544,128]{1,0:T(8,128)(2,1)}, u32[]{:S(2)}, u32[]{:S(2)}) collective-permute-start(bf16[544,128]{1,0:T(8,128)(2,1)} %get-tuple-element.6), channel_id=1, source_target_pairs={{2,0},{3,1},{0,2},{1,3},{6,4},{7,5},{4,6},{5,7},{10,8},{11,9},{8,1... | collective-permute-start | bytes 417800 | tf_op jit(solution)/shard_map/ppermute | solution.py:344
  84.2 2.5 %collective-permute-start.5 = (bf16[544,128]{1,0:T(8,128)(2,1)}, bf16[544,128]{1,0:T(8,128)(2,1)}, u32[]{:S(2)}, u32[]{:S(2)}) collective-permute-start(bf16[544,128]{1,0:T(8,128)(2,1)} %get-tuple-element.5), channel_id=1, source_target_pairs={{3,0},{0,1},{1,2},{2,3},{7,4},{4,5},{5,6},{6,7},{11,8},{8,9},{9,10... | collective-permute-start | bytes 417800 | tf_op jit(solution)/shard_map/ppermute | solution.py:344
  87.3 1.3 dynamic-slice_bitcast_fusion.col_ref
  88.6 0.0 collective-permute-done.3.w1
  88.7 2.0 %collective-permute-done.4.w2 = bf16[544,128]{1,0:T(8,128)(2,1)} collective-permute-done((bf16[544,128]{1,0:T(8,128)(2,1)}, bf16[544,128]{1,0:T(8,128)(2,1)}, u32[]{:S(2)}, u32[]{:S(2)}) %collective-permute-start.4) | collective-permute-done | bytes 139296 | tf_op jit(solution)/shard_map/ppermute | solution.py:344
  90.6 3.4 %collective-permute-done.5.w3 = bf16[544,128]{1,0:T(8,128)(2,1)} collective-permute-done((bf16[544,128]{1,0:T(8,128)(2,1)}, bf16[544,128]{1,0:T(8,128)(2,1)}, u32[]{:S(2)}, u32[]{:S(2)}) %collective-permute-start.5) | collective-permute-done | bytes 139296 | tf_op jit(solution)/shard_map/ppermute | solution.py:344
  94.0 31.6 %all-to-all-done.1 = bf16[32,256,128]{2,1,0:T(8,128)(2,1)S(1)} async-done(((bf16[32,256,128]{2,1,0:T(8,128)(2,1)}), bf16[32,256,128]{2,1,0:T(8,128)(2,1)S(1)}, u32[]{:S(2)}, u32[]{:S(2)}) %all-to-all-start.1) | async-done | bytes 2097184 | tf_op jit(solution)/shard_map/all_to_all | solution.py:310
  125.6 0.0 copy-done.5
  125.6 12.5 %shard_map.112 = f32[4,8,128]{2,1,0:T(8,128)} custom-call(s32[4]{0:T(128)S(1)} %and_select_fusion.order_ref, bf16[32,4,64,128]{3,2,1,0:T(8,128)(2,1)S(1)} %bitcast.33, bf16[544,128]{1,0:T(8,128)(2,1)S(1)} %get-tuple-element.8.w0, bf16[544,128]{1,0:T(8,128)(2,1)S(1)} %collective-permute-done.3.w1, bf16[544,128]{1,0:T(8,128)(2,1)} %collective-permute-done.4.w2, ...), custom_call_target="tpu_custom_call" | custom-call | flops 8589934592 | bytes 4194304 | tf_op jit(solution)/shard_map/pallas_call | solution.py:282
  138.1 3.8 %all-to-all-start.2 = ((f32[4,8,128]{2,1,0:T(8,128)}), f32[4,8,128]{2,1,0:T(8,128)S(1)}, u32[]{:S(2)}, u32[]{:S(2)}) async-start(f32[4,8,128]{2,1,0:T(8,128)} %shard_map.112), calls=%async_computation.2 | async-start | bytes 32768 | tf_op jit(solution)/shard_map/all_to_all | solution.py:310
  141.9 4.2 %all-to-all-done.2 = f32[4,8,128]{2,1,0:T(8,128)S(1)} async-done(((f32[4,8,128]{2,1,0:T(8,128)}), f32[4,8,128]{2,1,0:T(8,128)S(1)}, u32[]{:S(2)}, u32[]{:S(2)}) %all-to-all-start.2) | async-done | bytes 16416 | tf_op jit(solution)/shard_map/all_to_all | solution.py:310
  146.2 0.6 broadcast_select_fusion
  (8 shorter events, 0.1 us)
Async XLA Ops:
  0.0 1.0 copy-start.2
  1.0 0.9 copy-start.3
  3.4 57.4 %all-to-all-start = ((bf16[128,16,128]{2,1,0:T(8,128)(2,1)}), bf16[128,16,128]{2,1,0:T(8,128)(2,1)S(1)}, u32[]{:S(2)}, u32[]{:S(2)}) async-start(bf16[128,16,128]{2,1,0:T(8,128)(2,1)} %bitcast.8), calls=%async_computation | async-start | bytes 1048576 | tf_op jit(solution)/shard_map/all_to_all | solution.py:310
  24.9 10.7 %collective-permute-start.2 = (f32[4,4,128]{2,1,0:T(4,128)S(1)}, f32[4,4,128]{2,1,0:T(4,128)S(1)}, u32[]{:S(2)}, u32[]{:S(2)}) collective-permute-start(f32[4,4,128]{2,1,0:T(4,128)S(1)} %reshape.65), channel_id=1, source_target_pairs={{3,0},{0,1},{1,2},{2,3},{7,4},{4,5},{5,6},{6,7},{11,8},{8,9},{9,10... | collective-permute-start | bytes 24584 | tf_op jit(solution)/shard_map/ppermute | solution.py:327
  28.0 7.6 %collective-permute-start.1 = (f32[4,4,128]{2,1,0:T(4,128)S(1)}, f32[4,4,128]{2,1,0:T(4,128)S(1)}, u32[]{:S(2)}, u32[]{:S(2)}) collective-permute-start(f32[4,4,128]{2,1,0:T(4,128)S(1)} %reshape.65), channel_id=1, source_target_pairs={{2,0},{3,1},{0,2},{1,3},{6,4},{7,5},{4,6},{5,7},{10,8},{11,9},{8,1... | collective-permute-start | bytes 24584 | tf_op jit(solution)/shard_map/ppermute | solution.py:327
  32.4 4.7 %collective-permute-start = (f32[4,4,128]{2,1,0:T(4,128)S(1)}, f32[4,4,128]{2,1,0:T(4,128)S(1)}, u32[]{:S(2)}, u32[]{:S(2)}) collective-permute-start(f32[4,4,128]{2,1,0:T(4,128)S(1)} %reshape.65), channel_id=1, source_target_pairs={{1,0},{2,1},{3,2},{0,3},{5,4},{6,5},{7,6},{4,7},{9,8},{10,9},{11,1... | collective-permute-start | bytes 24584 | tf_op jit(solution)/shard_map/ppermute | solution.py:327
  60.8 15.1 %copy-start.7 = (f32[1,8,64]{2,1,0:T(8,128)S(1)}, f32[1,8,64]{2,1,0:T(8,128)}, u32[]{:S(2)}) copy-start(f32[1,8,64]{2,1,0:T(8,128)} %param.14) | copy-start | bytes 6148
  60.9 15.2 %copy-start.6 = (s32[2,1,8,64]{3,2,1,0:T(8,128)S(1)}, s32[2,1,8,64]{3,2,1,0:T(8,128)}, u32[]{:S(2)}) copy-start(s32[2,1,8,64]{3,2,1,0:T(8,128)} %param.13) | copy-start | bytes 12292
  60.9 15.2 %copy-start = (bf16[8,64,512]{2,1,0:T(8,128)(2,1)S(1)}, bf16[8,64,512]{2,1,0:T(8,128)(2,1)}, u32[]{:S(2)}) copy-start(bf16[8,64,512]{2,1,0:T(8,128)(2,1)} %spectra_ref.1) | copy-start | bytes 1572868
  60.9 15.2 %copy-start.1 = (bf16[16,64,256]{2,1,0:T(8,128)(2,1)S(1)}, bf16[16,64,256]{2,1,0:T(8,128)(2,1)}, u32[]{:S(2)}) copy-start(bf16[16,64,256]{2,1,0:T(8,128)(2,1)} %ctf_ref.1) | copy-start | bytes 1572868
  60.9 15.2 %copy-start.4 = (s32[8]{0:T(128)S(1)}, s32[8]{0:T(128)}, u32[]{:S(2)}) copy-start(s32[8]{0:T(128)} %class_ref.1) | copy-start | bytes 100
  65.6 60.0 %copy-start.5 = (f32[4,8,128]{2,1,0:T(8,128)S(1)}, f32[4,8,128]{2,1,0:T(8,128)}, u32[]{:S(2)}) copy-start(f32[4,8,128]{2,1,0:T(8,128)} %constant.109.clone.row_ref) | copy-start | bytes 49156
  65.6 60.0 %all-to-all-start.1 = ((bf16[32,256,128]{2,1,0:T(8,128)(2,1)}), bf16[32,256,128]{2,1,0:T(8,128)(2,1)S(1)}, u32[]{:S(2)}, u32[]{:S(2)}) async-start(bf16[32,256,128]{2,1,0:T(8,128)(2,1)} %bitcast.35), calls=%async_computation.1 | async-start | bytes 4194304 | tf_op jit(solution)/shard_map/all_to_all | solution.py:310
  77.7 10.9 %collective-permute-start.3 = (bf16[544,128]{1,0:T(8,128)(2,1)}, bf16[544,128]{1,0:T(8,128)(2,1)S(1)}, u32[]{:S(2)}, u32[]{:S(2)}) collective-permute-start(bf16[544,128]{1,0:T(8,128)(2,1)} %get-tuple-element.7), channel_id=1, source_target_pairs={{1,0},{2,1},{3,2},{0,3},{5,4},{6,5},{7,6},{4,7},{9,8},{10,9},{11,1... | collective-permute-start | bytes 417800 | tf_op jit(solution)/shard_map/ppermute | solution.py:344
  82.2 8.4 %collective-permute-start.4 = (bf16[544,128]{1,0:T(8,128)(2,1)}, bf16[544,128]{1,0:T(8,128)(2,1)}, u32[]{:S(2)}, u32[]{:S(2)}) collective-permute-start(bf16[544,128]{1,0:T(8,128)(2,1)} %get-tuple-element.6), channel_id=1, source_target_pairs={{2,0},{3,1},{0,2},{1,3},{6,4},{7,5},{4,6},{5,7},{10,8},{11,9},{8,1... | collective-permute-start | bytes 417800 | tf_op jit(solution)/shard_map/ppermute | solution.py:344
  84.2 9.8 %collective-permute-start.5 = (bf16[544,128]{1,0:T(8,128)(2,1)}, bf16[544,128]{1,0:T(8,128)(2,1)}, u32[]{:S(2)}, u32[]{:S(2)}) collective-permute-start(bf16[544,128]{1,0:T(8,128)(2,1)} %get-tuple-element.5), channel_id=1, source_target_pairs={{3,0},{0,1},{1,2},{2,3},{7,4},{4,5},{5,6},{6,7},{11,8},{8,9},{9,10... | collective-permute-start | bytes 417800 | tf_op jit(solution)/shard_map/ppermute | solution.py:344
  138.1 8.0 %all-to-all-start.2 = ((f32[4,8,128]{2,1,0:T(8,128)}), f32[4,8,128]{2,1,0:T(8,128)S(1)}, u32[]{:S(2)}, u32[]{:S(2)}) async-start(f32[4,8,128]{2,1,0:T(8,128)} %shard_map.112), calls=%async_computation.2 | async-start | bytes 32768 | tf_op jit(solution)/shard_map/all_to_all | solution.py:310

commit v8 on v7

--- a/solution.py
+++ b/solution.py
@@ -323,12 +323,9 @@
     place = ((wanted & 1) << 8) | (wanted & (NF - 2)) | (wanted >> 8)
     place = place.astype(jnp.float32).reshape(4, 4, 8, CAP).transpose(1, 0, 2, 3)
     place = place.reshape(4, 4, LANES)
-    maps = [place] + [
-        lax.ppermute(place, "x", [((i + k) % 4, i) for i in range(4)]) for k in range(1, 4)
-    ]
-    maps = lax.all_gather(jnp.stack(maps), "h", axis=0)
+    maps = lax.all_gather(lax.all_gather(place, "x", axis=0), "h", axis=0)
     maps = lax.dynamic_index_in_dim(maps, lax.axis_index("h"), 2, keepdims=False)
-    outgoing = pick((here + turn) % 4, maps, table)
+    outgoing = pick(turn, maps, table)
 
     slot = interp_index.reshape(2, TAKES)
     slab = slot >> 4

time: 147 us -> 147 us (level)
  blocking collectives: 23.7 us -> 35.9 us
  starting transfers between devices: 54.1 us -> 43.6 us
  waiting for transfers between devices: 42.7 us -> 41 us
    all_gather x1 -> x2, blocking collectives: 23.7 us -> 35.9 us  [shards(): maps = lax.all_gather(lax.all_gather(place, 'x', axis=0), 'h', axis=0)]
    ppermute x3 -> x0, starting transfers between devices: 10.5 us -> none  [shards(): lax.ppermute(place, 'x', [((i + k) % 4, i) for i in range(4)])]
    ppermute x3 -> x0, waiting for transfers between devices: 1.49 us -> none  [shards(): lax.ppermute(place, 'x', [((i + k) % 4, i) for i in range(4)])]
  transfers between devices with their start and end apart: 9 -> 6, of which waited for: 5 -> 4; matrix products, arithmetic and copies ran while one was open for 2% -> 2% of each run, Pallas kernels for 1% -> 1%
where the time goes in v8:
time: 147 us; the launch traced here: 146 us
  starting transfers between devices  43.6 us (30%)
  waiting for transfers between devices  41 us (28%)
  blocking collectives  35.9 us (24%)
  Pallas kernels  19.3 us (13%)
  local copies, waits for them, and re-layouts  4.49 us (3%)
    all_to_all x3, waiting for transfers between devices, exchange(): return lax.all_to_all(values, axes, split_axis=0, concat_axis=0, tiled=True)  36.1 us
    all_gather x2, blocking collectives, shards(): maps = lax.all_gather(lax.all_gather(place, 'x', axis=0), 'h', axis=0)  35.9 us
    all_to_all x3, starting transfers between devices, exchange(): return lax.all_to_all(values, axes, split_axis=0, concat_axis=0, tiled=True)  34.5 us
    pallas_call x1, Pallas kernels, score(): pl.pallas_call(score_kernel, grid_spec=pltpu.PrefetchScalarGridSpec(num_s...  12.4 us
    ppermute x3, starting transfers between devices, shards(): lax.ppermute(block, 'x', [((i + k) % 4, i) for i in range(4)])  9.14 us
    ppermute x3, waiting for transfers between devices, shards(): lax.ppermute(block, 'x', [((i + k) % 4, i) for i in range(4)])  4.91 us
    pallas_call x1, Pallas kernels, pick(): pl.pallas_call(pick_kernel, grid_spec=pltpu.PrefetchScalarGridSpec(num_sc...  4.71 us
  transfers between devices with their start and end apart: 6, of which 4 were waited for; matrix products, arithmetic and copies ran while one was open for 2% of the time, Pallas kernels for 1%

profile of v8, /device:TPU:1, one launch (start us, length us, event | category | flops | bytes accessed | tf_op | source)
XLA Modules:
  0.0 146.5 jit_solution(6000438657616239500)
XLA Ops:
  0.0 0.0 copy-start.2
  0.0 1.0 copy-done.2
  1.0 0.0 copy-start.3
  1.0 0.9 copy-done.3
  2.0 1.4 shard_map.109
  3.4 20.6 %all-to-all-start = ((bf16[128,16,128]{2,1,0:T(8,128)(2,1)}), bf16[128,16,128]{2,1,0:T(8,128)(2,1)S(1)}, u32[]{:S(2)}, u32[]{:S(2)}) async-start(bf16[128,16,128]{2,1,0:T(8,128)(2,1)} %bitcast.5), calls=%async_computation | async-start | bytes 1048576 | tf_op jit(solution)/shard_map/all_to_all | solution.py:310
  24.0 0.7 or_convert_fusion.1
  24.7 0.1 copy.18
  24.8 0.1 reshape.72
  24.9 10.1 %all_gather.9 = f32[4,4,4,128]{3,2,1,0:T(4,128)S(1)} all-gather(f32[1,4,4,128]{3,2,1,0:T(4,128)S(1)} %copy.21), channel_id=1, replica_groups=mesh['y'=4,'h'=4,'l'=4,'c'=2,'x'=4] {'x'}, dimensions={0}, use_global_device_ids=true | all-gather | bytes 40960 | tf_op jit(solution)/shard_map/all_gather | solution.py:326
  35.0 25.7 %all-gather = f32[16,4,4,128]{3,2,1,0:T(4,128)S(1)} all-gather(f32[4,4,4,128]{3,2,1,0:T(4,128)S(1)} %all_gather.9), channel_id=2, replica_groups=mesh['y'=4,'h'=4,'l'=4,'c'=2,'x'=4] {'h'}, dimensions={0}, use_global_device_ids=true | all-gather | bytes 163840 | tf_op jit(solution)/shard_map/all_gather | solution.py:326
  60.8 0.0 all-to-all-done
  60.8 0.0 copy-start.7
  60.8 0.0 copy-start.6
  60.8 0.0 copy-start
  60.8 0.0 copy-start.1
  60.8 0.0 copy-start.4
  60.8 4.7 %shard_map.110 = bf16[32,4,4,16,128]{4,3,2,1,0:T(8,128)(2,1)} custom-call(s32[4]{0:T(128)S(1)} %iota.12.order_ref, f32[4,4,4,128]{3,2,1,0:T(4,128)S(1)} %dynamic-slice_bitcast_fusion.5.place_ref, bf16[2048,128]{1,0:T(8,128)(2,1)S(1)} %bitcast.31), custom_call_target="tpu_custom_call" | custom-call | flops 2147483648 | bytes 4194304 | tf_op jit(solution)/shard_map/pallas_call | solution.py:179
  65.6 0.0 copy-start.5
  65.6 10.1 %all-to-all-start.1 = ((bf16[32,256,128]{2,1,0:T(8,128)(2,1)}), bf16[32,256,128]{2,1,0:T(8,128)(2,1)S(1)}, u32[]{:S(2)}, u32[]{:S(2)}) async-start(bf16[32,256,128]{2,1,0:T(8,128)(2,1)} %bitcast.32), calls=%async_computation.1 | async-start | bytes 4194304 | tf_op jit(solution)/shard_map/all_to_all | solution.py:310
  75.7 0.0 copy-done.7
  75.7 0.1 reshape.63
  75.8 0.0 copy-done.6
  75.8 0.1 reshape.70
  75.9 0.0 copy-done
  75.9 0.0 copy-done.1
  75.9 0.0 copy-done.4
  75.9 0.8 shard_map.111
  76.7 0.8 dynamic-slice_bitcast_fusion.1
  77.5 4.3 %collective-permute-start = (bf16[544,128]{1,0:T(8,128)(2,1)}, bf16[544,128]{1,0:T(8,128)(2,1)S(1)}, u32[]{:S(2)}, u32[]{:S(2)}) collective-permute-start(bf16[544,128]{1,0:T(8,128)(2,1)} %get-tuple-element.7), channel_id=1, source_target_pairs={{1,0},{2,1},{3,2},{0,3},{5,4},{6,5},{7,6},{4,7},{9,8},{10,9},{11,1... | collective-permute-start | bytes 417800 | tf_op jit(solution)/shard_map/ppermute | solution.py:341
  81.7 2.4 %collective-permute-start.1 = (bf16[544,128]{1,0:T(8,128)(2,1)}, bf16[544,128]{1,0:T(8,128)(2,1)}, u32[]{:S(2)}, u32[]{:S(2)}) collective-permute-start(bf16[544,128]{1,0:T(8,128)(2,1)} %get-tuple-element.6), channel_id=1, source_target_pairs={{2,0},{3,1},{0,2},{1,3},{6,4},{7,5},{4,6},{5,7},{10,8},{11,9},{8,1... | collective-permute-start | bytes 417800 | tf_op jit(solution)/shard_map/ppermute | solution.py:341
  84.2 2.5 %collective-permute-start.2 = (bf16[544,128]{1,0:T(8,128)(2,1)}, bf16[544,128]{1,0:T(8,128)(2,1)}, u32[]{:S(2)}, u32[]{:S(2)}) collective-permute-start(bf16[544,128]{1,0:T(8,128)(2,1)} %get-tuple-element.5), channel_id=1, source_target_pairs={{3,0},{0,1},{1,2},{2,3},{7,4},{4,5},{5,6},{6,7},{11,8},{8,9},{9,10... | collective-permute-start | bytes 417800 | tf_op jit(solution)/shard_map/ppermute | solution.py:341
  87.3 1.3 dynamic-slice_bitcast_fusion.col_ref
  88.6 0.0 collective-permute-done.w1
  88.6 1.5 %collective-permute-done.1.w2 = bf16[544,128]{1,0:T(8,128)(2,1)} collective-permute-done((bf16[544,128]{1,0:T(8,128)(2,1)}, bf16[544,128]{1,0:T(8,128)(2,1)}, u32[]{:S(2)}, u32[]{:S(2)}) %collective-permute-start.1) | collective-permute-done | bytes 139296 | tf_op jit(solution)/shard_map/ppermute | solution.py:341
  90.2 3.4 %collective-permute-done.2.w3 = bf16[544,128]{1,0:T(8,128)(2,1)} collective-permute-done((bf16[544,128]{1,0:T(8,128)(2,1)}, bf16[544,128]{1,0:T(8,128)(2,1)}, u32[]{:S(2)}, u32[]{:S(2)}) %collective-permute-start.2) | collective-permute-done | bytes 139296 | tf_op jit(solution)/shard_map/ppermute | solution.py:341
  93.5 31.9 %all-to-all-done.1 = bf16[32,256,128]{2,1,0:T(8,128)(2,1)S(1)} async-done(((bf16[32,256,128]{2,1,0:T(8,128)(2,1)}), bf16[32,256,128]{2,1,0:T(8,128)(2,1)S(1)}, u32[]{:S(2)}, u32[]{:S(2)}) %all-to-all-start.1) | async-done | bytes 2097184 | tf_op jit(solution)/shard_map/all_to_all | solution.py:310
  125.4 0.0 copy-done.5
  125.4 12.4 %shard_map.112 = f32[4,8,128]{2,1,0:T(8,128)} custom-call(s32[4]{0:T(128)S(1)} %and_select_fusion.order_ref, bf16[32,4,64,128]{3,2,1,0:T(8,128)(2,1)S(1)} %bitcast.30, bf16[544,128]{1,0:T(8,128)(2,1)S(1)} %get-tuple-element.8.w0, bf16[544,128]{1,0:T(8,128)(2,1)S(1)} %collective-permute-done.w1, bf16[544,128]{1,0:T(8,128)(2,1)} %collective-permute-done.1.w2, ...), custom_call_target="tpu_custom_call" | custom-call | flops 8589934592 | bytes 4194304 | tf_op jit(solution)/shard_map/pallas_call | solution.py:282
  137.8 3.8 %all-to-all-start.2 = ((f32[4,8,128]{2,1,0:T(8,128)}), f32[4,8,128]{2,1,0:T(8,128)S(1)}, u32[]{:S(2)}, u32[]{:S(2)}) async-start(f32[4,8,128]{2,1,0:T(8,128)} %shard_map.112), calls=%async_computation.2 | async-start | bytes 32768 | tf_op jit(solution)/shard_map/all_to_all | solution.py:310
  141.7 4.2 %all-to-all-done.2 = f32[4,8,128]{2,1,0:T(8,128)S(1)} async-done(((f32[4,8,128]{2,1,0:T(8,128)}), f32[4,8,128]{2,1,0:T(8,128)S(1)}, u32[]{:S(2)}, u32[]{:S(2)}) %all-to-all-start.2) | async-done | bytes 16416 | tf_op jit(solution)/shard_map/all_to_all | solution.py:310
  145.9 0.6 broadcast_select_fusion
  (8 shorter events, 0.1 us)
Async XLA Ops:
  0.0 1.0 copy-start.2
  1.0 0.9 copy-start.3
  3.4 57.4 %all-to-all-start = ((bf16[128,16,128]{2,1,0:T(8,128)(2,1)}), bf16[128,16,128]{2,1,0:T(8,128)(2,1)S(1)}, u32[]{:S(2)}, u32[]{:S(2)}) async-start(bf16[128,16,128]{2,1,0:T(8,128)(2,1)} %bitcast.5), calls=%async_computation | async-start | bytes 1048576 | tf_op jit(solution)/shard_map/all_to_all | solution.py:310
  60.8 14.9 %copy-start.7 = (f32[1,8,64]{2,1,0:T(8,128)S(1)}, f32[1,8,64]{2,1,0:T(8,128)}, u32[]{:S(2)}) copy-start(f32[1,8,64]{2,1,0:T(8,128)} %param.14) | copy-start | bytes 6148
  60.8 15.0 %copy-start.6 = (s32[2,1,8,64]{3,2,1,0:T(8,128)S(1)}, s32[2,1,8,64]{3,2,1,0:T(8,128)}, u32[]{:S(2)}) copy-start(s32[2,1,8,64]{3,2,1,0:T(8,128)} %param.13) | copy-start | bytes 12292
  60.8 15.1 %copy-start = (bf16[8,64,512]{2,1,0:T(8,128)(2,1)S(1)}, bf16[8,64,512]{2,1,0:T(8,128)(2,1)}, u32[]{:S(2)}) copy-start(bf16[8,64,512]{2,1,0:T(8,128)(2,1)} %spectra_ref.1) | copy-start | bytes 1572868
  60.8 15.0 %copy-start.1 = (bf16[16,64,256]{2,1,0:T(8,128)(2,1)S(1)}, bf16[16,64,256]{2,1,0:T(8,128)(2,1)}, u32[]{:S(2)}) copy-start(bf16[16,64,256]{2,1,0:T(8,128)(2,1)} %ctf_ref.1) | copy-start | bytes 1572868
  60.8 15.0 %copy-start.4 = (s32[8]{0:T(128)S(1)}, s32[8]{0:T(128)}, u32[]{:S(2)}) copy-start(s32[8]{0:T(128)} %class_ref.1) | copy-start | bytes 100
  65.6 59.8 %copy-start.5 = (f32[4,8,128]{2,1,0:T(8,128)S(1)}, f32[4,8,128]{2,1,0:T(8,128)}, u32[]{:S(2)}) copy-start(f32[4,8,128]{2,1,0:T(8,128)} %constant.106.clone.row_ref) | copy-start | bytes 49156
  65.6 59.8 %all-to-all-start.1 = ((bf16[32,256,128]{2,1,0:T(8,128)(2,1)}), bf16[32,256,128]{2,1,0:T(8,128)(2,1)S(1)}, u32[]{:S(2)}, u32[]{:S(2)}) async-start(bf16[32,256,128]{2,1,0:T(8,128)(2,1)} %bitcast.32), calls=%async_computation.1 | async-start | bytes 4194304 | tf_op jit(solution)/shard_map/all_to_all | solution.py:310
  77.5 11.1 %collective-permute-start = (bf16[544,128]{1,0:T(8,128)(2,1)}, bf16[544,128]{1,0:T(8,128)(2,1)S(1)}, u32[]{:S(2)}, u32[]{:S(2)}) collective-permute-start(bf16[544,128]{1,0:T(8,128)(2,1)} %get-tuple-element.7), channel_id=1, source_target_pairs={{1,0},{2,1},{3,2},{0,3},{5,4},{6,5},{7,6},{4,7},{9,8},{10,9},{11,1... | collective-permute-start | bytes 417800 | tf_op jit(solution)/shard_map/ppermute | solution.py:341
  81.7 8.4 %collective-permute-start.1 = (bf16[544,128]{1,0:T(8,128)(2,1)}, bf16[544,128]{1,0:T(8,128)(2,1)}, u32[]{:S(2)}, u32[]{:S(2)}) collective-permute-start(bf16[544,128]{1,0:T(8,128)(2,1)} %get-tuple-element.6), channel_id=1, source_target_pairs={{2,0},{3,1},{0,2},{1,3},{6,4},{7,5},{4,6},{5,7},{10,8},{11,9},{8,1... | collective-permute-start | bytes 417800 | tf_op jit(solution)/shard_map/ppermute | solution.py:341
  84.2 9.4 %collective-permute-start.2 = (bf16[544,128]{1,0:T(8,128)(2,1)}, bf16[544,128]{1,0:T(8,128)(2,1)}, u32[]{:S(2)}, u32[]{:S(2)}) collective-permute-start(bf16[544,128]{1,0:T(8,128)(2,1)} %get-tuple-element.5), channel_id=1, source_target_pairs={{3,0},{0,1},{1,2},{2,3},{7,4},{4,5},{5,6},{6,7},{11,8},{8,9},{9,10... | collective-permute-start | bytes 417800 | tf_op jit(solution)/shard_map/ppermute | solution.py:341
  137.8 8.0 %all-to-all-start.2 = ((f32[4,8,128]{2,1,0:T(8,128)}), f32[4,8,128]{2,1,0:T(8,128)S(1)}, u32[]{:S(2)}, u32[]{:S(2)}) async-start(f32[4,8,128]{2,1,0:T(8,128)} %shard_map.112), calls=%async_computation.2 | async-start | bytes 32768 | tf_op jit(solution)/shard_map/all_to_all | solution.py:310
